TPU v7x, 128 devices: a whole 4x4x4 slice. The times are simulated.
128 devices in a mesh: rep: 8 (over y_hi, z), fsdp: 16 (over y_lo, x, core).
Axes of the slice: x: 4, y: 4 (y_hi: 2, y_lo: 2; y = y_hi * 2 + y_lo), z: 4, core: 2. Of those that a mesh axis runs over, the one named last changes fastest.
Arguments:
- token_ids: int32 [49152], P(('rep', 'fsdp')), may hold values from 0 to 128255, as said below
- normed_inputs: bfloat16 [49152, 8192], P(('rep', 'fsdp')), may hold values from -24 to 24
- kv_cotangent: bfloat16 [49152, 1024], P(('rep', 'fsdp')), may hold values from -0.5 to 0.5
- replica_weights: bfloat16 [8, 8192, 1024], P('rep', 'fsdp'), may hold values from -6 to 6
- snapshot: bfloat16 [8192, 1024], P('fsdp'), may hold values from -6 to 6
- momentum: float32 [8192, 1024], P('fsdp', 'rep'), may hold values from -4 to 4
Outputs:
- input_grad: float32 [49152, 8192], P(('rep', 'fsdp'))
- weight_grad: float32 [8, 8192, 1024], P('rep', 'fsdp')
- new_weights: float32 [8192, 1024], P('fsdp')
- new_momentum: float32 [8192, 1024], P('fsdp', 'rep')
Inputs may be any that keep to these rules, and one draw needn't show every extreme that they name: `token_ids`: 0 is the padding id; it fills the end of each device's sequence of 384 tokens, and each sequence holds 96 or more other ids.
All inputs are finite; a program needn't handle non-finite values.
Results may differ from a plain program's by a relative error of at most 0.0003.
Values may be sent and summed in bfloat16 or wider, within the bound.
No kernel may reach another device: no remote copies, remote signals or barrier semaphores. Data moves between devices by JAX's collectives and lax.ppermute only.
A program may use at most 192 MiB of HBM per device.

v0:
```python
import jax
import jax.numpy as jnp
from jax import lax
from jax.sharding import PartitionSpec as P

outer_rate = 0.7
outer_beta = 0.9


def cut_along(array, dim, devices):
    dims = array.shape
    parts = array.reshape(*dims[:dim], devices, dims[dim] // devices, *dims[dim + 1 :])
    return jnp.moveaxis(parts, dim, 0)


def sum_at_owner(array, axis, dim):
    parts = cut_along(array, dim, lax.axis_size(axis))
    arrived = lax.all_to_all(parts, axis, split_axis=0, concat_axis=0, tiled=True)
    return arrived.sum(axis=0)


def in_order(parts, dim):
    dims = list(parts.shape[1:])
    dims[dim] *= parts.shape[0]
    return jnp.moveaxis(parts, 0, dim).reshape(dims)


def sent_to_all(array, axis):
    copies = jnp.broadcast_to(array, (lax.axis_size(axis), *array.shape))
    return lax.all_to_all(copies, axis, split_axis=0, concat_axis=0, tiled=True)


def gathered_copies(array, axis, dim):
    return in_order(sent_to_all(array, axis), dim)


def per_device(token_ids, normed_inputs, kv_cotangent, replica_weights, snapshot, momentum):
    live_rows = (token_ids != 0).astype(jnp.bfloat16)[:, None]
    masked = kv_cotangent * live_rows
    weights = replica_weights[0]
    input_grad = jnp.einsum(
        "tk,dk->td",
        masked,
        lax.all_gather(weights, "fsdp", axis=0, tiled=True),
        preferred_element_type=jnp.float32,
    )
    weight_grad = lax.psum_scatter(
        jnp.einsum("td,tk->dk", normed_inputs, masked, preferred_element_type=jnp.float32),
        "fsdp",
        scatter_dimension=0,
        tiled=True,
    )
    groups = lax.axis_size("rep")
    col_width = momentum.shape[1]
    pseudo_grad = snapshot.astype(jnp.float32) - weights.astype(jnp.float32)
    outer_grad = sum_at_owner(pseudo_grad, "rep", 1) / groups
    snap_part = lax.dynamic_slice_in_dim(snapshot, lax.axis_index("rep") * col_width, col_width, 1)
    new_momentum = outer_beta * momentum + outer_grad
    new_part = snap_part.astype(jnp.float32) - outer_rate * (outer_grad + outer_beta * new_momentum)
    new_weights = gathered_copies(new_part, "rep", 1)
    return (input_grad, weight_grad[None], new_weights, new_momentum)


def solution(mesh):
    return jax.shard_map(
        per_device,
        mesh=mesh,
        in_specs=(
            P(("rep", "fsdp")),
            P(("rep", "fsdp"), None),
            P(("rep", "fsdp"), None),
            P("rep", "fsdp", None),
            P("fsdp", None),
            P("fsdp", "rep"),
        ),
        out_specs=(
            P(("rep", "fsdp"), None),
            P("rep", "fsdp", None),
            P("fsdp", None),
            P("fsdp", "rep"),
        ),
        check_vma=False,
    )
```

profile of v0, /device:TPU:1, one launch (start us, length us, event | category | flops | bytes accessed | tf_op | source)
XLA Modules:
  0.0 343.3 jit_solution(2849240457339045110)
XLA Ops:
  7.2 0.0 all-gather.3.cloned.1.call-start
  7.2 0.7 all-gather.3.cloned.1.call-update
  7.9 0.0 reduce-scatter.2.cloned.1.call-start
  7.9 0.7 compare_convert_fusion
  8.6 18.0 %convolution_bitcast_fusion = f32[8192,1024]{0,1:T(8,128)} fusion(bf16[384,8192]{1,0:T(8,128)(2,1)} %param.7, bf16[384,1024]{1,0:T(8,128)(2,1)} %param.8, bf16[384]{0:T(512)(128)(2,1)S(1)} %compare_convert_fusion), kind=kOutput, calls=%fused_computation | convolution fusion | flops 6442844160 | bytes 40633088 | tf_op jit(solution)/shard_map/td,tk->dk/dot_general | solution.py:48
  26.6 0.0 copy-start
  26.6 0.0 copy-start.1
  26.6 0.0 reduce-scatter.2.cloned.1.call-update
  26.7 1.2 copy-done
  27.9 0.5 copy.13
  28.4 0.0 copy-done.1
  28.4 1.3 copy.12
  29.7 1.5 convert_subtract_fusion
  31.3 0.0 copy-start.3
  31.3 1.8 copy.14
  33.1 8.7 %all-to-all-start = ((f32[8,512,128]{2,1,0:T(8,128)}), f32[8,512,128]{2,1,0:T(8,128)S(1)}, u32[]{:S(2)}, u32[]{:S(2)}) async-start(f32[8,512,128]{2,1,0:T(8,128)} %copy.14), calls=%async_computation.1 | async-start | bytes 4194304 | tf_op jit(solution)/shard_map/all_to_all | solution.py:18
  41.8 48.9 %all-to-all-done = f32[8,512,128]{2,1,0:T(8,128)S(1)} async-done(((f32[8,512,128]{2,1,0:T(8,128)}), f32[8,512,128]{2,1,0:T(8,128)S(1)}, u32[]{:S(2)}, u32[]{:S(2)}) %all-to-all-start) | async-done | bytes 2097184 | tf_op jit(solution)/shard_map/all_to_all | solution.py:18
  90.6 0.1 reduce_sum.9
  90.8 0.0 copy-done.3
  90.8 1.7 multiply_subtract_fusion
  92.4 0.1 broadcast_in_dim.8
  92.6 0.0 copy-start.2
  92.6 52.8 %all_to_all.10 = f32[8,512,128]{2,1,0:T(8,128)S(1)} all-to-all(f32[8,512,128]{2,1,0:T(8,128)S(1)} %broadcast_in_dim.8), channel_id=1, replica_groups=mesh['rep'=8,'fsdp'=16] {'rep'}, dimensions={0} | all-to-all | bytes 4194304 | tf_op jit(solution)/shard_map/all_to_all | solution.py:30
  145.4 1.8 copy.15
  147.2 2.9 copy.17
  150.1 0.0 all-gather.3.cloned.1.call-done
  150.1 0.0 copy-done.2
  150.1 13.2 %fusion = f32[384,8192]{1,0:T(8,128)} fusion(bf16[1,8192,1024]{2,1,0:T(8,128)(2,1)} %all-gather.3.cloned.1.call-done, bf16[384,1024]{1,0:T(8,128)(2,1)S(1)} %copy-done.2, bf16[384]{0:T(512)(128)(2,1)S(1)} %compare_convert_fusion), kind=kOutput, calls=%fused_computation.1 | convolution fusion | flops 6442844160 | bytes 30147328 | tf_op jit(solution)/shard_map/tk,dk->td/dot_general | solution.py:41
  163.3 170.3 %reduce-scatter.2.cloned.1.call-done = f32[512,1024]{0,1:T(8,128)} async-done(((f32[8192,1024]{0,1:T(8,128)}), f32[512,1024]{0,1:T(8,128)}) %reduce-scatter.2.cloned.1.call-update) | async-done | bytes 2097168 | tf_op jit(solution)/shard_map/reduce_scatter | solution.py:47
  333.6 2.9 copy.16
Async XLA Ops:
  7.2 142.9 %all-gather.3.cloned.1.call-start = ((), (), s32[]{:S(2)}) async-start(), calls=%async_computation.4 | async-start | bytes 17825792 | tf_op jit(solution)/shard_map/all_gather | solution.py:44
  7.9 325.7 %reduce-scatter.2.cloned.1.call-start = ((), (), s32[]{:S(2)}) async-start(), calls=%async_computation.3 | async-start | bytes 35651584 | tf_op jit(solution)/shard_map/reduce_scatter | solution.py:47
  26.6 1.2 copy-start
  26.6 1.8 copy-start.1
  31.3 59.5 %copy-start.3 = (f32[512,128]{1,0:T(8,128)S(1)}, f32[512,128]{1,0:T(8,128)}, u32[]{:S(2)}) copy-start(f32[512,128]{1,0:T(8,128)} %param.11) | copy-start | bytes 786436
  33.1 57.5 %all-to-all-start = ((f32[8,512,128]{2,1,0:T(8,128)}), f32[8,512,128]{2,1,0:T(8,128)S(1)}, u32[]{:S(2)}, u32[]{:S(2)}) async-start(f32[8,512,128]{2,1,0:T(8,128)} %copy.14), calls=%async_computation.1 | async-start | bytes 4194304 | tf_op jit(solution)/shard_map/all_to_all | solution.py:18
  92.6 57.5 %copy-start.2 = (bf16[384,1024]{1,0:T(8,128)(2,1)S(1)}, bf16[384,1024]{1,0:T(8,128)(2,1)}, u32[]{:S(2)}) copy-start(bf16[384,1024]{1,0:T(8,128)(2,1)} %param.8) | copy-start | bytes 2359300
Sparse Core Ops, SparseCore 0:
  9.7 140.1 all-gather.2
  152.4 181.1 reduce-scatter.1
where the time goes:
time: 344 us; the launch traced here: 343 us
  waiting for transfers between devices  220 us (64%)
  blocking collectives  52.8 us (15%)
  matrix products  31.2 us (9%)
  between operations  14.1 us (4%)
  local copies, waits for them, and re-layouts  12.6 us (4%)
  starting transfers between devices  8.75 us (3%)
  other arithmetic  4.01 us (1%)
    reduce_scatter x1, waiting for transfers between devices, per_device(): lax.psum_scatter(jnp.einsum('td,tk->dk', normed_inputs, masked, preferred...  170 us
    all_to_all x1, blocking collectives, sent_to_all(): return lax.all_to_all(copies, axis, split_axis=0, concat_axis=0, tiled=True)  52.8 us
    all_to_all x1, waiting for transfers between devices, sum_at_owner(): lax.all_to_all(parts, axis, split_axis=0, concat_axis=0, tiled=True)  48.9 us
    dot_general x1, matrix products, per_device(): jnp.einsum('td,tk->dk', normed_inputs, masked, preferred_element_type=jnp...  18 us
    dot_general x1, matrix products, per_device(): jnp.einsum('tk,dk->td', masked, lax.all_gather(weights, 'fsdp', axis=0, t...  13.2 us
    unnamed x12, local copies, waits for them, and re-layouts  8.83 us
    all_to_all x1, starting transfers between devices, sum_at_owner(): lax.all_to_all(parts, axis, split_axis=0, concat_axis=0, tiled=True)  8.67 us
  transfers between devices with their start and end apart: 3, of which 2 were waited for; matrix products, arithmetic and copies ran while one was open for 13% of the time, Pallas kernels for 0%

commit v1 on v0

v1 whole, which is shorter than its diff:
```python
import jax
import jax.numpy as jnp
import numpy as np
from jax import lax
from jax.experimental import pallas as pl
from jax.experimental.pallas import tpu as pltpu
from jax.sharding import PartitionSpec as P

outer_rate = 0.7
outer_beta = 0.9
top_code = 32767.0
group_rows = 32
half = 256
MB = 1 << 20
vmem = 60 * MB
tiny = pl.CostEstimate(flops=1000, bytes_accessed=1000, transcendentals=0)


def fsdp_index(y, x, c):
    return y * 8 + x * 2 + c


def decoded(ref):
    rows = ref.shape[1] * group_rows // (group_rows + 1)
    codes = ref[0, :rows, :].astype(jnp.int32).astype(jnp.float32)
    unit = jnp.exp2(ref[0, rows:, :].astype(jnp.int32).astype(jnp.float32) * 0.25) * (1.0 / top_code)
    groups, width = unit.shape
    return (codes.reshape(groups, group_rows, width) * unit[:, None, :]).reshape(rows, width)


def store_coded(out_ref, total):
    rows, width = total.shape
    grouped = total.reshape(rows // group_rows, group_rows, width)
    peak = jnp.maximum(jnp.max(jnp.abs(grouped), axis=1), 1e-33)
    exponent = jnp.ceil(4.0 * jnp.log2(peak) + 0.01)
    scale = top_code / jnp.exp2(exponent * 0.25)
    codes = jnp.round(grouped * scale[:, None, :]).astype(jnp.int32).astype(jnp.int16)
    out_ref[0, :rows, :] = codes.reshape(rows, width)
    out_ref[0, rows:, :] = exponent.astype(jnp.int32).astype(jnp.int16)


def sums_kernel(groups, n_adds, at_ref, mt_ref, own_ref, sib_ref, *refs):
    step = pl.program_id(0)
    adds, outs = refs[:n_adds], refs[-len(groups) :]
    first = 0
    for (count, used, final), out_ref in zip(groups, outs, strict=True):

        @pl.when((step >= first) & (step < first + count))
        def _(used=used, final=final, out_ref=out_ref):
            tokens = jnp.concatenate([own_ref[...], sib_ref[...]], axis=0)
            total = jnp.dot(mt_ref[...], tokens, preferred_element_type=jnp.float32)
            for j in used:
                total = total + decoded(adds[j])
            if final:
                out_ref[...] = total.T
            else:
                store_coded(out_ref, total)

        first += count


def sums(at, offset, mt, x_own, x_sib, groups, adds=(), final_at=0):
    rows, both_tokens = mt.shape
    tokens = both_tokens // 2
    coded = rows + rows // group_rows
    specs = [
        pl.BlockSpec(mt.shape, lambda i, at: (0, 0)),
        pl.BlockSpec((tokens, half), lambda i, at: (0, at[offset + i])),
        pl.BlockSpec((tokens, half), lambda i, at: (0, at[offset + i])),
    ]
    for _, index in adds:
        specs.append(pl.BlockSpec((1, coded, half), lambda i, at, index=index: (index(i, at), 0, 0)))
    out_specs, out_shapes, first = [], [], 0
    for count, _, final in groups:
        if final:
            out_specs.append(pl.BlockSpec((half, rows), lambda i, at: (at[final_at], 0)))
            out_shapes.append(jax.ShapeDtypeStruct((2 * half, rows), jnp.float32))
        else:
            out_specs.append(
                pl.BlockSpec(
                    (1, coded, half),
                    lambda i, at, first=first, count=count: (jnp.clip(i - first, 0, count - 1), 0, 0),
                )
            )
            out_shapes.append(jax.ShapeDtypeStruct((count, coded, half), jnp.int16))
        first += count
    return pl.pallas_call(
        lambda *refs: sums_kernel(groups, len(adds), *refs),
        grid_spec=pltpu.PrefetchScalarGridSpec(
            num_scalar_prefetch=1, grid=(first,), in_specs=specs, out_specs=out_specs
        ),
        out_shape=out_shapes,
        compiler_params=pltpu.CompilerParams(vmem_limit_bytes=vmem),
        cost_estimate=tiny,
        name="partial_sums",
    )(at, mt, x_own, x_sib, *[array for array, _ in adds])


def last_kernel(at_ref, add_ref, _, out_ref):
    out_ref[...] = decoded(add_ref).T


def last_rows(at, offset, coded, so_far):
    return pl.pallas_call(
        last_kernel,
        grid_spec=pltpu.PrefetchScalarGridSpec(
            num_scalar_prefetch=1,
            grid=(1,),
            in_specs=[pl.BlockSpec(coded.shape, lambda i, at: (0, 0, 0)), pl.BlockSpec(memory_space=pl.ANY)],
            out_specs=pl.BlockSpec((half, so_far.shape[1]), lambda i, at: (at[offset], 0)),
        ),
        out_shape=jax.ShapeDtypeStruct(so_far.shape, so_far.dtype),
        input_output_aliases={2: 0},
        compiler_params=pltpu.CompilerParams(vmem_limit_bytes=vmem),
        cost_estimate=tiny,
        name="last_rows",
    )(at, coded, so_far)


def columns_kernel(n, at_ref, masked_ref, *refs):
    step = pl.program_id(0)
    out_ref = refs[-1]
    for j in range(n):

        @pl.when(step == j)
        def _(piece=refs[j]):
            out_ref[...] = lax.dot_general(
                masked_ref[...], piece[...], (((1,), (1,)), ((), ())), preferred_element_type=jnp.float32
            )


def grad_columns(at, offset, masked, pieces, wide, so_far, rows):
    n = len(pieces)
    features = pieces[0][0].shape[1]
    tokens = masked.shape[0]
    specs = [pl.BlockSpec(masked.shape, lambda i, at: (0, 0))]
    specs += [pl.BlockSpec((rows, features), lambda i, at, k=k: (k, 0)) for _, k in pieces]
    operands = [at, masked, *[array for array, _ in pieces]]
    aliases = {}
    if so_far is not None:
        specs.append(pl.BlockSpec(memory_space=pl.ANY))
        aliases = {len(operands): 0}
        operands.append(so_far)
    return pl.pallas_call(
        lambda *refs: columns_kernel(n, *refs),
        grid_spec=pltpu.PrefetchScalarGridSpec(
            num_scalar_prefetch=1,
            grid=(n,),
            in_specs=specs,
            out_specs=pl.BlockSpec((tokens, rows), lambda i, at: (0, at[offset + i])),
        ),
        out_shape=jax.ShapeDtypeStruct((tokens, wide), jnp.float32),
        input_output_aliases=aliases,
        compiler_params=pltpu.CompilerParams(vmem_limit_bytes=vmem),
        cost_estimate=tiny,
        name="grad_columns",
    )(*operands)


def assemble_kernel(at_ref, *refs):
    step = pl.program_id(0)
    out_ref = refs[-1]
    for j in range(4):
        for k in range(2):

            @pl.when(step == 2 * j + k)
            def _(piece=refs[j], k=k):
                rows = out_ref.shape[0]
                out_ref[...] = piece[k * rows : (k + 1) * rows, :]


def assembled(pieces, places):
    rows, width = pieces[0].shape
    return pl.pallas_call(
        assemble_kernel,
        grid_spec=pltpu.PrefetchScalarGridSpec(
            num_scalar_prefetch=1,
            grid=(8,),
            in_specs=[pl.BlockSpec((rows, width), lambda i, at: (0, 0))] * 4,
            out_specs=pl.BlockSpec((rows // 2, width), lambda i, at: (0, at[i])),
        ),
        out_shape=jax.ShapeDtypeStruct((rows // 2, 8 * width), jnp.float32),
        compiler_params=pltpu.CompilerParams(vmem_limit_bytes=vmem),
        cost_estimate=tiny,
        name="assembled",
    )(places, *pieces)


def group_columns(array, zz, h, width):
    cut = lambda hh: lax.dynamic_slice_in_dim(array, (hh * 4 + zz) * width, width, 1)
    return jnp.concatenate([cut(h), cut(1 - h)], axis=0)


def together(*arrays):
    return lax.optimization_barrier(arrays)


def sent(array, pairs):
    return lax.ppermute(array, "fsdp", pairs)


def sent_rep(array, dh=0, dz=0):
    pairs = [(h * 4 + z, (h ^ dh) * 4 + (z + dz) % 4) for h in range(2) for z in range(4)]
    return lax.ppermute(array, "rep", pairs)


chips = [(y, x, c) for y in range(2) for x in range(4) for c in range(2)]
to_core = [(fsdp_index(y, x, c), fsdp_index(y, x, 1 - c)) for y, x, c in chips]
to_y = [(fsdp_index(y, x, c), fsdp_index(1 - y, x, c)) for y, x, c in chips]
ahead = [(fsdp_index(y, x, c), fsdp_index(y, (x + 1 - 2 * c) % 4, c)) for y, x, c in chips]
behind = [(fsdp_index(y, x, c), fsdp_index(y, (x - 1 + 2 * c) % 4, c)) for y, x, c in chips]


def tables():
    starts, rows = {}, []
    for me in range(16):
        y, x, c = me // 8, (me // 2) % 4, me % 2
        s, o, row = 1 - 2 * c, 1 - c, []

        def cols(yy, dx):
            return [fsdp_index(yy, (x + dx) % 4, cc) * 2 + c for cc in range(2)]

        def places(*pieces):
            return [fsdp_index(y ^ dy, (x + dx) % 4, cc) for dy, dx, cc in pieces]

        for name, entries in (
            ("first", cols(1 - y, 2) + cols(y, -s) + cols(1 - y, -s) + cols(1 - y, s)),
            ("far", cols(y, 2)),
            ("near", cols(y, s) + cols(1 - y, 0)),
            ("home", [fsdp_index(y, x, cc) * 2 + c for cc in (o, c)]),
            ("cores", [o, c]),
            ("grad1", places((0, 0, c), (0, 0, o), (0, -s, c), (0, -s, o))),
            ("grad2", places((0, s, o), (0, s, c), (1, 0, c), (1, 0, o))),
            ("grad3", places((0, 2, c), (0, 2, o), (1, 2, c))),
            ("grad4", places((1, 2, o), (1, -s, c), (1, -s, o), (1, s, o), (1, s, c))),
        ):
            starts[name] = len(row)
            row += entries
        rows.append(row)
    rep_rows = []
    for me in range(8):
        h, z = me // 4, me % 4
        rep_rows.append([hh * 4 + (z - dz) % 4 for dz in (0, 1, 3, 2) for hh in (h, 1 - h)])
    return starts, np.array(rows, np.int32), np.array(rep_rows, np.int32)


def per_device(token_ids, normed_inputs, kv_cotangent, replica_weights, snapshot, momentum):
    wide = normed_inputs.shape[1]
    w = replica_weights[0]
    block = w.shape[0]
    groups = lax.axis_size("rep")
    rep = lax.axis_index("rep")
    gh, gz = rep // 4, rep % 4
    rows, width = momentum.shape
    starts, table, rep_table = tables()
    at = lax.dynamic_index_in_dim(jnp.asarray(table), lax.axis_index("fsdp"), 0, keepdims=False)
    rep_at = lax.dynamic_index_in_dim(jnp.asarray(rep_table), rep, 0, keepdims=False)

    def columns(name, pieces, so_far):
        return grad_columns(at, starts[name], masked, pieces, wide, so_far, block)

    def part_sums(name, *args, **kw):
        return sums(at, starts[name], mt, normed_inputs, x_sib, *args, **kw)

    x_sib = sent(normed_inputs, to_core)
    live_rows = (token_ids != 0).astype(jnp.bfloat16)[:, None]
    masked = kv_cotangent * live_rows
    masked_sib = sent(masked, to_core)
    both = jnp.concatenate([w, sent(w, to_core)], axis=0)
    f, v = sent(both, ahead), sent(w, to_y)
    mt = jnp.concatenate([masked, masked_sib], axis=0).T
    z1, z3, z2 = (sent_rep(group_columns(w, (gz + dz) % 4, gh, width), dz=dz) for dz in (1, 3, 2))
    far_y, b, near_o = part_sums("first", [(2, [], False), (4, [], False), (2, [], False)])
    both, f, v, far_y, b, near_o, z1, z3, z2, mt = together(both, f, v, far_y, b, near_o, z1, z3, z2, mt)

    b, f3, far_y = sent(b, behind), sent(f[:block], ahead), sent(far_y, to_y)
    d, v_s = sent(f, to_core), sent(v, to_core)
    snap = group_columns(snapshot, gz, gh, width).astype(jnp.float32)
    total = snap - group_columns(both[:block], gz, gh, width).astype(jnp.float32)
    for part in (z1, z3, z2):
        total = total + (snap - part.astype(jnp.float32))
    total_in = sent_rep(total[rows:], dh=1)
    grad = columns("grad1", [(both, 0), (both, 1), (f, 0), (f, 1)], None)
    v_both = jnp.concatenate([v, v_s], axis=0)
    (far,) = part_sums("far", [(2, [0], False)], [(far_y, lambda i, at: i)])
    b, f3, d, v_both, total, total_in, grad, far, near_o, mt = together(
        b, f3, d, v_both, total, total_in, grad, far, near_o, mt
    )

    far, near_o, h = sent(far, ahead), sent(near_o, ahead), sent(f3, to_y)
    d3 = sent(f3, to_core)
    outer_grad = (total[:rows] + total_in) / groups
    new_momentum = outer_beta * momentum + outer_grad
    new_part = snap[:rows] - outer_rate * (outer_grad + outer_beta * new_momentum)
    part_in = sent_rep(new_part, dh=1)
    grad = columns("grad2", [(d, 0), (d, 1), (v_both, 0), (v_both, 1)], grad)
    near, home_o = part_sums(
        "near",
        [(2, [0], False), (2, [1, 2], False)],
        [
            (far, lambda i, at: jnp.clip(i, 0, 1)),
            (b, lambda i, at: jnp.clip(i, 2, 3)),
            (near_o, lambda i, at: jnp.clip(i - 2, 0, 1)),
        ],
    )
    near, home_o, h, f3, d3, v_both, b, new_momentum, new_part, part_in, grad, mt = together(
        near, home_o, h, f3, d3, v_both, b, new_momentum, new_part, part_in, grad, mt
    )

    near, g, from_y = sent(near, ahead), sent(v_both, ahead), sent(home_o, to_y)
    part = jnp.concatenate([new_part, part_in], axis=0)
    z1, z3 = sent_rep(part, dz=1), sent_rep(part, dz=3)
    grad = columns("grad3", [(f3, 0), (d3, 0), (h, 0)], grad)
    by_core = [(array, lambda i, at: at[starts["cores"] + i]) for array in (b, near, from_y)]
    for_other, weight_grad = part_sums(
        "home", [(1, [0, 1, 2], False), (1, [0, 1, 2], True)], by_core, final_at=starts["cores"] + 1
    )
    h, g, part, z1, z3, grad, for_other, weight_grad = together(h, g, part, z1, z3, grad, for_other, weight_grad)

    from_other, e, h_s = sent(for_other, to_core), sent(g, to_core), sent(h, to_core)
    z2 = jnp.concatenate([sent_rep(z1[:rows], dz=1), sent_rep(z3[rows:], dz=3)], axis=0)
    weight_grad = last_rows(at, starts["cores"], from_other, weight_grad)
    input_grad = columns("grad4", [(h_s, 0), (g, 0), (g, 1), (e, 0), (e, 1)], grad)
    rep_at, _ = together(rep_at, input_grad)
    new_weights = assembled([part, z1, z3, z2], rep_at)
    return input_grad, weight_grad[None], new_weights, new_momentum


def solution(mesh):
    return jax.shard_map(
        per_device,
        mesh=mesh,
        in_specs=(
            P(("rep", "fsdp")),
            P(("rep", "fsdp"), None),
            P(("rep", "fsdp"), None),
            P("rep", "fsdp", None),
            P("fsdp", None),
            P("fsdp", "rep"),
        ),
        out_specs=(
            P(("rep", "fsdp"), None),
            P("rep", "fsdp", None),
            P("fsdp", None),
            P("fsdp", "rep"),
        ),
        check_vma=False,
    )
```

time: 344 us -> 193 us (0.56)
  waiting for transfers between devices: 220 us -> 52.7 us
  Pallas kernels: 0 us -> 64.4 us
  blocking collectives: 52.8 us -> 0 us
  starting transfers between devices: 8.75 us -> 41.8 us
  matrix products: 31.2 us -> 0 us
  between operations: 14.1 us -> 0.85 us
  other arithmetic: 4.01 us -> 14.3 us
  local copies, waits for them, and re-layouts: 12.6 us -> 18.4 us
    reduce_scatter x1 -> x0, waiting for transfers between devices: 170 us -> none  [per_device(): lax.psum_scatter(jnp.einsum('td,tk->dk', normed_inputs, masked, preferred...]
    pallas_call x0 -> x10, Pallas kernels: none -> 64.4 us  [the longest x4 29 us: sums(): pl.pallas_call(lambda *refs: sums_kernel(groups, len(adds), *refs), grid_...]
    all_to_all x1 -> x0, blocking collectives: 52.8 us -> none  [sent_to_all(): return lax.all_to_all(copies, axis, split_axis=0, concat_axis=0, tiled=True)]
    ppermute x0 -> x29, waiting for transfers between devices: none -> 52.7 us  [the longest x20 45.7 us: sent(): return lax.ppermute(array, 'fsdp', pairs)]
    all_to_all x1 -> x0, waiting for transfers between devices: 48.9 us -> none  [sum_at_owner(): lax.all_to_all(parts, axis, split_axis=0, concat_axis=0, tiled=True)]
    ppermute x0 -> x29, starting transfers between devices: none -> 41.8 us  [the longest x20 23.8 us: sent(): return lax.ppermute(array, 'fsdp', pairs)]
    dot_general x2 -> x0, matrix products: 31.2 us -> none  [the longest x1 18 us: per_device(): jnp.einsum('td,tk->dk', normed_inputs, masked, preferred_element_type=jnp...]
    concatenate x0 -> x6, other arithmetic: none -> 9.86 us  [the longest x1 3.03 us: per_device(): v_both = jnp.concatenate([v, v_s], axis=0)]
  transfers between devices with their start and end apart: 3 -> 29, of which waited for: 2 -> 9; matrix products, arithmetic and copies ran while one was open for 13% -> 16% of each run, Pallas kernels for 0% -> 27%
where the time goes in v1:
time: 193 us
  Pallas kernels  64.4 us (33%)
  waiting for transfers between devices  52.7 us (27%)
  starting transfers between devices  41.8 us (22%)
  local copies, waits for them, and re-layouts  18.4 us (10%)
  other arithmetic  14.3 us (7%)
    ppermute x20, waiting for transfers between devices, sent(): return lax.ppermute(array, 'fsdp', pairs)  45.7 us
    pallas_call x4, Pallas kernels, sums(): pl.pallas_call(lambda *refs: sums_kernel(groups, len(adds), *refs), grid_...  29 us
    pallas_call x4, Pallas kernels, grad_columns(): pl.pallas_call(lambda *refs: columns_kernel(n, *refs), grid_spec=pltpu.Pr...  27.1 us
    ppermute x20, starting transfers between devices, sent(): return lax.ppermute(array, 'fsdp', pairs)  23.8 us
    ppermute x9, starting transfers between devices, sent_rep(): return lax.ppermute(array, 'rep', pairs)  18.1 us
    ppermute x9, waiting for transfers between devices, sent_rep(): return lax.ppermute(array, 'rep', pairs)  7 us
    pallas_call x1, Pallas kernels, assembled(): pl.pallas_call(assemble_kernel, grid_spec=pltpu.PrefetchScalarGridSpec(nu...  5.25 us
    optimization_barrier x3, local copies, waits for them, and re-layouts, together(): return lax.optimization_barrier(arrays)  4.69 us
  transfers between devices with their start and end apart: 29, of which 9 were waited for; matrix products, arithmetic and copies ran while one was open for 16% of the time, Pallas kernels for 27%

profile of v1, /device:TPU:1, one launch (start us, length us, event | category | flops | bytes accessed | tf_op | source)
XLA Modules:
  0.0 192.5 jit_solution(16268375197787752664)
XLA Ops:
  0.6 1.5 collective-permute-start.4
  2.3 8.8 %collective-permute-done = bf16[512,1024]{1,0:T(8,128)(2,1)S(1)} collective-permute-done((bf16[512,1024]{1,0:T(8,128)(2,1)}, bf16[512,1024]{1,0:T(8,128)(2,1)S(1)}, u32[]{:S(2)}, u32[]{:S(2)}) %collective-permute-start) | collective-permute-done | bytes 1048608 | tf_op jit(solution)/shard_map/ppermute | solution.py:199
  11.1 2.8 %pad_maximum_fusion.refs_2_.refs_3_ = bf16[1024,1024]{1,0:T(8,128)(2,1)} fusion(bf16[512,1024]{1,0:T(8,128)(2,1)S(1)} %collective-permute-done, bf16[512,1024]{1,0:T(8,128)(2,1)} %bitcast.21), kind=kLoop, calls=%fused_computation | loop fusion | flops 4194304 | bytes 4194304 | tf_op jit(solution)/shard_map/concatenate | solution.py:269
  13.9 2.6 %collective-permute-start.1 = (bf16[1024,1024]{1,0:T(8,128)(2,1)}, bf16[1024,1024]{1,0:T(8,128)(2,1)}, u32[]{:S(2)}, u32[]{:S(2)}) collective-permute-start(bf16[1024,1024]{1,0:T(8,128)(2,1)} %pad_maximum_fusion.refs_2_.refs_3_), channel_id=1, source_target_pairs={{0,2},{1,7},{2,4},{3,1},{4,6},{5,3},{6,0},{7,5},{8,10},{9,15},{10,... | collective-permute-start | bytes 6291464 | tf_op jit(solution)/shard_map/ppermute | solution.py:199
  16.7 1.4 collective-permute-start.2
  19.0 3.6 %collective-permute-start.7 = (bf16[1024,128]{1,0:T(8,128)(2,1)}, bf16[1024,128]{1,0:T(8,128)(2,1)}, u32[]{:S(2)}, u32[]{:S(2)}) collective-permute-start(bf16[1024,128]{1,0:T(8,128)(2,1)} %pad_maximum_fusion.5), channel_id=1, source_target_pairs={{0,32},{16,48},{32,0},{48,16},{64,96},{80,112},{96,64},{112,80},{1... | collective-permute-start | bytes 786440 | tf_op jit(solution)/shard_map/ppermute | solution.py:204
  28.0 1.6 copy.16.refs_1_
  29.6 10.6 %partial_sums.4 = (s16[2,1056,256]{2,1,0:T(8,128)(2,1)}, s16[4,1056,256]{2,1,0:T(8,128)(2,1)}, s16[2,1056,256]{2,1,0:T(8,128)(2,1)}) custom-call(s32[34]{0:T(128)} %fusion.refs_0_.at_ref, bf16[1024,768]{1,0:T(8,128)(2,1)} %copy.16.refs_1_, bf16[384,8192]{1,0:T(8,128)(2,1)} %refs_2_.7, bf16[384,8192]{1,0:T(8,128)(2,1)} %collective-permute-done.4.refs_3_), custom_call_target="tpu_custom_call" | custom-call | flops 1000 | bytes 1000 | tf_op jit(solution)/shard_map/partial_sums/pallas_call | solution.py:87
  41.9 1.4 collective-permute-start.10
  43.3 1.3 collective-permute-start.13
  44.6 2.3 %slice.21 = bf16[512,1024]{1,0:T(8,128)(2,1)} slice(bf16[1024,1024]{1,0:T(8,128)(2,1)} %collective-permute-done.1.refs_4_.refs_5_), slice={[0:512], [0:1024]} | slice | bytes 2097152 | tf_op jit(solution)/shard_map/slice | solution.py:276
  46.9 1.3 collective-permute-start.9
  49.1 1.3 slice.22
  50.5 1.3 subtract_add_fusion
  52.6 2.6 %collective-permute-start.12 = (f32[512,128]{1,0:T(8,128)}, f32[512,128]{1,0:T(8,128)}, u32[]{:S(2)}, u32[]{:S(2)}) collective-permute-start(f32[512,128]{1,0:T(8,128)} %slice.28), channel_id=1, source_target_pairs={{0,64},{16,80},{32,96},{48,112},{64,0},{80,16},{96,32},{112,48},{1... | collective-permute-start | bytes 786440 | tf_op jit(solution)/shard_map/ppermute | solution.py:204
  55.2 6.7 %grad_columns.4.refs_6_ = f32[384,8192]{1,0:T(8,128)} custom-call(s32[34]{0:T(128)} %fusion.refs_0_.at_ref, bf16[384,1024]{1,0:T(8,128)(2,1)} %copy-done, bf16[1024,1024]{1,0:T(8,128)(2,1)} %pad_maximum_fusion.refs_2_.refs_3_, bf16[1024,1024]{1,0:T(8,128)(2,1)} %pad_maximum_fusion.refs_2_.refs_3_, bf16[1024,1024]{1,0:T(8,128)(2,1)} %collective-permute-done.1.refs_4_.refs_5_, ...), custom_call_target="tpu_custom_call" | custom-call | flops 1000 | bytes 1000 | tf_op jit(solution)/shard_map/grad_columns/pallas_call | solution.py:144
  61.9 1.6 copy.17.refs_1_
  63.5 3.0 %pad_maximum_fusion.1.refs_4_.refs_5_ = bf16[1024,1024]{1,0:T(8,128)(2,1)} fusion(bf16[512,1024]{1,0:T(8,128)(2,1)} %collective-permute-done.11, bf16[512,1024]{1,0:T(8,128)(2,1)} %collective-permute-done.2), kind=kLoop, calls=%fused_computation.1 | loop fusion | flops 4194304 | bytes 4194304 | tf_op jit(solution)/shard_map/concatenate | solution.py:284
  66.5 2.0 %collective-permute-done.13.refs_4_ = s16[2,1056,256]{2,1,0:T(8,128)(2,1)S(1)} collective-permute-done((s16[2,1056,256]{2,1,0:T(8,128)(2,1)}, s16[2,1056,256]{2,1,0:T(8,128)(2,1)S(1)}, u32[]{:S(2)}, u32[]{:S(2)}) %collective-permute-start.13) | collective-permute-done | bytes 1081376 | tf_op jit(solution)/shard_map/ppermute | solution.py:199
  69.6 4.9 %partial_sums.5 = s16[2,1056,256]{2,1,0:T(8,128)(2,1)} custom-call(s32[34]{0:T(128)} %fusion.refs_0_.at_ref, bf16[1024,768]{1,0:T(8,128)(2,1)} %copy.17.refs_1_, bf16[384,8192]{1,0:T(8,128)(2,1)} %refs_2_.7, bf16[384,8192]{1,0:T(8,128)(2,1)} %collective-permute-done.4.refs_3_, s16[2,1056,256]{2,1,0:T(8,128)(2,1)} %copy-done.6), custom_call_target="tpu_custom_call" | custom-call | flops 1000 | bytes 1000 | tf_op jit(solution)/shard_map/partial_sums/pallas_call | solution.py:87
  74.4 2.2 %collective-permute-done.12 = f32[512,128]{1,0:T(8,128)} collective-permute-done((f32[512,128]{1,0:T(8,128)}, f32[512,128]{1,0:T(8,128)}, u32[]{:S(2)}, u32[]{:S(2)}) %collective-permute-start.12) | collective-permute-done | bytes 262176 | tf_op jit(solution)/shard_map/ppermute | solution.py:204
  76.6 3.0 %collective-permute-done.8.refs_5_.refs_4_ = s16[4,1056,256]{2,1,0:T(8,128)(2,1)} collective-permute-done((s16[4,1056,256]{2,1,0:T(8,128)(2,1)}, s16[4,1056,256]{2,1,0:T(8,128)(2,1)}, u32[]{:S(2)}, u32[]{:S(2)}) %collective-permute-start.8) | collective-permute-done | bytes 2162720 | tf_op jit(solution)/shard_map/ppermute | solution.py:199
  80.8 1.3 collective-permute-start.16
  82.1 2.0 %collective-permute-start.17 = (bf16[512,1024]{1,0:T(8,128)(2,1)}, bf16[512,1024]{1,0:T(8,128)(2,1)}, u32[]{:S(2)}, u32[]{:S(2)}) collective-permute-start(bf16[512,1024]{1,0:T(8,128)(2,1)} %collective-permute-done.9.refs_2_), channel_id=1, source_target_pairs={{0,1},{1,0},{2,3},{3,2},{4,5},{5,4},{6,7},{7,6},{8,9},{9,8},{10,11... | collective-permute-start | bytes 3145736 | tf_op jit(solution)/shard_map/ppermute | solution.py:199
  84.1 1.8 slice_subtract_fusion
  85.9 2.6 %collective-permute-start.18 = (f32[512,128]{1,0:T(8,128)S(1)}, f32[512,128]{1,0:T(8,128)}, u32[]{:S(2)}, u32[]{:S(2)}) collective-permute-start(f32[512,128]{1,0:T(8,128)S(1)} %get-tuple-element.79), channel_id=1, source_target_pairs={{0,64},{16,80},{32,96},{48,112},{64,0},{80,16},{96,32},{112,48},{1... | collective-permute-start | bytes 786440 | tf_op jit(solution)/shard_map/ppermute | solution.py:204
  88.5 6.7 %grad_columns.5.refs_5_ = f32[384,8192]{1,0:T(8,128)} custom-call(s32[34]{0:T(128)} %fusion.refs_0_.at_ref, bf16[384,1024]{1,0:T(8,128)(2,1)} %copy-done, bf16[1024,1024]{1,0:T(8,128)(2,1)} %collective-permute-done.10.refs_2_.refs_3_, bf16[1024,1024]{1,0:T(8,128)(2,1)} %collective-permute-done.10.refs_2_.refs_3_, ...), custom_call_target="tpu_custom_call", output_to_operand_aliasing={{}: (6, {})} | custom-call | flops 1000 | bytes 1000 | tf_op jit(solution)/shard_map/grad_columns/pallas_call | solution.py:144
  95.3 1.6 copy.18.refs_1_
  96.8 8.9 %collective-permute-done.15.refs_6_ = s16[2,1056,256]{2,1,0:T(8,128)(2,1)} collective-permute-done((s16[2,1056,256]{2,1,0:T(8,128)(2,1)}, s16[2,1056,256]{2,1,0:T(8,128)(2,1)}, u32[]{:S(2)}, u32[]{:S(2)}) %collective-permute-start.15) | collective-permute-done | bytes 1081376 | tf_op jit(solution)/shard_map/ppermute | solution.py:199
  105.8 7.7 %partial_sums.6 = (s16[2,1056,256]{2,1,0:T(8,128)(2,1)}, s16[2,1056,256]{2,1,0:T(8,128)(2,1)}) custom-call(s32[34]{0:T(128)} %fusion.refs_0_.at_ref, bf16[1024,768]{1,0:T(8,128)(2,1)} %copy.18.refs_1_, bf16[384,8192]{1,0:T(8,128)(2,1)} %refs_2_.7, bf16[384,8192]{1,0:T(8,128)(2,1)} %collective-permute-done.4.refs_3_, s16[2,1056,256]{2,1,0:T(8,128)(2,1)} %copy-done.7, ...), custom_call_target="tpu_custom_call" | custom-call | flops 1000 | bytes 1000 | tf_op jit(solution)/shard_map/partial_sums/pallas_call | solution.py:87
  113.5 1.7 collective-permute-start.19
  115.3 1.3 collective-permute-start.23
  117.6 1.7 collective-permute-start.20
  119.3 2.2 %collective-permute-start.21 = (f32[1024,128]{1,0:T(8,128)S(1)}, f32[1024,128]{1,0:T(8,128)S(1)}, u32[]{:S(2)}, u32[]{:S(2)}) collective-permute-start(f32[1024,128]{1,0:T(8,128)S(1)} %constant_dynamic-update-slice_fusion.refs_0_), channel_id=1, source_target_pairs={{0,48},{16,0},{32,16},{48,32},{64,112},{80,64},{96,80},{112,96},{1... | collective-permute-start | bytes 1572872 | tf_op jit(solution)/shard_map/ppermute | solution.py:204
  121.5 5.8 %grad_columns.6.refs_7_ = f32[384,8192]{1,0:T(8,128)} custom-call(s32[34]{0:T(128)} %fusion.refs_0_.at_ref, bf16[384,1024]{1,0:T(8,128)(2,1)} %copy-done, bf16[512,1024]{1,0:T(8,128)(2,1)} %collective-permute-done.9.refs_2_, bf16[512,1024]{1,0:T(8,128)(2,1)} %collective-permute-done.17.refs_3_, ...), custom_call_target="tpu_custom_call", output_to_operand_aliasing={{}: (5, {})} | custom-call | flops 1000 | bytes 1000 | tf_op jit(solution)/shard_map/grad_columns/pallas_call | solution.py:144
  127.3 1.6 copy.19.refs_1_
  128.9 21.8 %collective-permute-done.22.refs_5_ = s16[2,1056,256]{2,1,0:T(8,128)(2,1)} collective-permute-done((s16[2,1056,256]{2,1,0:T(8,128)(2,1)}, s16[2,1056,256]{2,1,0:T(8,128)(2,1)}, u32[]{:S(2)}, u32[]{:S(2)}) %collective-permute-start.22) | collective-permute-done | bytes 1081376 | tf_op jit(solution)/shard_map/ppermute | solution.py:199
  150.7 5.8 %partial_sums.7 = (s16[1,1056,256]{2,1,0:T(8,128)(2,1)}, f32[512,1024]{1,0:T(8,128)}) custom-call(s32[34]{0:T(128)} %fusion.refs_0_.at_ref, bf16[1024,768]{1,0:T(8,128)(2,1)} %copy.19.refs_1_, bf16[384,8192]{1,0:T(8,128)(2,1)} %refs_2_.7, bf16[384,8192]{1,0:T(8,128)(2,1)} %collective-permute-done.4.refs_3_, ...), custom_call_target="tpu_custom_call" | custom-call | flops 1000 | bytes 1000 | tf_op jit(solution)/shard_map/partial_sums/pallas_call | solution.py:87
  156.6 5.4 %collective-permute-start.25 = (bf16[1024,1024]{1,0:T(8,128)(2,1)}, bf16[1024,1024]{1,0:T(8,128)(2,1)S(1)}, u32[]{:S(2)}, u32[]{:S(2)}) collective-permute-start(bf16[1024,1024]{1,0:T(8,128)(2,1)} %collective-permute-done.19.refs_3_.refs_4_), channel_id=1, source_target_pairs={{0,1},{1,0},{2,3},{3,2},{4,5},{5,4},{6,7},{7,6},{8,9},{9,8},{10,11... | collective-permute-start | bytes 6291464 | tf_op jit(solution)/shard_map/ppermute | solution.py:199
  162.5 1.7 collective-permute-start.27
  164.9 2.1 %collective-permute-start.28 = (f32[512,128]{1,0:T(8,128)}, f32[512,128]{1,0:T(8,128)}, u32[]{:S(2)}, u32[]{:S(2)}) collective-permute-start(f32[512,128]{1,0:T(8,128)} %slice.27), channel_id=1, source_target_pairs={{0,48},{16,0},{32,16},{48,32},{64,112},{80,64},{96,80},{112,96},{1... | collective-permute-start | bytes 786440 | tf_op jit(solution)/shard_map/ppermute | solution.py:204
  167.1 1.3 fusion.1.at_ref
  168.3 4.7 %collective-permute-done.27 = f32[512,128]{1,0:T(8,128)} collective-permute-done((f32[512,128]{1,0:T(8,128)S(1)}, f32[512,128]{1,0:T(8,128)}, u32[]{:S(2)}, u32[]{:S(2)}) %collective-permute-start.27) | collective-permute-done | bytes 262176 | tf_op jit(solution)/shard_map/ppermute | solution.py:204
  173.2 1.9 pad_maximum_fusion.2.refs_3_
  175.0 3.0 %last_rows.1 = f32[512,1024]{1,0:T(8,128)} custom-call(s32[34]{0:T(128)} %fusion.refs_0_.at_ref, s16[1,1056,256]{2,1,0:T(8,128)(2,1)} %collective-permute-done.26.add_ref, f32[512,1024]{1,0:T(8,128)} %get-tuple-element.94._), custom_call_target="tpu_custom_call", output_to_operand_aliasing={{}: (2, {})} | custom-call | flops 1000 | bytes 1000 | tf_op jit(solution)/shard_map/last_rows/pallas_call | solution.py:104
  178.1 1.3 copy-done.1
  179.4 7.9 %grad_columns.7 = f32[384,8192]{1,0:T(8,128)} custom-call(s32[34]{0:T(128)} %fusion.refs_0_.at_ref, bf16[384,1024]{1,0:T(8,128)(2,1)} %copy-done, bf16[512,1024]{1,0:T(8,128)(2,1)} %collective-permute-done.24.refs_2_, bf16[1024,1024]{1,0:T(8,128)(2,1)} %collective-permute-done.19.refs_3_.refs_4_, ...), custom_call_target="tpu_custom_call", output_to_operand_aliasing={{}: (7, {})} | custom-call | flops 1000 | bytes 1000 | tf_op jit(solution)/shard_map/grad_columns/pallas_call | solution.py:144
  187.3 5.2 %assembled.1 = f32[512,1024]{1,0:T(8,128)} custom-call(s32[8]{0:T(128)} %fusion.1.at_ref, f32[1024,128]{1,0:T(8,128)} %copy-done.5, f32[1024,128]{1,0:T(8,128)} %copy-done.3, f32[1024,128]{1,0:T(8,128)} %copy-done.4, f32[1024,128]{1,0:T(8,128)} %pad_maximum_fusion.2.refs_3_), custom_call_target="tpu_custom_call" | custom-call | flops 1000 | bytes 1000 | tf_op jit(solution)/shard_map/assembled/pallas_call | solution.py:174
  (70 shorter events, 15.0 us)
Async XLA Ops:
  0.6 23.9 %collective-permute-start.4 = (bf16[384,8192]{1,0:T(8,128)(2,1)}, bf16[384,8192]{1,0:T(8,128)(2,1)}, u32[]{:S(2)}, u32[]{:S(2)}) collective-permute-start(bf16[384,8192]{1,0:T(8,128)(2,1)} %refs_2_.7), channel_id=1, source_target_pairs={{0,1},{1,0},{2,3},{3,2},{4,5},{5,4},{6,7},{7,6},{8,9},{9,8},{10,11... | collective-permute-start | bytes 18874376 | tf_op jit(solution)/shard_map/ppermute | solution.py:199
  2.1 14.3 %copy-start.10 = (s32[384]{0:T(512)S(1)}, s32[384]{0:T(512)}, u32[]{:S(2)}) copy-start(s32[384]{0:T(512)} %param.8) | copy-start | bytes 4612
  2.1 14.3 %copy-start.8 = (bf16[384,1024]{1,0:T(8,128)(2,1)S(1)}, bf16[384,1024]{1,0:T(8,128)(2,1)}, u32[]{:S(2)}) copy-start(bf16[384,1024]{1,0:T(8,128)(2,1)} %param.10) | copy-start | bytes 2359300
  2.1 14.6 %copy-start.2 = (bf16[1,512,1024]{2,1,0:T(8,128)(2,1)S(1)}, bf16[1,512,1024]{2,1,0:T(8,128)(2,1)}, u32[]{:S(2)}) copy-start(bf16[1,512,1024]{2,1,0:T(8,128)(2,1)} %param.11) | copy-start | bytes 3145732
  2.1 8.9 %collective-permute-start = (bf16[512,1024]{1,0:T(8,128)(2,1)}, bf16[512,1024]{1,0:T(8,128)(2,1)S(1)}, u32[]{:S(2)}, u32[]{:S(2)}) collective-permute-start(bf16[512,1024]{1,0:T(8,128)(2,1)} %bitcast.20), channel_id=1, source_target_pairs={{0,1},{1,0},{2,3},{3,2},{4,5},{5,4},{6,7},{7,6},{8,9},{9,8},{10,11... | collective-permute-start | bytes 3145736 | tf_op jit(solution)/shard_map/ppermute | solution.py:199
  13.9 27.3 %collective-permute-start.1 = (bf16[1024,1024]{1,0:T(8,128)(2,1)}, bf16[1024,1024]{1,0:T(8,128)(2,1)}, u32[]{:S(2)}, u32[]{:S(2)}) collective-permute-start(bf16[1024,1024]{1,0:T(8,128)(2,1)} %pad_maximum_fusion.refs_2_.refs_3_), channel_id=1, source_target_pairs={{0,2},{1,7},{2,4},{3,1},{4,6},{5,3},{6,0},{7,5},{8,10},{9,15},{10,... | collective-permute-start | bytes 6291464 | tf_op jit(solution)/shard_map/ppermute | solution.py:199
  16.6 11.4 %copy-start = (bf16[384,1024]{1,0:T(8,128)(2,1)}, bf16[384,1024]{1,0:T(8,128)(2,1)S(1)}, u32[]{:S(2)}) copy-start(bf16[384,1024]{1,0:T(8,128)(2,1)S(1)} %broadcast_multiply_fusion.refs_1_) | copy-start | bytes 2359300
  16.6 7.5 %collective-permute-start.3 = (bf16[384,1024]{1,0:T(8,128)(2,1)S(1)}, bf16[384,1024]{1,0:T(8,128)(2,1)}, u32[]{:S(2)}, u32[]{:S(2)}) collective-permute-start(bf16[384,1024]{1,0:T(8,128)(2,1)S(1)} %broadcast_multiply_fusion.refs_1_), channel_id=1, source_target_pairs={{0,1},{1,0},{2,3},{3,2},{4,5},{5,4},{6,7},{7,6},{8,9},{9,8},{10,11... | collective-permute-start | bytes 2359304 | tf_op jit(solution)/shard_map/ppermute | solution.py:199
  16.7 24.5 %collective-permute-start.2 = (bf16[512,1024]{1,0:T(8,128)(2,1)S(1)}, bf16[512,1024]{1,0:T(8,128)(2,1)}, u32[]{:S(2)}, u32[]{:S(2)}) collective-permute-start(bf16[512,1024]{1,0:T(8,128)(2,1)S(1)} %bitcast.22), channel_id=1, source_target_pairs={{0,8},{1,9},{2,10},{3,11},{4,12},{5,13},{6,14},{7,15},{8,0},{9,1},... | collective-permute-start | bytes 3145736 | tf_op jit(solution)/shard_map/ppermute | solution.py:199
  19.0 21.1 %collective-permute-start.7 = (bf16[1024,128]{1,0:T(8,128)(2,1)}, bf16[1024,128]{1,0:T(8,128)(2,1)}, u32[]{:S(2)}, u32[]{:S(2)}) collective-permute-start(bf16[1024,128]{1,0:T(8,128)(2,1)} %pad_maximum_fusion.5), channel_id=1, source_target_pairs={{0,32},{16,48},{32,0},{48,16},{64,96},{80,112},{96,64},{112,80},{1... | collective-permute-start | bytes 786440 | tf_op jit(solution)/shard_map/ppermute | solution.py:204
  24.1 16.1 %collective-permute-start.6 = (bf16[1024,128]{1,0:T(8,128)(2,1)}, bf16[1024,128]{1,0:T(8,128)(2,1)}, u32[]{:S(2)}, u32[]{:S(2)}) collective-permute-start(bf16[1024,128]{1,0:T(8,128)(2,1)} %pad_maximum_fusion.4), channel_id=1, source_target_pairs={{0,48},{16,0},{32,16},{48,32},{64,112},{80,64},{96,80},{112,96},{1... | collective-permute-start | bytes 786440 | tf_op jit(solution)/shard_map/ppermute | solution.py:204
  24.5 15.7 %collective-permute-start.5 = (bf16[1024,128]{1,0:T(8,128)(2,1)}, bf16[1024,128]{1,0:T(8,128)(2,1)}, u32[]{:S(2)}, u32[]{:S(2)}) collective-permute-start(bf16[1024,128]{1,0:T(8,128)(2,1)} %pad_maximum_fusion.3), channel_id=1, source_target_pairs={{0,16},{16,32},{32,48},{48,0},{64,80},{80,96},{96,112},{112,64},{1... | collective-permute-start | bytes 786440 | tf_op jit(solution)/shard_map/ppermute | solution.py:204
  41.2 38.3 %collective-permute-start.8 = (s16[4,1056,256]{2,1,0:T(8,128)(2,1)}, s16[4,1056,256]{2,1,0:T(8,128)(2,1)}, u32[]{:S(2)}, u32[]{:S(2)}) collective-permute-start(s16[4,1056,256]{2,1,0:T(8,128)(2,1)} %get-tuple-element.55), channel_id=1, source_target_pairs={{0,6},{1,3},{2,0},{3,5},{4,2},{5,7},{6,4},{7,1},{8,14},{9,11},{10,... | collective-permute-start | bytes 6488072 | tf_op jit(solution)/shard_map/ppermute | solution.py:199
  41.9 34.7 %collective-permute-start.10 = (bf16[1024,1024]{1,0:T(8,128)(2,1)}, bf16[1024,1024]{1,0:T(8,128)(2,1)}, u32[]{:S(2)}, u32[]{:S(2)}) collective-permute-start(bf16[1024,1024]{1,0:T(8,128)(2,1)} %collective-permute-done.1.refs_4_.refs_5_), channel_id=1, source_target_pairs={{0,1},{1,0},{2,3},{3,2},{4,5},{5,4},{6,7},{7,6},{8,9},{9,8},{10,11... | collective-permute-start | bytes 6291464 | tf_op jit(solution)/shard_map/ppermute | solution.py:199
  43.3 9.2 %collective-permute-start.11 = (bf16[512,1024]{1,0:T(8,128)(2,1)}, bf16[512,1024]{1,0:T(8,128)(2,1)}, u32[]{:S(2)}, u32[]{:S(2)}) collective-permute-start(bf16[512,1024]{1,0:T(8,128)(2,1)} %collective-permute-done.2), channel_id=1, source_target_pairs={{0,1},{1,0},{2,3},{3,2},{4,5},{5,4},{6,7},{7,6},{8,9},{9,8},{10,11... | collective-permute-start | bytes 3145736 | tf_op jit(solution)/shard_map/ppermute | solution.py:199
  43.3 25.2 %collective-permute-start.13 = (s16[2,1056,256]{2,1,0:T(8,128)(2,1)}, s16[2,1056,256]{2,1,0:T(8,128)(2,1)S(1)}, u32[]{:S(2)}, u32[]{:S(2)}) collective-permute-start(s16[2,1056,256]{2,1,0:T(8,128)(2,1)} %get-tuple-element.63), channel_id=1, source_target_pairs={{0,8},{1,9},{2,10},{3,11},{4,12},{5,13},{6,14},{7,15},{8,0},{9,1},... | collective-permute-start | bytes 3244040 | tf_op jit(solution)/shard_map/ppermute | solution.py:199
  46.9 29.7 %collective-permute-start.9 = (bf16[512,1024]{1,0:T(8,128)(2,1)}, bf16[512,1024]{1,0:T(8,128)(2,1)}, u32[]{:S(2)}, u32[]{:S(2)}) collective-permute-start(bf16[512,1024]{1,0:T(8,128)(2,1)} %slice.21), channel_id=1, source_target_pairs={{0,2},{1,7},{2,4},{3,1},{4,6},{5,3},{6,0},{7,5},{8,10},{9,15},{10,... | collective-permute-start | bytes 3145736 | tf_op jit(solution)/shard_map/ppermute | solution.py:199
  52.6 24.1 %collective-permute-start.12 = (f32[512,128]{1,0:T(8,128)}, f32[512,128]{1,0:T(8,128)}, u32[]{:S(2)}, u32[]{:S(2)}) collective-permute-start(f32[512,128]{1,0:T(8,128)} %slice.28), channel_id=1, source_target_pairs={{0,64},{16,80},{32,96},{48,112},{64,0},{80,16},{96,32},{112,48},{1... | collective-permute-start | bytes 786440 | tf_op jit(solution)/shard_map/ppermute | solution.py:204
  66.5 17.6 %copy-start.9 = (f32[512,128]{1,0:T(8,128)S(1)}, f32[512,128]{1,0:T(8,128)}, u32[]{:S(2)}) copy-start(f32[512,128]{1,0:T(8,128)} %param.13) | copy-start | bytes 786436
  68.5 1.0 copy-start.6
  79.6 17.2 %collective-permute-start.14 = (s16[2,1056,256]{2,1,0:T(8,128)(2,1)}, s16[2,1056,256]{2,1,0:T(8,128)(2,1)S(1)}, u32[]{:S(2)}, u32[]{:S(2)}) collective-permute-start(s16[2,1056,256]{2,1,0:T(8,128)(2,1)} %partial_sums.5), channel_id=1, source_target_pairs={{0,2},{1,7},{2,4},{3,1},{4,6},{5,3},{6,0},{7,5},{8,10},{9,15},{10,... | collective-permute-start | bytes 3244040 | tf_op jit(solution)/shard_map/ppermute | solution.py:199
  80.3 25.5 %collective-permute-start.15 = (s16[2,1056,256]{2,1,0:T(8,128)(2,1)}, s16[2,1056,256]{2,1,0:T(8,128)(2,1)}, u32[]{:S(2)}, u32[]{:S(2)}) collective-permute-start(s16[2,1056,256]{2,1,0:T(8,128)(2,1)} %get-tuple-element.68), channel_id=1, source_target_pairs={{0,2},{1,7},{2,4},{3,1},{4,6},{5,3},{6,0},{7,5},{8,10},{9,15},{10,... | collective-permute-start | bytes 3244040 | tf_op jit(solution)/shard_map/ppermute | solution.py:199
  80.8 32.7 %collective-permute-start.16 = (bf16[512,1024]{1,0:T(8,128)(2,1)}, bf16[512,1024]{1,0:T(8,128)(2,1)}, u32[]{:S(2)}, u32[]{:S(2)}) collective-permute-start(bf16[512,1024]{1,0:T(8,128)(2,1)} %collective-permute-done.9.refs_2_), channel_id=1, source_target_pairs={{0,8},{1,9},{2,10},{3,11},{4,12},{5,13},{6,14},{7,15},{8,0},{9,1},... | collective-permute-start | bytes 3145736 | tf_op jit(solution)/shard_map/ppermute | solution.py:199
  82.1 31.4 %collective-permute-start.17 = (bf16[512,1024]{1,0:T(8,128)(2,1)}, bf16[512,1024]{1,0:T(8,128)(2,1)}, u32[]{:S(2)}, u32[]{:S(2)}) collective-permute-start(bf16[512,1024]{1,0:T(8,128)(2,1)} %collective-permute-done.9.refs_2_), channel_id=1, source_target_pairs={{0,1},{1,0},{2,3},{3,2},{4,5},{5,4},{6,7},{7,6},{8,9},{9,8},{10,11... | collective-permute-start | bytes 3145736 | tf_op jit(solution)/shard_map/ppermute | solution.py:199
  85.9 27.6 %collective-permute-start.18 = (f32[512,128]{1,0:T(8,128)S(1)}, f32[512,128]{1,0:T(8,128)}, u32[]{:S(2)}, u32[]{:S(2)}) collective-permute-start(f32[512,128]{1,0:T(8,128)S(1)} %get-tuple-element.79), channel_id=1, source_target_pairs={{0,64},{16,80},{32,96},{48,112},{64,0},{80,16},{96,32},{112,48},{1... | collective-permute-start | bytes 786440 | tf_op jit(solution)/shard_map/ppermute | solution.py:204
  96.8 9.0 %copy-start.7 = (s16[2,1056,256]{2,1,0:T(8,128)(2,1)}, s16[2,1056,256]{2,1,0:T(8,128)(2,1)S(1)}, u32[]{:S(2)}) copy-start(s16[2,1056,256]{2,1,0:T(8,128)(2,1)S(1)} %collective-permute-done.14.refs_4_) | copy-start | bytes 3244036
  113.5 43.0 %collective-permute-start.19 = (bf16[1024,1024]{1,0:T(8,128)(2,1)}, bf16[1024,1024]{1,0:T(8,128)(2,1)}, u32[]{:S(2)}, u32[]{:S(2)}) collective-permute-start(bf16[1024,1024]{1,0:T(8,128)(2,1)} %pad_maximum_fusion.1.refs_4_.refs_5_), channel_id=1, source_target_pairs={{0,2},{1,7},{2,4},{3,1},{4,6},{5,3},{6,0},{7,5},{8,10},{9,15},{10,... | collective-permute-start | bytes 6291464 | tf_op jit(solution)/shard_map/ppermute | solution.py:199
  115.2 35.4 %collective-permute-start.22 = (s16[2,1056,256]{2,1,0:T(8,128)(2,1)}, s16[2,1056,256]{2,1,0:T(8,128)(2,1)}, u32[]{:S(2)}, u32[]{:S(2)}) collective-permute-start(s16[2,1056,256]{2,1,0:T(8,128)(2,1)} %get-tuple-element.86), channel_id=1, source_target_pairs={{0,2},{1,7},{2,4},{3,1},{4,6},{5,3},{6,0},{7,5},{8,10},{9,15},{10,... | collective-permute-start | bytes 3244040 | tf_op jit(solution)/shard_map/ppermute | solution.py:199
  115.3 35.4 %collective-permute-start.23 = (s16[2,1056,256]{2,1,0:T(8,128)(2,1)}, s16[2,1056,256]{2,1,0:T(8,128)(2,1)}, u32[]{:S(2)}, u32[]{:S(2)}) collective-permute-start(s16[2,1056,256]{2,1,0:T(8,128)(2,1)} %get-tuple-element.87), channel_id=1, source_target_pairs={{0,8},{1,9},{2,10},{3,11},{4,12},{5,13},{6,14},{7,15},{8,0},{9,1},... | collective-permute-start | bytes 3244040 | tf_op jit(solution)/shard_map/ppermute | solution.py:199
  117.6 9.7 %copy-start.5 = (f32[1024,128]{1,0:T(8,128)}, f32[1024,128]{1,0:T(8,128)S(1)}, u32[]{:S(2)}) copy-start(f32[1024,128]{1,0:T(8,128)S(1)} %constant_dynamic-update-slice_fusion.refs_0_) | copy-start | bytes 1572868
  117.6 38.9 %collective-permute-start.20 = (f32[1024,128]{1,0:T(8,128)S(1)}, f32[1024,128]{1,0:T(8,128)S(1)}, u32[]{:S(2)}, u32[]{:S(2)}) collective-permute-start(f32[1024,128]{1,0:T(8,128)S(1)} %constant_dynamic-update-slice_fusion.refs_0_), channel_id=1, source_target_pairs={{0,16},{16,32},{32,48},{48,0},{64,80},{80,96},{96,112},{112,64},{1... | collective-permute-start | bytes 1572872 | tf_op jit(solution)/shard_map/ppermute | solution.py:204
  119.3 37.2 %collective-permute-start.21 = (f32[1024,128]{1,0:T(8,128)S(1)}, f32[1024,128]{1,0:T(8,128)S(1)}, u32[]{:S(2)}, u32[]{:S(2)}) collective-permute-start(f32[1024,128]{1,0:T(8,128)S(1)} %constant_dynamic-update-slice_fusion.refs_0_), channel_id=1, source_target_pairs={{0,48},{16,0},{32,16},{48,32},{64,112},{80,64},{96,80},{112,96},{1... | collective-permute-start | bytes 1572872 | tf_op jit(solution)/shard_map/ppermute | solution.py:204
  156.5 21.5 %copy-start.3 = (f32[1024,128]{1,0:T(8,128)}, f32[1024,128]{1,0:T(8,128)S(1)}, u32[]{:S(2)}) copy-start(f32[1024,128]{1,0:T(8,128)S(1)} %collective-permute-done.20.refs_1_) | copy-start | bytes 1572868
  156.5 21.5 %copy-start.4 = (f32[1024,128]{1,0:T(8,128)}, f32[1024,128]{1,0:T(8,128)S(1)}, u32[]{:S(2)}) copy-start(f32[1024,128]{1,0:T(8,128)S(1)} %collective-permute-done.21.refs_2_) | copy-start | bytes 1572868
  156.6 21.5 %collective-permute-start.25 = (bf16[1024,1024]{1,0:T(8,128)(2,1)}, bf16[1024,1024]{1,0:T(8,128)(2,1)S(1)}, u32[]{:S(2)}, u32[]{:S(2)}) collective-permute-start(bf16[1024,1024]{1,0:T(8,128)(2,1)} %collective-permute-done.19.refs_3_.refs_4_), channel_id=1, source_target_pairs={{0,1},{1,0},{2,3},{3,2},{4,5},{5,4},{6,7},{7,6},{8,9},{9,8},{10,11... | collective-permute-start | bytes 6291464 | tf_op jit(solution)/shard_map/ppermute | solution.py:199
  162.0 16.1 %collective-permute-start.24 = (bf16[512,1024]{1,0:T(8,128)(2,1)}, bf16[512,1024]{1,0:T(8,128)(2,1)}, u32[]{:S(2)}, u32[]{:S(2)}) collective-permute-start(bf16[512,1024]{1,0:T(8,128)(2,1)} %collective-permute-done.16.refs_4_), channel_id=1, source_target_pairs={{0,1},{1,0},{2,3},{3,2},{4,5},{5,4},{6,7},{7,6},{8,9},{9,8},{10,11... | collective-permute-start | bytes 3145736 | tf_op jit(solution)/shard_map/ppermute | solution.py:199
  162.1 13.0 %collective-permute-start.26 = (s16[1,1056,256]{2,1,0:T(8,128)(2,1)}, s16[1,1056,256]{2,1,0:T(8,128)(2,1)}, u32[]{:S(2)}, u32[]{:S(2)}) collective-permute-start(s16[1,1056,256]{2,1,0:T(8,128)(2,1)} %get-tuple-element.93), channel_id=1, source_target_pairs={{0,1},{1,0},{2,3},{3,2},{4,5},{5,4},{6,7},{7,6},{8,9},{9,8},{10,11... | collective-permute-start | bytes 1622024 | tf_op jit(solution)/shard_map/ppermute | solution.py:199
  162.5 10.5 %collective-permute-start.27 = (f32[512,128]{1,0:T(8,128)S(1)}, f32[512,128]{1,0:T(8,128)}, u32[]{:S(2)}, u32[]{:S(2)}) collective-permute-start(f32[512,128]{1,0:T(8,128)S(1)} %slice.26), channel_id=1, source_target_pairs={{0,16},{16,32},{32,48},{48,0},{64,80},{80,96},{96,112},{112,64},{1... | collective-permute-start | bytes 786440 | tf_op jit(solution)/shard_map/ppermute | solution.py:204
  164.9 8.2 %collective-permute-start.28 = (f32[512,128]{1,0:T(8,128)}, f32[512,128]{1,0:T(8,128)}, u32[]{:S(2)}, u32[]{:S(2)}) collective-permute-start(f32[512,128]{1,0:T(8,128)} %slice.27), channel_id=1, source_target_pairs={{0,48},{16,0},{32,16},{48,32},{64,112},{80,64},{96,80},{112,96},{1... | collective-permute-start | bytes 786440 | tf_op jit(solution)/shard_map/ppermute | solution.py:204
  178.1 1.3 copy-start.1

commit v2 on v1

--- a/solution.py
+++ b/solution.py
@@ -158,32 +158,29 @@
 
 
 def assemble_kernel(at_ref, *refs):
-    step = pl.program_id(0)
     out_ref = refs[-1]
-    for j in range(4):
-        for k in range(2):
-
-            @pl.when(step == 2 * j + k)
-            def _(piece=refs[j], k=k):
-                rows = out_ref.shape[0]
-                out_ref[...] = piece[k * rows : (k + 1) * rows, :]
+    for k, piece in enumerate(refs[:-1]):
+        width = piece.shape[1]
+        out_ref[:, pl.ds(pl.multiple_of(at_ref[k] * width, width), width)] = piece[...]
 
 
 def assembled(pieces, places):
-    rows, width = pieces[0].shape
+    both_rows, width = pieces[0].shape
+    rows, steps = both_rows // 2, 4
+    tile = rows // steps
     return pl.pallas_call(
         assemble_kernel,
         grid_spec=pltpu.PrefetchScalarGridSpec(
             num_scalar_prefetch=1,
-            grid=(8,),
-            in_specs=[pl.BlockSpec((rows, width), lambda i, at: (0, 0))] * 4,
-            out_specs=pl.BlockSpec((rows // 2, width), lambda i, at: (0, at[i])),
-        ),
-        out_shape=jax.ShapeDtypeStruct((rows // 2, 8 * width), jnp.float32),
+            grid=(steps,),
+            in_specs=[pl.BlockSpec((tile, width), lambda i, at, k=k: (k * steps + i, 0)) for _ in pieces for k in range(2)],
+            out_specs=pl.BlockSpec((tile, 8 * width), lambda i, at: (i, 0)),
+        ),
+        out_shape=jax.ShapeDtypeStruct((rows, 8 * width), jnp.float32),
         compiler_params=pltpu.CompilerParams(vmem_limit_bytes=vmem),
         cost_estimate=tiny,
         name="assembled",
-    )(places, *pieces)
+    )(places, *[piece for piece in pieces for _ in range(2)])
 
 
 def group_columns(array, zz, h, width):
@@ -231,8 +228,8 @@
             ("cores", [o, c]),
             ("grad1", places((0, 0, c), (0, 0, o), (0, -s, c), (0, -s, o))),
             ("grad2", places((0, s, o), (0, s, c), (1, 0, c), (1, 0, o))),
-            ("grad3", places((0, 2, c), (0, 2, o), (1, 2, c))),
-            ("grad4", places((1, 2, o), (1, -s, c), (1, -s, o), (1, s, o), (1, s, c))),
+            ("grad3", places((0, 2, c), (0, 2, o), (1, 2, c), (1, -s, c), (1, s, o))),
+            ("grad4", places((1, 2, o), (1, -s, o), (1, s, c))),
         ):
             starts[name] = len(row)
             row += entries
@@ -263,37 +260,45 @@
         return sums(at, starts[name], mt, normed_inputs, x_sib, *args, **kw)
 
     x_sib = sent(normed_inputs, to_core)
+    f1, v, w_s = sent(w, ahead), sent(w, to_y), sent(w, to_core)
     live_rows = (token_ids != 0).astype(jnp.bfloat16)[:, None]
     masked = kv_cotangent * live_rows
     masked_sib = sent(masked, to_core)
-    both = jnp.concatenate([w, sent(w, to_core)], axis=0)
-    f, v = sent(both, ahead), sent(w, to_y)
     mt = jnp.concatenate([masked, masked_sib], axis=0).T
-    z1, z3, z2 = (sent_rep(group_columns(w, (gz + dz) % 4, gh, width), dz=dz) for dz in (1, 3, 2))
+    w_z, masked_sib, w_s = together(w, masked_sib, w_s)
+    c1, c2, c3 = (group_columns(w_z, (gz + dz) % 4, gh, width) for dz in (1, 2, 3))
+    w_later, f1, mt, at, rep_at, c1, c2, c3 = together(w_s, f1, mt, at, rep_at, c1, c2, c3)
+    f2 = sent(w_later, ahead)
+    z2, z3 = sent_rep(c2, dz=2), sent_rep(c3, dz=3)
+    c1, x_sib = together(c1, x_sib)
+    z1 = sent_rep(c1, dz=1)
     far_y, b, near_o = part_sums("first", [(2, [], False), (4, [], False), (2, [], False)])
-    both, f, v, far_y, b, near_o, z1, z3, z2, mt = together(both, f, v, far_y, b, near_o, z1, z3, z2, mt)
-
-    b, f3, far_y = sent(b, behind), sent(f[:block], ahead), sent(far_y, to_y)
-    d, v_s = sent(f, to_core), sent(v, to_core)
+    w, w_s, f1, f2, v, far_y, b, near_o, z1, z3, z2 = together(w, w_s, f1, f2, v, far_y, b, near_o, z1, z3, z2)
+
+    b, f3, far_y = sent(b, behind), sent(f1, ahead), sent(far_y, to_y)
+    d1, d2 = sent(f1, to_core), sent(f2, to_core)
+    v_later, f1, d1 = together(v, f1, d1)
+    v_s = sent(v_later, to_core)
     snap = group_columns(snapshot, gz, gh, width).astype(jnp.float32)
-    total = snap - group_columns(both[:block], gz, gh, width).astype(jnp.float32)
+    total = snap - group_columns(w, gz, gh, width).astype(jnp.float32)
     for part in (z1, z3, z2):
         total = total + (snap - part.astype(jnp.float32))
+    total, f2, d2 = together(total, f2, d2)
     total_in = sent_rep(total[rows:], dh=1)
-    grad = columns("grad1", [(both, 0), (both, 1), (f, 0), (f, 1)], None)
-    v_both = jnp.concatenate([v, v_s], axis=0)
+    grad = columns("grad1", [(w, 0), (w_s, 0), (f1, 0), (f2, 0)], None)
     (far,) = part_sums("far", [(2, [0], False)], [(far_y, lambda i, at: i)])
-    b, f3, d, v_both, total, total_in, grad, far, near_o, mt = together(
-        b, f3, d, v_both, total, total_in, grad, far, near_o, mt
-    )
-
-    far, near_o, h = sent(far, ahead), sent(near_o, ahead), sent(f3, to_y)
-    d3 = sent(f3, to_core)
+    b, f3, d1, d2, v, v_s, total, total_in, grad, far, near_o = together(
+        b, f3, d1, d2, v, v_s, total, total_in, grad, far, near_o
+    )
+
+    far, near_o, h, d3 = sent(far, ahead), sent(near_o, ahead), sent(f3, to_y), sent(f3, to_core)
     outer_grad = (total[:rows] + total_in) / groups
     new_momentum = outer_beta * momentum + outer_grad
     new_part = snap[:rows] - outer_rate * (outer_grad + outer_beta * new_momentum)
     part_in = sent_rep(new_part, dh=1)
-    grad = columns("grad2", [(d, 0), (d, 1), (v_both, 0), (v_both, 1)], grad)
+    grad = columns("grad2", [(d1, 0), (d2, 0), (v, 0), (v_s, 0)], grad)
+    v_later, far, grad = together(v, far, grad)
+    g1 = sent(v_later, ahead)
     near, home_o = part_sums(
         "near",
         [(2, [0], False), (2, [1, 2], False)],
@@ -303,24 +308,26 @@
             (near_o, lambda i, at: jnp.clip(i - 2, 0, 1)),
         ],
     )
-    near, home_o, h, f3, d3, v_both, b, new_momentum, new_part, part_in, grad, mt = together(
-        near, home_o, h, f3, d3, v_both, b, new_momentum, new_part, part_in, grad, mt
-    )
-
-    near, g, from_y = sent(near, ahead), sent(v_both, ahead), sent(home_o, to_y)
+    near, home_o, h, f3, d3, v_s, g1, b, new_momentum, new_part, part_in, grad = together(
+        near, home_o, h, f3, d3, v_s, g1, b, new_momentum, new_part, part_in, grad
+    )
+
+    near, from_y, g2, e1 = sent(near, ahead), sent(home_o, to_y), sent(v_s, ahead), sent(g1, to_core)
     part = jnp.concatenate([new_part, part_in], axis=0)
-    z1, z3 = sent_rep(part, dz=1), sent_rep(part, dz=3)
-    grad = columns("grad3", [(f3, 0), (d3, 0), (h, 0)], grad)
+    z1 = sent_rep(part, dz=1)
+    part_later, e1 = together(part, e1)
+    z3 = sent_rep(part_later, dz=3)
+    grad = columns("grad3", [(f3, 0), (d3, 0), (h, 0), (g1, 0), (e1, 0)], grad)
     by_core = [(array, lambda i, at: at[starts["cores"] + i]) for array in (b, near, from_y)]
     for_other, weight_grad = part_sums(
         "home", [(1, [0, 1, 2], False), (1, [0, 1, 2], True)], by_core, final_at=starts["cores"] + 1
     )
-    h, g, part, z1, z3, grad, for_other, weight_grad = together(h, g, part, z1, z3, grad, for_other, weight_grad)
-
-    from_other, e, h_s = sent(for_other, to_core), sent(g, to_core), sent(h, to_core)
-    z2 = jnp.concatenate([sent_rep(z1[:rows], dz=1), sent_rep(z3[rows:], dz=3)], axis=0)
+    h, g2, part, z1, z3, grad, for_other, weight_grad = together(h, g2, part, z1, z3, grad, for_other, weight_grad)
+
+    from_other, e2, h_s = sent(for_other, to_core), sent(g2, to_core), sent(h, to_core)
+    z2 = sent_rep(z1, dz=1)
     weight_grad = last_rows(at, starts["cores"], from_other, weight_grad)
-    input_grad = columns("grad4", [(h_s, 0), (g, 0), (g, 1), (e, 0), (e, 1)], grad)
+    input_grad = columns("grad4", [(h_s, 0), (g2, 0), (e2, 0)], grad)
     rep_at, _ = together(rep_at, input_grad)
     new_weights = assembled([part, z1, z3, z2], rep_at)
     return input_grad, weight_grad[None], new_weights, new_momentum

time: 193 us -> 174 us (0.902)
  other arithmetic: 14.3 us -> 6.41 us
  local copies, waits for them, and re-layouts: 18.4 us -> 10.9 us
  starting transfers between devices: 41.8 us -> 34.9 us
  waiting for transfers between devices: 52.7 us -> 56.4 us
    concatenate x3 -> x0, other arithmetic: 7.7 us -> none  [the longest x1 3.03 us: per_device(): v_both = jnp.concatenate([v, v_s], axis=0)]
    ppermute x20 -> x24, waiting for transfers between devices: 45.7 us -> 51.3 us  [sent(): return lax.ppermute(array, 'fsdp', pairs)]
    ppermute x9 -> x8, starting transfers between devices: 18.1 us -> 13.2 us  [sent_rep(): return lax.ppermute(array, 'rep', pairs)]
    slice x4 -> x0, local copies, waits for them, and re-layouts: 4.3 us -> none  [the longest x1 2.27 us: per_device(): b, f3, far_y = (sent(b, behind), sent(f[:block], ahead), sent(far_y, to_y))]
    unnamed x23 -> x27, local copies, waits for them, and re-layouts: 2.39 us -> 5.53 us
    optimization_barrier x3 -> x1, local copies, waits for them, and re-layouts: 4.69 us -> 1.56 us  [together(): return lax.optimization_barrier(arrays)]
    concatenate x3 -> x2, other arithmetic: 2.17 us -> 0.06 us  [group_columns(): return jnp.concatenate([cut(h), cut(1 - h)], axis=0)]
    ppermute x20 -> x24, starting transfers between devices: 23.8 us -> 21.8 us  [sent(): return lax.ppermute(array, 'fsdp', pairs)]
  transfers between devices with their start and end apart: 29 -> 32, of which waited for: 9 -> 13; matrix products, arithmetic and copies ran while one was open for 16% -> 7% of each run, Pallas kernels for 27% -> 34%
where the time goes in v2:
time: 174 us; the launch traced here: 173 us
  Pallas kernels  63.7 us (37%)
  waiting for transfers between devices  56.4 us (32%)
  starting transfers between devices  34.9 us (20%)
  local copies, waits for them, and re-layouts  10.9 us (6%)
  other arithmetic  6.41 us (4%)
    ppermute x24, waiting for transfers between devices, sent(): return lax.ppermute(array, 'fsdp', pairs)  51.3 us
    pallas_call x4, Pallas kernels, sums(): pl.pallas_call(lambda *refs: sums_kernel(groups, len(adds), *refs), grid_...  29 us
    pallas_call x4, Pallas kernels, grad_columns(): pl.pallas_call(lambda *refs: columns_kernel(n, *refs), grid_spec=pltpu.Pr...  27.1 us
    ppermute x24, starting transfers between devices, sent(): return lax.ppermute(array, 'fsdp', pairs)  21.8 us
    ppermute x8, starting transfers between devices, sent_rep(): return lax.ppermute(array, 'rep', pairs)  13.2 us
    unnamed x27, local copies, waits for them, and re-layouts  5.53 us
    ppermute x8, waiting for transfers between devices, sent_rep(): return lax.ppermute(array, 'rep', pairs)  5.11 us
    pallas_call x1, Pallas kernels, assembled(): pl.pallas_call(assemble_kernel, grid_spec=pltpu.PrefetchScalarGridSpec(nu...  4.49 us
  transfers between devices with their start and end apart: 32, of which 13 were waited for; matrix products, arithmetic and copies ran while one was open for 7% of the time, Pallas kernels for 34%

profile of v2, /device:TPU:1, one launch (start us, length us, event | category | flops | bytes accessed | tf_op | source)
XLA Modules:
  0.0 173.2 jit_solution(5831929845733544649)
XLA Ops:
  0.6 1.5 collective-permute-start.3
  2.9 1.2 broadcast_multiply_fusion.refs_1_
  4.7 2.6 %collective-permute-start.2 = (bf16[512,1024]{1,0:T(8,128)(2,1)S(1)}, bf16[512,1024]{1,0:T(8,128)(2,1)}, u32[]{:S(2)}, u32[]{:S(2)}) collective-permute-start(bf16[512,1024]{1,0:T(8,128)(2,1)S(1)} %bitcast.10), channel_id=1, source_target_pairs={{0,2},{1,7},{2,4},{3,1},{4,6},{5,3},{6,0},{7,5},{8,10},{9,15},{10,... | collective-permute-start | bytes 3145736 | tf_op jit(solution)/shard_map/ppermute | solution.py:196
  7.3 1.3 collective-permute-start.5
  8.5 1.3 fusion.1.at_ref
  9.8 1.3 fusion.refs_0_.at_ref
  11.1 3.2 %collective-permute-done = bf16[384,1024]{1,0:T(8,128)(2,1)} collective-permute-done((bf16[384,1024]{1,0:T(8,128)(2,1)S(1)}, bf16[384,1024]{1,0:T(8,128)(2,1)}, u32[]{:S(2)}, u32[]{:S(2)}) %collective-permute-start) | collective-permute-done | bytes 786464 | tf_op jit(solution)/shard_map/ppermute | solution.py:196
  14.3 1.3 maximum_bitcast_fusion
  15.9 3.1 %collective-permute-done.2.refs_4_ = bf16[512,1024]{1,0:T(8,128)(2,1)} collective-permute-done((bf16[512,1024]{1,0:T(8,128)(2,1)S(1)}, bf16[512,1024]{1,0:T(8,128)(2,1)}, u32[]{:S(2)}, u32[]{:S(2)}) %collective-permute-start.2) | collective-permute-done | bytes 1048608 | tf_op jit(solution)/shard_map/ppermute | solution.py:196
  19.0 3.2 %collective-permute-start.4 = (bf16[512,1024]{1,0:T(8,128)(2,1)}, bf16[512,1024]{1,0:T(8,128)(2,1)}, u32[]{:S(2)}, u32[]{:S(2)}) collective-permute-start(bf16[512,1024]{1,0:T(8,128)(2,1)} %collective-permute-done.1.refs_3_), channel_id=1, source_target_pairs={{0,2},{1,7},{2,4},{3,1},{4,6},{5,3},{6,0},{7,5},{8,10},{9,15},{10,... | collective-permute-start | bytes 3145736 | tf_op jit(solution)/shard_map/ppermute | solution.py:196
  22.2 3.8 %collective-permute-start.7 = (bf16[1024,128]{1,0:T(8,128)(2,1)S(1)}, bf16[1024,128]{1,0:T(8,128)(2,1)}, u32[]{:S(2)}, u32[]{:S(2)}) collective-permute-start(bf16[1024,128]{1,0:T(8,128)(2,1)S(1)} %pad_maximum_fusion.2), channel_id=1, source_target_pairs={{0,48},{16,0},{32,16},{48,32},{64,112},{80,64},{96,80},{112,96},{1... | collective-permute-start | bytes 786440 | tf_op jit(solution)/shard_map/ppermute | solution.py:201
  26.7 1.6 copy.18.refs_1_
  28.2 10.6 %partial_sums.4 = (s16[2,1056,256]{2,1,0:T(8,128)(2,1)}, s16[4,1056,256]{2,1,0:T(8,128)(2,1)}, s16[2,1056,256]{2,1,0:T(8,128)(2,1)}) custom-call(s32[34]{0:T(128)} %fusion.refs_0_.at_ref, bf16[1024,768]{1,0:T(8,128)(2,1)} %copy.18.refs_1_, bf16[384,8192]{1,0:T(8,128)(2,1)} %refs_2_.7, bf16[384,8192]{1,0:T(8,128)(2,1)} %collective-permute-done.3.refs_3_), custom_call_target="tpu_custom_call" | custom-call | flops 1000 | bytes 1000 | tf_op jit(solution)/shard_map/partial_sums/pallas_call | solution.py:87
  38.9 1.9 %collective-permute-done.6 = bf16[1024,128]{1,0:T(8,128)(2,1)} collective-permute-done((bf16[1024,128]{1,0:T(8,128)(2,1)S(1)}, bf16[1024,128]{1,0:T(8,128)(2,1)}, u32[]{:S(2)}, u32[]{:S(2)}) %collective-permute-start.6) | collective-permute-done | bytes 262176 | tf_op jit(solution)/shard_map/ppermute | solution.py:201
  40.8 1.1 collective-permute-start.11
  41.9 1.3 collective-permute-start.15
  43.2 2.1 %collective-permute-start.10 = (bf16[512,1024]{1,0:T(8,128)(2,1)}, bf16[512,1024]{1,0:T(8,128)(2,1)}, u32[]{:S(2)}, u32[]{:S(2)}) collective-permute-start(bf16[512,1024]{1,0:T(8,128)(2,1)} %collective-permute-done.2.refs_4_), channel_id=1, source_target_pairs={{0,2},{1,7},{2,4},{3,1},{4,6},{5,3},{6,0},{7,5},{8,10},{9,15},{10,... | collective-permute-start | bytes 3145736 | tf_op jit(solution)/shard_map/ppermute | solution.py:196
  45.3 1.0 constant_dynamic-slice_fusion.3
  46.4 1.3 subtract_add_fusion
  47.8 2.7 %collective-permute-start.14 = (f32[512,128]{1,0:T(8,128)S(1)}, f32[512,128]{1,0:T(8,128)S(1)}, u32[]{:S(2)}, u32[]{:S(2)}) collective-permute-start(f32[512,128]{1,0:T(8,128)S(1)} %slice.9), channel_id=1, source_target_pairs={{0,64},{16,80},{32,96},{48,112},{64,0},{80,16},{96,32},{112,48},{1... | collective-permute-start | bytes 786440 | tf_op jit(solution)/shard_map/ppermute | solution.py:201
  50.5 6.7 %grad_columns.4.refs_6_ = f32[384,8192]{1,0:T(8,128)} custom-call(s32[34]{0:T(128)} %fusion.refs_0_.at_ref, bf16[384,1024]{1,0:T(8,128)(2,1)} %copy-done, bf16[512,1024]{1,0:T(8,128)(2,1)} %bitcast.9, bf16[512,1024]{1,0:T(8,128)(2,1)} %collective-permute-done.1.refs_3_, bf16[512,1024]{1,0:T(8,128)(2,1)} %collective-permute-done.2.refs_4_, ...), custom_call_target="tpu_custom_call" | custom-call | flops 1000 | bytes 1000 | tf_op jit(solution)/shard_map/grad_columns/pallas_call | solution.py:144
  57.2 10.0 %collective-permute-done.15.refs_4_ = s16[2,1056,256]{2,1,0:T(8,128)(2,1)} collective-permute-done((s16[2,1056,256]{2,1,0:T(8,128)(2,1)}, s16[2,1056,256]{2,1,0:T(8,128)(2,1)}, u32[]{:S(2)}, u32[]{:S(2)}) %collective-permute-start.15) | collective-permute-done | bytes 1081376 | tf_op jit(solution)/shard_map/ppermute | solution.py:196
  67.2 4.9 %partial_sums.5 = s16[2,1056,256]{2,1,0:T(8,128)(2,1)} custom-call(s32[34]{0:T(128)} %fusion.refs_0_.at_ref, bf16[1024,768]{1,0:T(8,128)(2,1)} %copy.18.refs_1_, bf16[384,8192]{1,0:T(8,128)(2,1)} %refs_2_.7, bf16[384,8192]{1,0:T(8,128)(2,1)} %collective-permute-done.3.refs_3_, s16[2,1056,256]{2,1,0:T(8,128)(2,1)} %collective-permute-done.15.refs_4_), custom_call_target="tpu_custom_call" | custom-call | flops 1000 | bytes 1000 | tf_op jit(solution)/shard_map/partial_sums/pallas_call | solution.py:87
  72.0 3.1 %collective-permute-done.14 = f32[512,128]{1,0:T(8,128)S(1)} collective-permute-done((f32[512,128]{1,0:T(8,128)S(1)}, f32[512,128]{1,0:T(8,128)S(1)}, u32[]{:S(2)}, u32[]{:S(2)}) %collective-permute-start.14) | collective-permute-done | bytes 262176 | tf_op jit(solution)/shard_map/ppermute | solution.py:201
  75.8 3.2 %collective-permute-done.9.refs_5_.refs_4_ = s16[4,1056,256]{2,1,0:T(8,128)(2,1)S(1)} collective-permute-done((s16[4,1056,256]{2,1,0:T(8,128)(2,1)}, s16[4,1056,256]{2,1,0:T(8,128)(2,1)S(1)}, u32[]{:S(2)}, u32[]{:S(2)}) %collective-permute-start.9) | collective-permute-done | bytes 2162720 | tf_op jit(solution)/shard_map/ppermute | solution.py:196
  79.1 1.6 collective-permute-start.18
  81.3 6.7 %grad_columns.5.refs_7_ = f32[384,8192]{1,0:T(8,128)} custom-call(s32[34]{0:T(128)} %fusion.refs_0_.at_ref, bf16[384,1024]{1,0:T(8,128)(2,1)} %copy-done, bf16[512,1024]{1,0:T(8,128)(2,1)} %collective-permute-done.11.refs_2_, bf16[512,1024]{1,0:T(8,128)(2,1)} %collective-permute-done.12.refs_3_, ...), custom_call_target="tpu_custom_call", output_to_operand_aliasing={{}: (6, {})} | custom-call | flops 1000 | bytes 1000 | tf_op jit(solution)/shard_map/grad_columns/pallas_call | solution.py:144
  88.0 5.6 %collective-permute-done.16.refs_4_ = s16[2,1056,256]{2,1,0:T(8,128)(2,1)S(1)} collective-permute-done((s16[2,1056,256]{2,1,0:T(8,128)(2,1)}, s16[2,1056,256]{2,1,0:T(8,128)(2,1)S(1)}, u32[]{:S(2)}, u32[]{:S(2)}) %collective-permute-start.16) | collective-permute-done | bytes 1081376 | tf_op jit(solution)/shard_map/ppermute | solution.py:196
  93.7 1.0 copy-done.7
  95.5 1.8 %slice_subtract_fusion = (f32[512,128]{1,0:T(8,128)S(1)}, f32[512,128]{1,0:T(8,128)}) fusion(f32[1024,128]{1,0:T(8,128)S(1)} %maximum_convert_fusion, f32[512,128]{1,0:T(8,128)} %copy-done.12, f32[1024,128]{1,0:T(8,128)S(1)} %subtract_add_fusion, f32[512,128]{1,0:T(8,128)} %param.13), kind=kLoop, calls=%fused_computation.3 | loop fusion | flops 524288 | bytes 1572864 | tf_op jit(solution)/shard_map/sub | solution.py:297
  97.3 2.9 %collective-permute-start.21 = (f32[512,128]{1,0:T(8,128)S(1)}, f32[512,128]{1,0:T(8,128)S(1)}, u32[]{:S(2)}, u32[]{:S(2)}) collective-permute-start(f32[512,128]{1,0:T(8,128)S(1)} %get-tuple-element.126), channel_id=1, source_target_pairs={{0,64},{16,80},{32,96},{48,112},{64,0},{80,16},{96,32},{112,48},{1... | collective-permute-start | bytes 786440 | tf_op jit(solution)/shard_map/ppermute | solution.py:201
  100.2 5.0 %collective-permute-done.17.refs_6_ = s16[2,1056,256]{2,1,0:T(8,128)(2,1)} collective-permute-done((s16[2,1056,256]{2,1,0:T(8,128)(2,1)}, s16[2,1056,256]{2,1,0:T(8,128)(2,1)}, u32[]{:S(2)}, u32[]{:S(2)}) %collective-permute-start.17) | collective-permute-done | bytes 1081376 | tf_op jit(solution)/shard_map/ppermute | solution.py:196
  105.3 7.7 %partial_sums.6 = (s16[2,1056,256]{2,1,0:T(8,128)(2,1)}, s16[2,1056,256]{2,1,0:T(8,128)(2,1)}) custom-call(s32[34]{0:T(128)} %fusion.refs_0_.at_ref, bf16[1024,768]{1,0:T(8,128)(2,1)} %copy.18.refs_1_, bf16[384,8192]{1,0:T(8,128)(2,1)} %refs_2_.7, bf16[384,8192]{1,0:T(8,128)(2,1)} %collective-permute-done.3.refs_3_, s16[2,1056,256]{2,1,0:T(8,128)(2,1)} %copy-done.7, ...), custom_call_target="tpu_custom_call" | custom-call | flops 1000 | bytes 1000 | tf_op jit(solution)/shard_map/partial_sums/pallas_call | solution.py:87
  113.0 3.5 %collective-permute-done.20.refs_5_ = bf16[512,1024]{1,0:T(8,128)(2,1)} collective-permute-done((bf16[512,1024]{1,0:T(8,128)(2,1)}, bf16[512,1024]{1,0:T(8,128)(2,1)}, u32[]{:S(2)}, u32[]{:S(2)}) %collective-permute-start.20) | collective-permute-done | bytes 1048608 | tf_op jit(solution)/shard_map/ppermute | solution.py:196
  116.5 2.4 %collective-permute-start.24 = (bf16[512,1024]{1,0:T(8,128)(2,1)}, bf16[512,1024]{1,0:T(8,128)(2,1)}, u32[]{:S(2)}, u32[]{:S(2)}) collective-permute-start(bf16[512,1024]{1,0:T(8,128)(2,1)} %collective-permute-done.20.refs_5_), channel_id=1, source_target_pairs={{0,1},{1,0},{2,3},{3,2},{4,5},{5,4},{6,7},{7,6},{8,9},{9,8},{10,11... | collective-permute-start | bytes 3145736 | tf_op jit(solution)/shard_map/ppermute | solution.py:196
  119.3 1.3 collective-permute-start.27
  120.7 1.9 %collective-permute-start.23 = (f32[1024,128]{1,0:T(8,128)S(1)}, f32[1024,128]{1,0:T(8,128)S(1)}, u32[]{:S(2)}, u32[]{:S(2)}) collective-permute-start(f32[1024,128]{1,0:T(8,128)S(1)} %constant_dynamic-update-slice_fusion.refs_0_.refs_1_), channel_id=1, source_target_pairs={{0,16},{16,32},{32,48},{48,0},{64,80},{80,96},{96,112},{112,64},{1... | collective-permute-start | bytes 1572872 | tf_op jit(solution)/shard_map/ppermute | solution.py:201
  123.4 7.9 %grad_columns.6.refs_5_ = f32[384,8192]{1,0:T(8,128)} custom-call(s32[34]{0:T(128)} %fusion.refs_0_.at_ref, bf16[384,1024]{1,0:T(8,128)(2,1)} %copy-done, bf16[512,1024]{1,0:T(8,128)(2,1)} %collective-permute-done.10.refs_2_, bf16[512,1024]{1,0:T(8,128)(2,1)} %collective-permute-done.19.refs_3_, ...), custom_call_target="tpu_custom_call", output_to_operand_aliasing={{}: (7, {})} | custom-call | flops 1000 | bytes 1000 | tf_op jit(solution)/shard_map/grad_columns/pallas_call | solution.py:144
  131.3 2.1 %collective-permute-done.26.refs_5_ = s16[2,1056,256]{2,1,0:T(8,128)(2,1)S(1)} collective-permute-done((s16[2,1056,256]{2,1,0:T(8,128)(2,1)}, s16[2,1056,256]{2,1,0:T(8,128)(2,1)S(1)}, u32[]{:S(2)}, u32[]{:S(2)}) %collective-permute-start.26) | collective-permute-done | bytes 1081376 | tf_op jit(solution)/shard_map/ppermute | solution.py:196
  133.4 12.1 %collective-permute-done.27.refs_6_ = s16[2,1056,256]{2,1,0:T(8,128)(2,1)S(1)} collective-permute-done((s16[2,1056,256]{2,1,0:T(8,128)(2,1)}, s16[2,1056,256]{2,1,0:T(8,128)(2,1)S(1)}, u32[]{:S(2)}, u32[]{:S(2)}) %collective-permute-start.27) | collective-permute-done | bytes 1081376 | tf_op jit(solution)/shard_map/ppermute | solution.py:196
  145.5 1.0 copy-done.9
  146.5 5.8 %partial_sums.7 = (s16[1,1056,256]{2,1,0:T(8,128)(2,1)}, f32[512,1024]{1,0:T(8,128)}) custom-call(s32[34]{0:T(128)} %fusion.refs_0_.at_ref, bf16[1024,768]{1,0:T(8,128)(2,1)} %copy.18.refs_1_, bf16[384,8192]{1,0:T(8,128)(2,1)} %refs_2_.7, bf16[384,8192]{1,0:T(8,128)(2,1)} %collective-permute-done.3.refs_3_, s16[4,1056,256]{2,1,0:T(8,128)(2,1)} %copy-done.1, ...), custom_call_target="tpu_custom_call" | custom-call | flops 1000 | bytes 1000 | tf_op jit(solution)/shard_map/partial_sums/pallas_call | solution.py:87
  153.6 3.4 %collective-permute-done.30.add_ref = s16[1,1056,256]{2,1,0:T(8,128)(2,1)} collective-permute-done((s16[1,1056,256]{2,1,0:T(8,128)(2,1)}, s16[1,1056,256]{2,1,0:T(8,128)(2,1)}, u32[]{:S(2)}, u32[]{:S(2)}) %collective-permute-start.30) | collective-permute-done | bytes 540704 | tf_op jit(solution)/shard_map/ppermute | solution.py:196
  157.0 3.0 %last_rows.1 = f32[512,1024]{1,0:T(8,128)} custom-call(s32[34]{0:T(128)} %fusion.refs_0_.at_ref, s16[1,1056,256]{2,1,0:T(8,128)(2,1)} %collective-permute-done.30.add_ref, f32[512,1024]{1,0:T(8,128)} %get-tuple-element.143._), custom_call_target="tpu_custom_call", output_to_operand_aliasing={{}: (2, {})} | custom-call | flops 1000 | bytes 1000 | tf_op jit(solution)/shard_map/last_rows/pallas_call | solution.py:104
  160.0 0.9 copy-done.10
  161.0 1.0 copy-done.11
  162.0 5.8 %grad_columns.7 = f32[384,8192]{1,0:T(8,128)} custom-call(s32[34]{0:T(128)} %fusion.refs_0_.at_ref, bf16[384,1024]{1,0:T(8,128)(2,1)} %copy-done, bf16[512,1024]{1,0:T(8,128)(2,1)} %copy-done.10, bf16[512,1024]{1,0:T(8,128)(2,1)} %collective-permute-done.22.refs_3_, bf16[512,1024]{1,0:T(8,128)(2,1)} %copy-done.11, ...), custom_call_target="tpu_custom_call", output_to_operand_aliasing={{}: (5, {})} | custom-call | flops 1000 | bytes 1000 | tf_op jit(solution)/shard_map/grad_columns/pallas_call | solution.py:144
  168.7 4.5 %assembled.1 = f32[512,1024]{1,0:T(8,128)} custom-call(s32[8]{0:T(128)} %fusion.1.at_ref, f32[1024,128]{1,0:T(8,128)} %copy-done.3, f32[1024,128]{1,0:T(8,128)} %copy-done.3, f32[1024,128]{1,0:T(8,128)} %copy-done.4, f32[1024,128]{1,0:T(8,128)} %copy-done.4, f32[1024,128]{1,0:T(8,128)} %copy-done.5, f32[1024,128]{1,0:T(8,128)} %copy-done.5, ...), custom_call_target="tpu_custom_call" | custom-call | flops 1000 | bytes 1000 | tf_op jit(solution)/shard_map/assembled/pallas_call | solution.py:171
  (69 shorter events, 8.2 us)
Async XLA Ops:
  0.6 4.1 %copy-start.2 = (bf16[1,512,1024]{2,1,0:T(8,128)(2,1)S(1)}, bf16[1,512,1024]{2,1,0:T(8,128)(2,1)}, u32[]{:S(2)}) copy-start(bf16[1,512,1024]{2,1,0:T(8,128)(2,1)} %param.11) | copy-start | bytes 3145732
  0.6 25.3 %collective-permute-start.3 = (bf16[384,8192]{1,0:T(8,128)(2,1)}, bf16[384,8192]{1,0:T(8,128)(2,1)}, u32[]{:S(2)}, u32[]{:S(2)}) collective-permute-start(bf16[384,8192]{1,0:T(8,128)(2,1)} %refs_2_.7), channel_id=1, source_target_pairs={{0,1},{1,0},{2,3},{3,2},{4,5},{5,4},{6,7},{7,6},{8,9},{9,8},{10,11... | collective-permute-start | bytes 18874376 | tf_op jit(solution)/shard_map/ppermute | solution.py:196
  2.1 13.4 %collective-permute-start.1 = (bf16[512,1024]{1,0:T(8,128)(2,1)}, bf16[512,1024]{1,0:T(8,128)(2,1)}, u32[]{:S(2)}, u32[]{:S(2)}) collective-permute-start(bf16[512,1024]{1,0:T(8,128)(2,1)} %bitcast.8), channel_id=1, source_target_pairs={{0,1},{1,0},{2,3},{3,2},{4,5},{5,4},{6,7},{7,6},{8,9},{9,8},{10,11... | collective-permute-start | bytes 3145736 | tf_op jit(solution)/shard_map/ppermute | solution.py:196
  4.2 11.4 %copy-start = (bf16[384,1024]{1,0:T(8,128)(2,1)}, bf16[384,1024]{1,0:T(8,128)(2,1)S(1)}, u32[]{:S(2)}) copy-start(bf16[384,1024]{1,0:T(8,128)(2,1)S(1)} %broadcast_multiply_fusion.refs_1_) | copy-start | bytes 2359300
  4.2 10.1 %collective-permute-start = (bf16[384,1024]{1,0:T(8,128)(2,1)S(1)}, bf16[384,1024]{1,0:T(8,128)(2,1)}, u32[]{:S(2)}, u32[]{:S(2)}) collective-permute-start(bf16[384,1024]{1,0:T(8,128)(2,1)S(1)} %broadcast_multiply_fusion.refs_1_), channel_id=1, source_target_pairs={{0,1},{1,0},{2,3},{3,2},{4,5},{5,4},{6,7},{7,6},{8,9},{9,8},{10,11... | collective-permute-start | bytes 2359304 | tf_op jit(solution)/shard_map/ppermute | solution.py:196
  4.7 14.3 %collective-permute-start.2 = (bf16[512,1024]{1,0:T(8,128)(2,1)S(1)}, bf16[512,1024]{1,0:T(8,128)(2,1)}, u32[]{:S(2)}, u32[]{:S(2)}) collective-permute-start(bf16[512,1024]{1,0:T(8,128)(2,1)S(1)} %bitcast.10), channel_id=1, source_target_pairs={{0,2},{1,7},{2,4},{3,1},{4,6},{5,3},{6,0},{7,5},{8,10},{9,15},{10,... | collective-permute-start | bytes 3145736 | tf_op jit(solution)/shard_map/ppermute | solution.py:196
  7.3 31.6 %collective-permute-start.5 = (bf16[512,1024]{1,0:T(8,128)(2,1)S(1)}, bf16[512,1024]{1,0:T(8,128)(2,1)}, u32[]{:S(2)}, u32[]{:S(2)}) collective-permute-start(bf16[512,1024]{1,0:T(8,128)(2,1)S(1)} %bitcast.11), channel_id=1, source_target_pairs={{0,8},{1,9},{2,10},{3,11},{4,12},{5,13},{6,14},{7,15},{8,0},{9,1},... | collective-permute-start | bytes 3145736 | tf_op jit(solution)/shard_map/ppermute | solution.py:196
  19.0 19.9 %collective-permute-start.4 = (bf16[512,1024]{1,0:T(8,128)(2,1)}, bf16[512,1024]{1,0:T(8,128)(2,1)}, u32[]{:S(2)}, u32[]{:S(2)}) collective-permute-start(bf16[512,1024]{1,0:T(8,128)(2,1)} %collective-permute-done.1.refs_3_), channel_id=1, source_target_pairs={{0,2},{1,7},{2,4},{3,1},{4,6},{5,3},{6,0},{7,5},{8,10},{9,15},{10,... | collective-permute-start | bytes 3145736 | tf_op jit(solution)/shard_map/ppermute | solution.py:196
  22.2 16.6 %collective-permute-start.7 = (bf16[1024,128]{1,0:T(8,128)(2,1)S(1)}, bf16[1024,128]{1,0:T(8,128)(2,1)}, u32[]{:S(2)}, u32[]{:S(2)}) collective-permute-start(bf16[1024,128]{1,0:T(8,128)(2,1)S(1)} %pad_maximum_fusion.2), channel_id=1, source_target_pairs={{0,48},{16,0},{32,16},{48,32},{64,112},{80,64},{96,80},{112,96},{1... | collective-permute-start | bytes 786440 | tf_op jit(solution)/shard_map/ppermute | solution.py:201
  26.0 12.9 %collective-permute-start.8 = (bf16[1024,128]{1,0:T(8,128)(2,1)S(1)}, bf16[1024,128]{1,0:T(8,128)(2,1)}, u32[]{:S(2)}, u32[]{:S(2)}) collective-permute-start(bf16[1024,128]{1,0:T(8,128)(2,1)S(1)} %get-tuple-element.90), channel_id=1, source_target_pairs={{0,32},{16,48},{32,0},{48,16},{64,96},{80,112},{96,64},{112,80},{1... | collective-permute-start | bytes 786440 | tf_op jit(solution)/shard_map/ppermute | solution.py:201
  26.0 14.8 %collective-permute-start.6 = (bf16[1024,128]{1,0:T(8,128)(2,1)S(1)}, bf16[1024,128]{1,0:T(8,128)(2,1)}, u32[]{:S(2)}, u32[]{:S(2)}) collective-permute-start(bf16[1024,128]{1,0:T(8,128)(2,1)S(1)} %get-tuple-element.88), channel_id=1, source_target_pairs={{0,16},{16,32},{32,48},{48,0},{64,80},{80,96},{96,112},{112,64},{1... | collective-permute-start | bytes 786440 | tf_op jit(solution)/shard_map/ppermute | solution.py:201
  40.8 38.2 %collective-permute-start.9 = (s16[4,1056,256]{2,1,0:T(8,128)(2,1)}, s16[4,1056,256]{2,1,0:T(8,128)(2,1)S(1)}, u32[]{:S(2)}, u32[]{:S(2)}) collective-permute-start(s16[4,1056,256]{2,1,0:T(8,128)(2,1)} %get-tuple-element.91), channel_id=1, source_target_pairs={{0,6},{1,3},{2,0},{3,5},{4,2},{5,7},{6,4},{7,1},{8,14},{9,11},{10,... | collective-permute-start | bytes 6488072 | tf_op jit(solution)/shard_map/ppermute | solution.py:196
  40.8 4.5 %collective-permute-start.11 = (bf16[512,1024]{1,0:T(8,128)(2,1)}, bf16[512,1024]{1,0:T(8,128)(2,1)}, u32[]{:S(2)}, u32[]{:S(2)}) collective-permute-start(bf16[512,1024]{1,0:T(8,128)(2,1)} %collective-permute-done.2.refs_4_), channel_id=1, source_target_pairs={{0,1},{1,0},{2,3},{3,2},{4,5},{5,4},{6,7},{7,6},{8,9},{9,8},{10,11... | collective-permute-start | bytes 3145736 | tf_op jit(solution)/shard_map/ppermute | solution.py:196
  41.9 5.8 %collective-permute-start.12 = (bf16[512,1024]{1,0:T(8,128)(2,1)}, bf16[512,1024]{1,0:T(8,128)(2,1)}, u32[]{:S(2)}, u32[]{:S(2)}) collective-permute-start(bf16[512,1024]{1,0:T(8,128)(2,1)} %collective-permute-done.4.refs_5_), channel_id=1, source_target_pairs={{0,1},{1,0},{2,3},{3,2},{4,5},{5,4},{6,7},{7,6},{8,9},{9,8},{10,11... | collective-permute-start | bytes 3145736 | tf_op jit(solution)/shard_map/ppermute | solution.py:196
  41.9 25.2 %collective-permute-start.15 = (s16[2,1056,256]{2,1,0:T(8,128)(2,1)}, s16[2,1056,256]{2,1,0:T(8,128)(2,1)}, u32[]{:S(2)}, u32[]{:S(2)}) collective-permute-start(s16[2,1056,256]{2,1,0:T(8,128)(2,1)} %get-tuple-element.106), channel_id=1, source_target_pairs={{0,8},{1,9},{2,10},{3,11},{4,12},{5,13},{6,14},{7,15},{8,0},{9,1},... | collective-permute-start | bytes 3244040 | tf_op jit(solution)/shard_map/ppermute | solution.py:196
  43.2 28.8 %collective-permute-start.10 = (bf16[512,1024]{1,0:T(8,128)(2,1)}, bf16[512,1024]{1,0:T(8,128)(2,1)}, u32[]{:S(2)}, u32[]{:S(2)}) collective-permute-start(bf16[512,1024]{1,0:T(8,128)(2,1)} %collective-permute-done.2.refs_4_), channel_id=1, source_target_pairs={{0,2},{1,7},{2,4},{3,1},{4,6},{5,3},{6,0},{7,5},{8,10},{9,15},{10,... | collective-permute-start | bytes 3145736 | tf_op jit(solution)/shard_map/ppermute | solution.py:196
  45.3 29.8 %collective-permute-start.13 = (bf16[512,1024]{1,0:T(8,128)(2,1)}, bf16[512,1024]{1,0:T(8,128)(2,1)}, u32[]{:S(2)}, u32[]{:S(2)}) collective-permute-start(bf16[512,1024]{1,0:T(8,128)(2,1)} %collective-permute-done.5.refs_4_), channel_id=1, source_target_pairs={{0,1},{1,0},{2,3},{3,2},{4,5},{5,4},{6,7},{7,6},{8,9},{9,8},{10,11... | collective-permute-start | bytes 3145736 | tf_op jit(solution)/shard_map/ppermute | solution.py:196
  47.8 27.4 %collective-permute-start.14 = (f32[512,128]{1,0:T(8,128)S(1)}, f32[512,128]{1,0:T(8,128)S(1)}, u32[]{:S(2)}, u32[]{:S(2)}) collective-permute-start(f32[512,128]{1,0:T(8,128)S(1)} %slice.9), channel_id=1, source_target_pairs={{0,64},{16,80},{32,96},{48,112},{64,0},{80,16},{96,32},{112,48},{1... | collective-permute-start | bytes 786440 | tf_op jit(solution)/shard_map/ppermute | solution.py:201
  75.1 0.7 copy-start.12
  79.1 9.0 %copy-start.1 = (s16[4,1056,256]{2,1,0:T(8,128)(2,1)}, s16[4,1056,256]{2,1,0:T(8,128)(2,1)S(1)}, u32[]{:S(2)}) copy-start(s16[4,1056,256]{2,1,0:T(8,128)(2,1)S(1)} %collective-permute-done.9.refs_5_.refs_4_) | copy-start | bytes 6488068
  79.1 14.6 %collective-permute-start.16 = (s16[2,1056,256]{2,1,0:T(8,128)(2,1)}, s16[2,1056,256]{2,1,0:T(8,128)(2,1)S(1)}, u32[]{:S(2)}, u32[]{:S(2)}) collective-permute-start(s16[2,1056,256]{2,1,0:T(8,128)(2,1)} %partial_sums.5), channel_id=1, source_target_pairs={{0,2},{1,7},{2,4},{3,1},{4,6},{5,3},{6,0},{7,5},{8,10},{9,15},{10,... | collective-permute-start | bytes 3244040 | tf_op jit(solution)/shard_map/ppermute | solution.py:196
  79.1 26.2 %collective-permute-start.17 = (s16[2,1056,256]{2,1,0:T(8,128)(2,1)}, s16[2,1056,256]{2,1,0:T(8,128)(2,1)}, u32[]{:S(2)}, u32[]{:S(2)}) collective-permute-start(s16[2,1056,256]{2,1,0:T(8,128)(2,1)} %get-tuple-element.116), channel_id=1, source_target_pairs={{0,2},{1,7},{2,4},{3,1},{4,6},{5,3},{6,0},{7,5},{8,10},{9,15},{10,... | collective-permute-start | bytes 3244040 | tf_op jit(solution)/shard_map/ppermute | solution.py:196
  79.1 33.9 %collective-permute-start.18 = (bf16[512,1024]{1,0:T(8,128)(2,1)}, bf16[512,1024]{1,0:T(8,128)(2,1)}, u32[]{:S(2)}, u32[]{:S(2)}) collective-permute-start(bf16[512,1024]{1,0:T(8,128)(2,1)} %collective-permute-done.10.refs_2_), channel_id=1, source_target_pairs={{0,8},{1,9},{2,10},{3,11},{4,12},{5,13},{6,14},{7,15},{8,0},{9,1},... | collective-permute-start | bytes 3145736 | tf_op jit(solution)/shard_map/ppermute | solution.py:196
  80.6 32.4 %collective-permute-start.19 = (bf16[512,1024]{1,0:T(8,128)(2,1)}, bf16[512,1024]{1,0:T(8,128)(2,1)}, u32[]{:S(2)}, u32[]{:S(2)}) collective-permute-start(bf16[512,1024]{1,0:T(8,128)(2,1)} %collective-permute-done.10.refs_2_), channel_id=1, source_target_pairs={{0,1},{1,0},{2,3},{3,2},{4,5},{5,4},{6,7},{7,6},{8,9},{9,8},{10,11... | collective-permute-start | bytes 3145736 | tf_op jit(solution)/shard_map/ppermute | solution.py:196
  93.7 1.0 copy-start.7
  94.7 21.8 %collective-permute-start.20 = (bf16[512,1024]{1,0:T(8,128)(2,1)}, bf16[512,1024]{1,0:T(8,128)(2,1)}, u32[]{:S(2)}, u32[]{:S(2)}) collective-permute-start(bf16[512,1024]{1,0:T(8,128)(2,1)} %collective-permute-done.5.refs_4_), channel_id=1, source_target_pairs={{0,2},{1,7},{2,4},{3,1},{4,6},{5,3},{6,0},{7,5},{8,10},{9,15},{10,... | collective-permute-start | bytes 3145736 | tf_op jit(solution)/shard_map/ppermute | solution.py:196
  97.3 15.7 %collective-permute-start.21 = (f32[512,128]{1,0:T(8,128)S(1)}, f32[512,128]{1,0:T(8,128)S(1)}, u32[]{:S(2)}, u32[]{:S(2)}) collective-permute-start(f32[512,128]{1,0:T(8,128)S(1)} %get-tuple-element.126), channel_id=1, source_target_pairs={{0,64},{16,80},{32,96},{48,112},{64,0},{80,16},{96,32},{112,48},{1... | collective-permute-start | bytes 786440 | tf_op jit(solution)/shard_map/ppermute | solution.py:201
  116.5 6.1 %collective-permute-start.24 = (bf16[512,1024]{1,0:T(8,128)(2,1)}, bf16[512,1024]{1,0:T(8,128)(2,1)}, u32[]{:S(2)}, u32[]{:S(2)}) collective-permute-start(bf16[512,1024]{1,0:T(8,128)(2,1)} %collective-permute-done.20.refs_5_), channel_id=1, source_target_pairs={{0,1},{1,0},{2,3},{3,2},{4,5},{5,4},{6,7},{7,6},{8,9},{9,8},{10,11... | collective-permute-start | bytes 3145736 | tf_op jit(solution)/shard_map/ppermute | solution.py:196
  118.9 14.5 %collective-permute-start.26 = (s16[2,1056,256]{2,1,0:T(8,128)(2,1)}, s16[2,1056,256]{2,1,0:T(8,128)(2,1)S(1)}, u32[]{:S(2)}, u32[]{:S(2)}) collective-permute-start(s16[2,1056,256]{2,1,0:T(8,128)(2,1)} %get-tuple-element.135), channel_id=1, source_target_pairs={{0,2},{1,7},{2,4},{3,1},{4,6},{5,3},{6,0},{7,5},{8,10},{9,15},{10,... | collective-permute-start | bytes 3244040 | tf_op jit(solution)/shard_map/ppermute | solution.py:196
  119.3 26.2 %collective-permute-start.27 = (s16[2,1056,256]{2,1,0:T(8,128)(2,1)}, s16[2,1056,256]{2,1,0:T(8,128)(2,1)S(1)}, u32[]{:S(2)}, u32[]{:S(2)}) collective-permute-start(s16[2,1056,256]{2,1,0:T(8,128)(2,1)} %get-tuple-element.136), channel_id=1, source_target_pairs={{0,8},{1,9},{2,10},{3,11},{4,12},{5,13},{6,14},{7,15},{8,0},{9,1},... | collective-permute-start | bytes 3244040 | tf_op jit(solution)/shard_map/ppermute | solution.py:196
  120.6 31.7 %collective-permute-start.22 = (bf16[512,1024]{1,0:T(8,128)(2,1)}, bf16[512,1024]{1,0:T(8,128)(2,1)}, u32[]{:S(2)}, u32[]{:S(2)}) collective-permute-start(bf16[512,1024]{1,0:T(8,128)(2,1)} %collective-permute-done.13.refs_5_), channel_id=1, source_target_pairs={{0,2},{1,7},{2,4},{3,1},{4,6},{5,3},{6,0},{7,5},{8,10},{9,15},{10,... | collective-permute-start | bytes 3145736 | tf_op jit(solution)/shard_map/ppermute | solution.py:196
  120.7 10.7 %copy-start.3 = (f32[1024,128]{1,0:T(8,128)}, f32[1024,128]{1,0:T(8,128)S(1)}, u32[]{:S(2)}) copy-start(f32[1024,128]{1,0:T(8,128)S(1)} %constant_dynamic-update-slice_fusion.refs_0_.refs_1_) | copy-start | bytes 1572868
  120.7 31.6 %collective-permute-start.23 = (f32[1024,128]{1,0:T(8,128)S(1)}, f32[1024,128]{1,0:T(8,128)S(1)}, u32[]{:S(2)}, u32[]{:S(2)}) collective-permute-start(f32[1024,128]{1,0:T(8,128)S(1)} %constant_dynamic-update-slice_fusion.refs_0_.refs_1_), channel_id=1, source_target_pairs={{0,16},{16,32},{32,48},{48,0},{64,80},{80,96},{96,112},{112,64},{1... | collective-permute-start | bytes 1572872 | tf_op jit(solution)/shard_map/ppermute | solution.py:201
  122.6 29.8 %collective-permute-start.25 = (f32[1024,128]{1,0:T(8,128)S(1)}, f32[1024,128]{1,0:T(8,128)S(1)}, u32[]{:S(2)}, u32[]{:S(2)}) collective-permute-start(f32[1024,128]{1,0:T(8,128)S(1)} %constant_dynamic-update-slice_fusion.refs_0_.refs_1_), channel_id=1, source_target_pairs={{0,48},{16,0},{32,16},{48,32},{64,112},{80,64},{96,80},{112,96},{1... | collective-permute-start | bytes 1572872 | tf_op jit(solution)/shard_map/ppermute | solution.py:201
  133.4 12.1 %copy-start.8 = (s16[2,1056,256]{2,1,0:T(8,128)(2,1)}, s16[2,1056,256]{2,1,0:T(8,128)(2,1)S(1)}, u32[]{:S(2)}) copy-start(s16[2,1056,256]{2,1,0:T(8,128)(2,1)S(1)} %collective-permute-done.26.refs_5_) | copy-start | bytes 3244036
  145.5 1.0 copy-start.9
  152.3 7.7 %copy-start.4 = (f32[1024,128]{1,0:T(8,128)}, f32[1024,128]{1,0:T(8,128)S(1)}, u32[]{:S(2)}) copy-start(f32[1024,128]{1,0:T(8,128)S(1)} %collective-permute-done.23.refs_2_.refs_3_) | copy-start | bytes 1572868
  152.3 7.7 %copy-start.5 = (f32[1024,128]{1,0:T(8,128)}, f32[1024,128]{1,0:T(8,128)S(1)}, u32[]{:S(2)}) copy-start(f32[1024,128]{1,0:T(8,128)S(1)} %collective-permute-done.25.refs_4_.refs_5_) | copy-start | bytes 1572868
  152.3 7.7 %collective-permute-start.28 = (bf16[512,1024]{1,0:T(8,128)(2,1)}, bf16[512,1024]{1,0:T(8,128)(2,1)S(1)}, u32[]{:S(2)}, u32[]{:S(2)}) collective-permute-start(bf16[512,1024]{1,0:T(8,128)(2,1)} %collective-permute-done.18.refs_4_), channel_id=1, source_target_pairs={{0,1},{1,0},{2,3},{3,2},{4,5},{5,4},{6,7},{7,6},{8,9},{9,8},{10,11... | collective-permute-start | bytes 3145736 | tf_op jit(solution)/shard_map/ppermute | solution.py:196
  152.8 7.3 %collective-permute-start.29 = (bf16[512,1024]{1,0:T(8,128)(2,1)}, bf16[512,1024]{1,0:T(8,128)(2,1)S(1)}, u32[]{:S(2)}, u32[]{:S(2)}) collective-permute-start(bf16[512,1024]{1,0:T(8,128)(2,1)} %collective-permute-done.22.refs_3_), channel_id=1, source_target_pairs={{0,1},{1,0},{2,3},{3,2},{4,5},{5,4},{6,7},{7,6},{8,9},{9,8},{10,11... | collective-permute-start | bytes 3145736 | tf_op jit(solution)/shard_map/ppermute | solution.py:196
  152.9 4.0 %collective-permute-start.30 = (s16[1,1056,256]{2,1,0:T(8,128)(2,1)}, s16[1,1056,256]{2,1,0:T(8,128)(2,1)}, u32[]{:S(2)}, u32[]{:S(2)}) collective-permute-start(s16[1,1056,256]{2,1,0:T(8,128)(2,1)} %get-tuple-element.142), channel_id=1, source_target_pairs={{0,1},{1,0},{2,3},{3,2},{4,5},{5,4},{6,7},{7,6},{8,9},{9,8},{10,11... | collective-permute-start | bytes 1622024 | tf_op jit(solution)/shard_map/ppermute | solution.py:196
  153.3 14.6 %collective-permute-start.31 = (f32[1024,128]{1,0:T(8,128)S(1)}, f32[1024,128]{1,0:T(8,128)S(1)}, u32[]{:S(2)}, u32[]{:S(2)}) collective-permute-start(f32[1024,128]{1,0:T(8,128)S(1)} %collective-permute-done.23.refs_2_.refs_3_), channel_id=1, source_target_pairs={{0,16},{16,32},{32,48},{48,0},{64,80},{80,96},{96,112},{112,64},{1... | collective-permute-start | bytes 1572872 | tf_op jit(solution)/shard_map/ppermute | solution.py:201
  160.0 1.0 copy-start.10
  161.0 1.0 copy-start.11
  167.8 0.9 copy-start.6

commit v3 on v2

--- a/solution.py
+++ b/solution.py
@@ -9,7 +9,7 @@
 outer_rate = 0.7
 outer_beta = 0.9
 top_code = 32767.0
-group_rows = 32
+group_rows = 64
 half = 256
 MB = 1 << 20
 vmem = 60 * MB
@@ -157,6 +157,26 @@
     )(*operands)
 
 
+def transpose_kernel(own_ref, sib_ref, out_ref):
+    tokens = own_ref.shape[0]
+    out_ref[:, :tokens] = own_ref[...].T
+    out_ref[:, tokens:] = sib_ref[...].T
+
+
+def transposed(own, sib):
+    tokens, features = own.shape
+    return pl.pallas_call(
+        transpose_kernel,
+        grid=(1,),
+        in_specs=[pl.BlockSpec(own.shape, lambda i: (0, 0))] * 2,
+        out_specs=pl.BlockSpec((features, 2 * tokens), lambda i: (0, 0)),
+        out_shape=jax.ShapeDtypeStruct((features, 2 * tokens), own.dtype),
+        compiler_params=pltpu.CompilerParams(vmem_limit_bytes=vmem),
+        cost_estimate=tiny,
+        name="transposed",
+    )(own, sib)
+
+
 def assemble_kernel(at_ref, *refs):
     out_ref = refs[-1]
     for k, piece in enumerate(refs[:-1]):
@@ -264,13 +284,12 @@
     live_rows = (token_ids != 0).astype(jnp.bfloat16)[:, None]
     masked = kv_cotangent * live_rows
     masked_sib = sent(masked, to_core)
-    mt = jnp.concatenate([masked, masked_sib], axis=0).T
+    mt = transposed(masked, masked_sib)
     w_z, masked_sib, w_s = together(w, masked_sib, w_s)
     c1, c2, c3 = (group_columns(w_z, (gz + dz) % 4, gh, width) for dz in (1, 2, 3))
-    w_later, f1, mt, at, rep_at, c1, c2, c3 = together(w_s, f1, mt, at, rep_at, c1, c2, c3)
-    f2 = sent(w_later, ahead)
-    z2, z3 = sent_rep(c2, dz=2), sent_rep(c3, dz=3)
-    c1, x_sib = together(c1, x_sib)
+    w_later, x_sib, mt, at, rep_at, c1, c2, c3 = together(w_s, x_sib, mt, at, rep_at, c1, c2, c3)
+    f2, z2, z3 = sent(w_later, ahead), sent_rep(c2, dz=2), sent_rep(c3, dz=3)
+    c1, f1 = together(c1, f1)
     z1 = sent_rep(c1, dz=1)
     far_y, b, near_o = part_sums("first", [(2, [], False), (4, [], False), (2, [], False)])
     w, w_s, f1, f2, v, far_y, b, near_o, z1, z3, z2 = together(w, w_s, f1, f2, v, far_y, b, near_o, z1, z3, z2)

time: 174 us -> 171 us (0.983)
  waiting for transfers between devices: 56.4 us -> 45.5 us
  starting transfers between devices: 34.9 us -> 44.2 us
  local copies, waits for them, and re-layouts: 10.9 us -> 8.24 us
  Pallas kernels: 63.7 us -> 66 us
    ppermute x24, waiting for transfers between devices: 51.3 us -> 41.9 us  [sent(): return lax.ppermute(array, 'fsdp', pairs)]
    ppermute x24, starting transfers between devices: 21.8 us -> 29.6 us  [sent(): return lax.ppermute(array, 'fsdp', pairs)]
    pallas_call x0 -> x1, Pallas kernels: none -> 2.97 us  [transposed(): pl.pallas_call(transpose_kernel, grid=(1,), in_specs=[pl.BlockSpec(own.sh...]
    unnamed x27 -> x29, local copies, waits for them, and re-layouts: 5.53 us -> 4.5 us
  transfers between devices with their start and end apart: 32 -> 32, of which waited for: 13 -> 13; matrix products, arithmetic and copies ran while one was open for 7% -> 5% of each run, Pallas kernels for 34% -> 36%
where the time goes in v3:
time: 171 us; the launch traced here: 170 us
  Pallas kernels  66 us (39%)
  waiting for transfers between devices  45.5 us (27%)
  starting transfers between devices  44.2 us (26%)
  local copies, waits for them, and re-layouts  8.24 us (5%)
  other arithmetic  5.16 us (3%)
    ppermute x24, waiting for transfers between devices, sent(): return lax.ppermute(array, 'fsdp', pairs)  41.9 us
    ppermute x24, starting transfers between devices, sent(): return lax.ppermute(array, 'fsdp', pairs)  29.6 us
    pallas_call x4, Pallas kernels, sums(): pl.pallas_call(lambda *refs: sums_kernel(groups, len(adds), *refs), grid_...  28.4 us
    pallas_call x4, Pallas kernels, grad_columns(): pl.pallas_call(lambda *refs: columns_kernel(n, *refs), grid_spec=pltpu.Pr...  27.1 us
    ppermute x8, starting transfers between devices, sent_rep(): return lax.ppermute(array, 'rep', pairs)  14.6 us
    unnamed x29, local copies, waits for them, and re-layouts  4.5 us
    pallas_call x1, Pallas kernels, assembled(): pl.pallas_call(assemble_kernel, grid_spec=pltpu.PrefetchScalarGridSpec(nu...  4.49 us
    ppermute x8, waiting for transfers between devices, sent_rep(): return lax.ppermute(array, 'rep', pairs)  3.56 us
  transfers between devices with their start and end apart: 32, of which 13 were waited for; matrix products, arithmetic and copies ran while one was open for 5% of the time, Pallas kernels for 36%

profile of v3, /device:TPU:1, one launch (start us, length us, event | category | flops | bytes accessed | tf_op | source)
XLA Modules:
  0.0 169.9 jit_solution(10994467544950416607)
XLA Ops:
  0.6 1.5 collective-permute-start.2
  2.9 1.3 broadcast_multiply_fusion.own_ref.refs_1_
  4.8 2.6 %collective-permute-start.3 = (bf16[512,1024]{1,0:T(8,128)(2,1)}, bf16[512,1024]{1,0:T(8,128)(2,1)}, u32[]{:S(2)}, u32[]{:S(2)}) collective-permute-start(bf16[512,1024]{1,0:T(8,128)(2,1)} %bitcast.7), channel_id=1, source_target_pairs={{0,2},{1,7},{2,4},{3,1},{4,6},{5,3},{6,0},{7,5},{8,10},{9,15},{10,... | collective-permute-start | bytes 3145736 | tf_op jit(solution)/shard_map/ppermute | solution.py:216
  7.3 1.3 collective-permute-start.5
  8.6 1.2 fusion.1.at_ref
  9.8 1.3 fusion.refs_0_.at_ref
  11.1 3.2 %collective-permute-done.sib_ref = bf16[384,1024]{1,0:T(8,128)(2,1)} collective-permute-done((bf16[384,1024]{1,0:T(8,128)(2,1)S(1)}, bf16[384,1024]{1,0:T(8,128)(2,1)}, u32[]{:S(2)}, u32[]{:S(2)}) %collective-permute-start) | collective-permute-done | bytes 786464 | tf_op jit(solution)/shard_map/ppermute | solution.py:216
  14.3 3.0 %transposed.1.refs_1_ = bf16[1024,768]{1,0:T(8,128)(2,1)} custom-call(bf16[384,1024]{1,0:T(8,128)(2,1)} %copy-done, bf16[384,1024]{1,0:T(8,128)(2,1)} %collective-permute-done.sib_ref), custom_call_target="tpu_custom_call" | custom-call | flops 1000 | bytes 1000 | tf_op jit(solution)/shard_map/transposed/pallas_call | solution.py:168
  17.6 2.6 %collective-permute-start.4 = (bf16[512,1024]{1,0:T(8,128)(2,1)}, bf16[512,1024]{1,0:T(8,128)(2,1)}, u32[]{:S(2)}, u32[]{:S(2)}) collective-permute-start(bf16[512,1024]{1,0:T(8,128)(2,1)} %collective-permute-done.1.refs_3_), channel_id=1, source_target_pairs={{0,2},{1,7},{2,4},{3,1},{4,6},{5,3},{6,0},{7,5},{8,10},{9,15},{10,... | collective-permute-start | bytes 3145736 | tf_op jit(solution)/shard_map/ppermute | solution.py:216
  20.2 1.6 collective-permute-start.6
  21.8 2.1 %collective-permute-start.7 = (bf16[1024,128]{1,0:T(8,128)(2,1)S(1)}, bf16[1024,128]{1,0:T(8,128)(2,1)}, u32[]{:S(2)}, u32[]{:S(2)}) collective-permute-start(bf16[1024,128]{1,0:T(8,128)(2,1)S(1)} %pad_maximum_fusion.2), channel_id=1, source_target_pairs={{0,48},{16,0},{32,16},{48,32},{64,112},{80,64},{96,80},{112,96},{1... | collective-permute-start | bytes 786440 | tf_op jit(solution)/shard_map/ppermute | solution.py:221
  24.0 1.3 collective-permute-start.8
  25.3 10.5 %partial_sums.4 = (s16[2,1040,256]{2,1,0:T(8,128)(2,1)}, s16[4,1040,256]{2,1,0:T(8,128)(2,1)}, s16[2,1040,256]{2,1,0:T(8,128)(2,1)}) custom-call(s32[34]{0:T(128)} %fusion.refs_0_.at_ref, bf16[1024,768]{1,0:T(8,128)(2,1)} %transposed.1.refs_1_, bf16[384,8192]{1,0:T(8,128)(2,1)} %refs_2_.7, bf16[384,8192]{1,0:T(8,128)(2,1)} %collective-permute-done.2.refs_3_), custom_call_target="tpu_custom_call" | custom-call | flops 1000 | bytes 1000 | tf_op jit(solution)/shard_map/partial_sums/pallas_call | solution.py:87
  37.0 4.3 %collective-permute-start.11 = (bf16[512,1024]{1,0:T(8,128)(2,1)}, bf16[512,1024]{1,0:T(8,128)(2,1)}, u32[]{:S(2)}, u32[]{:S(2)}) collective-permute-start(bf16[512,1024]{1,0:T(8,128)(2,1)} %collective-permute-done.3.refs_4_), channel_id=1, source_target_pairs={{0,1},{1,0},{2,3},{3,2},{4,5},{5,4},{6,7},{7,6},{8,9},{9,8},{10,11... | collective-permute-start | bytes 3145736 | tf_op jit(solution)/shard_map/ppermute | solution.py:216
  41.3 1.3 collective-permute-start.15
  42.6 1.3 collective-permute-done.11.refs_2_
  44.3 1.0 constant_dynamic-slice_fusion.3
  45.4 1.2 subtract_add_fusion
  46.7 3.0 %collective-permute-start.14 = (f32[512,128]{1,0:T(8,128)S(1)}, f32[512,128]{1,0:T(8,128)S(1)}, u32[]{:S(2)}, u32[]{:S(2)}) collective-permute-start(f32[512,128]{1,0:T(8,128)S(1)} %slice.9), channel_id=1, source_target_pairs={{0,64},{16,80},{32,96},{48,112},{64,0},{80,16},{96,32},{112,48},{1... | collective-permute-start | bytes 786440 | tf_op jit(solution)/shard_map/ppermute | solution.py:221
  49.7 6.7 %grad_columns.4.refs_6_ = f32[384,8192]{1,0:T(8,128)} custom-call(s32[34]{0:T(128)} %fusion.refs_0_.at_ref, bf16[384,1024]{1,0:T(8,128)(2,1)} %copy-done, bf16[512,1024]{1,0:T(8,128)(2,1)} %bitcast.9, bf16[512,1024]{1,0:T(8,128)(2,1)} %collective-permute-done.1.refs_3_, bf16[512,1024]{1,0:T(8,128)(2,1)} %collective-permute-done.3.refs_4_, ...), custom_call_target="tpu_custom_call" | custom-call | flops 1000 | bytes 1000 | tf_op jit(solution)/shard_map/grad_columns/pallas_call | solution.py:144
  56.4 9.8 %collective-permute-done.15.refs_4_ = s16[2,1040,256]{2,1,0:T(8,128)(2,1)} collective-permute-done((s16[2,1040,256]{2,1,0:T(8,128)(2,1)}, s16[2,1040,256]{2,1,0:T(8,128)(2,1)}, u32[]{:S(2)}, u32[]{:S(2)}) %collective-permute-start.15) | collective-permute-done | bytes 1064992 | tf_op jit(solution)/shard_map/ppermute | solution.py:216
  66.2 4.8 %partial_sums.5 = s16[2,1040,256]{2,1,0:T(8,128)(2,1)} custom-call(s32[34]{0:T(128)} %fusion.refs_0_.at_ref, bf16[1024,768]{1,0:T(8,128)(2,1)} %transposed.1.refs_1_, bf16[384,8192]{1,0:T(8,128)(2,1)} %refs_2_.7, bf16[384,8192]{1,0:T(8,128)(2,1)} %collective-permute-done.2.refs_3_, s16[2,1040,256]{2,1,0:T(8,128)(2,1)} %collective-permute-done.15.refs_4_), custom_call_target="tpu_custom_call" | custom-call | flops 1000 | bytes 1000 | tf_op jit(solution)/shard_map/partial_sums/pallas_call | solution.py:87
  70.9 3.2 %collective-permute-done.14 = f32[512,128]{1,0:T(8,128)S(1)} collective-permute-done((f32[512,128]{1,0:T(8,128)S(1)}, f32[512,128]{1,0:T(8,128)S(1)}, u32[]{:S(2)}, u32[]{:S(2)}) %collective-permute-start.14) | collective-permute-done | bytes 262176 | tf_op jit(solution)/shard_map/ppermute | solution.py:221
  74.2 1.3 collective-permute-done.9.refs_5_.refs_4_
  75.4 1.8 %collective-permute-start.16 = (s16[2,1040,256]{2,1,0:T(8,128)(2,1)}, s16[2,1040,256]{2,1,0:T(8,128)(2,1)}, u32[]{:S(2)}, u32[]{:S(2)}) collective-permute-start(s16[2,1040,256]{2,1,0:T(8,128)(2,1)} %partial_sums.5), channel_id=1, source_target_pairs={{0,2},{1,7},{2,4},{3,1},{4,6},{5,3},{6,0},{7,5},{8,10},{9,15},{10,... | collective-permute-start | bytes 3194888 | tf_op jit(solution)/shard_map/ppermute | solution.py:216
  77.2 1.3 collective-permute-start.18
  78.5 1.6 collective-permute-start.19
  80.1 6.7 %grad_columns.5.refs_7_ = f32[384,8192]{1,0:T(8,128)} custom-call(s32[34]{0:T(128)} %fusion.refs_0_.at_ref, bf16[384,1024]{1,0:T(8,128)(2,1)} %copy-done, bf16[512,1024]{1,0:T(8,128)(2,1)} %collective-permute-done.11.refs_2_, bf16[512,1024]{1,0:T(8,128)(2,1)} %collective-permute-done.12.refs_3_, ...), custom_call_target="tpu_custom_call", output_to_operand_aliasing={{}: (6, {})} | custom-call | flops 1000 | bytes 1000 | tf_op jit(solution)/shard_map/grad_columns/pallas_call | solution.py:144
  86.9 3.0 %collective-permute-done.16.refs_4_ = s16[2,1040,256]{2,1,0:T(8,128)(2,1)} collective-permute-done((s16[2,1040,256]{2,1,0:T(8,128)(2,1)}, s16[2,1040,256]{2,1,0:T(8,128)(2,1)}, u32[]{:S(2)}, u32[]{:S(2)}) %collective-permute-start.16) | collective-permute-done | bytes 1064992 | tf_op jit(solution)/shard_map/ppermute | solution.py:216
  89.9 2.7 %collective-permute-start.20 = (bf16[512,1024]{1,0:T(8,128)(2,1)}, bf16[512,1024]{1,0:T(8,128)(2,1)}, u32[]{:S(2)}, u32[]{:S(2)}) collective-permute-start(bf16[512,1024]{1,0:T(8,128)(2,1)} %copy-done.9), channel_id=1, source_target_pairs={{0,2},{1,7},{2,4},{3,1},{4,6},{5,3},{6,0},{7,5},{8,10},{9,15},{10,... | collective-permute-start | bytes 3145736 | tf_op jit(solution)/shard_map/ppermute | solution.py:216
  92.6 1.8 %slice_subtract_fusion = (f32[512,128]{1,0:T(8,128)S(1)}, f32[512,128]{1,0:T(8,128)}) fusion(f32[1024,128]{1,0:T(8,128)S(1)} %maximum_convert_fusion, f32[512,128]{1,0:T(8,128)} %copy-done.13, f32[1024,128]{1,0:T(8,128)S(1)} %subtract_add_fusion, f32[512,128]{1,0:T(8,128)} %param.13), kind=kLoop, calls=%fused_computation.2 | loop fusion | flops 524288 | bytes 1572864 | tf_op jit(solution)/shard_map/sub | solution.py:316
  94.4 2.9 %collective-permute-start.21 = (f32[512,128]{1,0:T(8,128)S(1)}, f32[512,128]{1,0:T(8,128)S(1)}, u32[]{:S(2)}, u32[]{:S(2)}) collective-permute-start(f32[512,128]{1,0:T(8,128)S(1)} %get-tuple-element.126), channel_id=1, source_target_pairs={{0,64},{16,80},{32,96},{48,112},{64,0},{80,16},{96,32},{112,48},{1... | collective-permute-start | bytes 786440 | tf_op jit(solution)/shard_map/ppermute | solution.py:221
  97.3 4.0 %collective-permute-done.17.refs_6_ = s16[2,1040,256]{2,1,0:T(8,128)(2,1)} collective-permute-done((s16[2,1040,256]{2,1,0:T(8,128)(2,1)}, s16[2,1040,256]{2,1,0:T(8,128)(2,1)}, u32[]{:S(2)}, u32[]{:S(2)}) %collective-permute-start.17) | collective-permute-done | bytes 1064992 | tf_op jit(solution)/shard_map/ppermute | solution.py:216
  101.3 7.5 %partial_sums.6 = (s16[2,1040,256]{2,1,0:T(8,128)(2,1)}, s16[2,1040,256]{2,1,0:T(8,128)(2,1)}) custom-call(s32[34]{0:T(128)} %fusion.refs_0_.at_ref, bf16[1024,768]{1,0:T(8,128)(2,1)} %transposed.1.refs_1_, bf16[384,8192]{1,0:T(8,128)(2,1)} %refs_2_.7, bf16[384,8192]{1,0:T(8,128)(2,1)} %collective-permute-done.2.refs_3_, ...), custom_call_target="tpu_custom_call" | custom-call | flops 1000 | bytes 1000 | tf_op jit(solution)/shard_map/partial_sums/pallas_call | solution.py:87
  108.8 3.7 %collective-permute-done.20.refs_5_ = bf16[512,1024]{1,0:T(8,128)(2,1)} collective-permute-done((bf16[512,1024]{1,0:T(8,128)(2,1)}, bf16[512,1024]{1,0:T(8,128)(2,1)}, u32[]{:S(2)}, u32[]{:S(2)}) %collective-permute-start.20) | collective-permute-done | bytes 1048608 | tf_op jit(solution)/shard_map/ppermute | solution.py:216
  112.5 3.8 %collective-permute-start.24 = (bf16[512,1024]{1,0:T(8,128)(2,1)}, bf16[512,1024]{1,0:T(8,128)(2,1)}, u32[]{:S(2)}, u32[]{:S(2)}) collective-permute-start(bf16[512,1024]{1,0:T(8,128)(2,1)} %collective-permute-done.20.refs_5_), channel_id=1, source_target_pairs={{0,1},{1,0},{2,3},{3,2},{4,5},{5,4},{6,7},{7,6},{8,9},{9,8},{10,11... | collective-permute-start | bytes 3145736 | tf_op jit(solution)/shard_map/ppermute | solution.py:216
  116.3 1.7 %collective-permute-start.26 = (s16[2,1040,256]{2,1,0:T(8,128)(2,1)}, s16[2,1040,256]{2,1,0:T(8,128)(2,1)S(1)}, u32[]{:S(2)}, u32[]{:S(2)}) collective-permute-start(s16[2,1040,256]{2,1,0:T(8,128)(2,1)} %get-tuple-element.135), channel_id=1, source_target_pairs={{0,2},{1,7},{2,4},{3,1},{4,6},{5,3},{6,0},{7,5},{8,10},{9,15},{10,... | collective-permute-start | bytes 3194888 | tf_op jit(solution)/shard_map/ppermute | solution.py:216
  118.0 1.3 collective-permute-start.27
  120.3 1.8 %collective-permute-start.25 = (f32[1024,128]{1,0:T(8,128)S(1)}, f32[1024,128]{1,0:T(8,128)S(1)}, u32[]{:S(2)}, u32[]{:S(2)}) collective-permute-start(f32[1024,128]{1,0:T(8,128)S(1)} %constant_dynamic-update-slice_fusion.refs_0_.refs_1_), channel_id=1, source_target_pairs={{0,48},{16,0},{32,16},{48,32},{64,112},{80,64},{96,80},{112,96},{1... | collective-permute-start | bytes 1572872 | tf_op jit(solution)/shard_map/ppermute | solution.py:221
  122.1 7.9 %grad_columns.6.refs_5_ = f32[384,8192]{1,0:T(8,128)} custom-call(s32[34]{0:T(128)} %fusion.refs_0_.at_ref, bf16[384,1024]{1,0:T(8,128)(2,1)} %copy-done, bf16[512,1024]{1,0:T(8,128)(2,1)} %collective-permute-done.10.refs_2_, bf16[512,1024]{1,0:T(8,128)(2,1)} %collective-permute-done.19.refs_3_, ...), custom_call_target="tpu_custom_call", output_to_operand_aliasing={{}: (7, {})} | custom-call | flops 1000 | bytes 1000 | tf_op jit(solution)/shard_map/grad_columns/pallas_call | solution.py:144
  130.6 12.0 %collective-permute-done.27.refs_6_ = s16[2,1040,256]{2,1,0:T(8,128)(2,1)S(1)} collective-permute-done((s16[2,1040,256]{2,1,0:T(8,128)(2,1)}, s16[2,1040,256]{2,1,0:T(8,128)(2,1)S(1)}, u32[]{:S(2)}, u32[]{:S(2)}) %collective-permute-start.27) | collective-permute-done | bytes 1064992 | tf_op jit(solution)/shard_map/ppermute | solution.py:216
  142.6 1.0 copy-done.8
  143.5 5.7 %partial_sums.7 = (s16[1,1040,256]{2,1,0:T(8,128)(2,1)}, f32[512,1024]{1,0:T(8,128)}) custom-call(s32[34]{0:T(128)} %fusion.refs_0_.at_ref, bf16[1024,768]{1,0:T(8,128)(2,1)} %transposed.1.refs_1_, bf16[384,8192]{1,0:T(8,128)(2,1)} %refs_2_.7, bf16[384,8192]{1,0:T(8,128)(2,1)} %collective-permute-done.2.refs_3_, s16[4,1040,256]{2,1,0:T(8,128)(2,1)} %copy-done.1, ...), custom_call_target="tpu_custom_call" | custom-call | flops 1000 | bytes 1000 | tf_op jit(solution)/shard_map/partial_sums/pallas_call | solution.py:87
  150.8 3.1 %collective-permute-done.30.add_ref = s16[1,1040,256]{2,1,0:T(8,128)(2,1)} collective-permute-done((s16[1,1040,256]{2,1,0:T(8,128)(2,1)}, s16[1,1040,256]{2,1,0:T(8,128)(2,1)}, u32[]{:S(2)}, u32[]{:S(2)}) %collective-permute-start.30) | collective-permute-done | bytes 532512 | tf_op jit(solution)/shard_map/ppermute | solution.py:216
  153.9 3.0 %last_rows.1 = f32[512,1024]{1,0:T(8,128)} custom-call(s32[34]{0:T(128)} %fusion.refs_0_.at_ref, s16[1,1040,256]{2,1,0:T(8,128)(2,1)} %collective-permute-done.30.add_ref, f32[512,1024]{1,0:T(8,128)} %get-tuple-element.143._), custom_call_target="tpu_custom_call", output_to_operand_aliasing={{}: (2, {})} | custom-call | flops 1000 | bytes 1000 | tf_op jit(solution)/shard_map/last_rows/pallas_call | solution.py:104
  157.9 1.0 copy-done.11
  158.9 5.8 %grad_columns.7 = f32[384,8192]{1,0:T(8,128)} custom-call(s32[34]{0:T(128)} %fusion.refs_0_.at_ref, bf16[384,1024]{1,0:T(8,128)(2,1)} %copy-done, bf16[512,1024]{1,0:T(8,128)(2,1)} %copy-done.10, bf16[512,1024]{1,0:T(8,128)(2,1)} %collective-permute-done.22.refs_3_, bf16[512,1024]{1,0:T(8,128)(2,1)} %copy-done.11, ...), custom_call_target="tpu_custom_call", output_to_operand_aliasing={{}: (5, {})} | custom-call | flops 1000 | bytes 1000 | tf_op jit(solution)/shard_map/grad_columns/pallas_call | solution.py:144
  165.4 4.5 %assembled.1 = f32[512,1024]{1,0:T(8,128)} custom-call(s32[8]{0:T(128)} %fusion.1.at_ref, f32[1024,128]{1,0:T(8,128)} %copy-done.3, f32[1024,128]{1,0:T(8,128)} %copy-done.3, f32[1024,128]{1,0:T(8,128)} %copy-done.4, f32[1024,128]{1,0:T(8,128)} %copy-done.4, f32[1024,128]{1,0:T(8,128)} %copy-done.5, f32[1024,128]{1,0:T(8,128)} %copy-done.5, ...), custom_call_target="tpu_custom_call" | custom-call | flops 1000 | bytes 1000 | tf_op jit(solution)/shard_map/assembled/pallas_call | solution.py:191
  (70 shorter events, 8.3 us)
Async XLA Ops:
  0.6 16.9 %collective-permute-start.2 = (bf16[384,8192]{1,0:T(8,128)(2,1)}, bf16[384,8192]{1,0:T(8,128)(2,1)}, u32[]{:S(2)}, u32[]{:S(2)}) collective-permute-start(bf16[384,8192]{1,0:T(8,128)(2,1)} %refs_2_.7), channel_id=1, source_target_pairs={{0,1},{1,0},{2,3},{3,2},{4,5},{5,4},{6,7},{7,6},{8,9},{9,8},{10,11... | collective-permute-start | bytes 18874376 | tf_op jit(solution)/shard_map/ppermute | solution.py:216
  2.1 15.1 %collective-permute-start.1 = (bf16[512,1024]{1,0:T(8,128)(2,1)}, bf16[512,1024]{1,0:T(8,128)(2,1)}, u32[]{:S(2)}, u32[]{:S(2)}) collective-permute-start(bf16[512,1024]{1,0:T(8,128)(2,1)} %bitcast.6), channel_id=1, source_target_pairs={{0,1},{1,0},{2,3},{3,2},{4,5},{5,4},{6,7},{7,6},{8,9},{9,8},{10,11... | collective-permute-start | bytes 3145736 | tf_op jit(solution)/shard_map/ppermute | solution.py:216
  2.9 14.4 %copy-start.2 = (bf16[1,512,1024]{2,1,0:T(8,128)(2,1)S(1)}, bf16[1,512,1024]{2,1,0:T(8,128)(2,1)}, u32[]{:S(2)}) copy-start(bf16[1,512,1024]{2,1,0:T(8,128)(2,1)} %param.11) | copy-start | bytes 3145732
  4.3 10.0 %copy-start = (bf16[384,1024]{1,0:T(8,128)(2,1)}, bf16[384,1024]{1,0:T(8,128)(2,1)S(1)}, u32[]{:S(2)}) copy-start(bf16[384,1024]{1,0:T(8,128)(2,1)S(1)} %broadcast_multiply_fusion.own_ref.refs_1_) | copy-start | bytes 2359300
  4.3 10.0 %collective-permute-start = (bf16[384,1024]{1,0:T(8,128)(2,1)S(1)}, bf16[384,1024]{1,0:T(8,128)(2,1)}, u32[]{:S(2)}, u32[]{:S(2)}) collective-permute-start(bf16[384,1024]{1,0:T(8,128)(2,1)S(1)} %broadcast_multiply_fusion.own_ref.refs_1_), channel_id=1, source_target_pairs={{0,1},{1,0},{2,3},{3,2},{4,5},{5,4},{6,7},{7,6},{8,9},{9,8},{10,11... | collective-permute-start | bytes 2359304 | tf_op jit(solution)/shard_map/ppermute | solution.py:216
  4.8 15.4 %collective-permute-start.3 = (bf16[512,1024]{1,0:T(8,128)(2,1)}, bf16[512,1024]{1,0:T(8,128)(2,1)}, u32[]{:S(2)}, u32[]{:S(2)}) collective-permute-start(bf16[512,1024]{1,0:T(8,128)(2,1)} %bitcast.7), channel_id=1, source_target_pairs={{0,2},{1,7},{2,4},{3,1},{4,6},{5,3},{6,0},{7,5},{8,10},{9,15},{10,... | collective-permute-start | bytes 3145736 | tf_op jit(solution)/shard_map/ppermute | solution.py:216
  7.3 28.4 %collective-permute-start.5 = (bf16[512,1024]{1,0:T(8,128)(2,1)}, bf16[512,1024]{1,0:T(8,128)(2,1)S(1)}, u32[]{:S(2)}, u32[]{:S(2)}) collective-permute-start(bf16[512,1024]{1,0:T(8,128)(2,1)} %bitcast.8), channel_id=1, source_target_pairs={{0,8},{1,9},{2,10},{3,11},{4,12},{5,13},{6,14},{7,15},{8,0},{9,1},... | collective-permute-start | bytes 3145736 | tf_op jit(solution)/shard_map/ppermute | solution.py:216
  17.6 18.5 %collective-permute-start.4 = (bf16[512,1024]{1,0:T(8,128)(2,1)}, bf16[512,1024]{1,0:T(8,128)(2,1)}, u32[]{:S(2)}, u32[]{:S(2)}) collective-permute-start(bf16[512,1024]{1,0:T(8,128)(2,1)} %collective-permute-done.1.refs_3_), channel_id=1, source_target_pairs={{0,2},{1,7},{2,4},{3,1},{4,6},{5,3},{6,0},{7,5},{8,10},{9,15},{10,... | collective-permute-start | bytes 3145736 | tf_op jit(solution)/shard_map/ppermute | solution.py:216
  20.2 15.5 %collective-permute-start.6 = (bf16[1024,128]{1,0:T(8,128)(2,1)S(1)}, bf16[1024,128]{1,0:T(8,128)(2,1)S(1)}, u32[]{:S(2)}, u32[]{:S(2)}) collective-permute-start(bf16[1024,128]{1,0:T(8,128)(2,1)S(1)} %get-tuple-element.88), channel_id=1, source_target_pairs={{0,16},{16,32},{32,48},{48,0},{64,80},{80,96},{96,112},{112,64},{1... | collective-permute-start | bytes 786440 | tf_op jit(solution)/shard_map/ppermute | solution.py:221
  21.8 13.9 %collective-permute-start.7 = (bf16[1024,128]{1,0:T(8,128)(2,1)S(1)}, bf16[1024,128]{1,0:T(8,128)(2,1)}, u32[]{:S(2)}, u32[]{:S(2)}) collective-permute-start(bf16[1024,128]{1,0:T(8,128)(2,1)S(1)} %pad_maximum_fusion.2), channel_id=1, source_target_pairs={{0,48},{16,0},{32,16},{48,32},{64,112},{80,64},{96,80},{112,96},{1... | collective-permute-start | bytes 786440 | tf_op jit(solution)/shard_map/ppermute | solution.py:221
  24.0 12.1 %collective-permute-start.8 = (bf16[1024,128]{1,0:T(8,128)(2,1)S(1)}, bf16[1024,128]{1,0:T(8,128)(2,1)S(1)}, u32[]{:S(2)}, u32[]{:S(2)}) collective-permute-start(bf16[1024,128]{1,0:T(8,128)(2,1)S(1)} %get-tuple-element.90), channel_id=1, source_target_pairs={{0,32},{16,48},{32,0},{48,16},{64,96},{80,112},{96,64},{112,80},{1... | collective-permute-start | bytes 786440 | tf_op jit(solution)/shard_map/ppermute | solution.py:221
  35.7 1.0 copy-start.9
  36.0 0.8 copy-start.12
  36.8 38.6 %collective-permute-start.9 = (s16[4,1040,256]{2,1,0:T(8,128)(2,1)}, s16[4,1040,256]{2,1,0:T(8,128)(2,1)S(1)}, u32[]{:S(2)}, u32[]{:S(2)}) collective-permute-start(s16[4,1040,256]{2,1,0:T(8,128)(2,1)} %get-tuple-element.91), channel_id=1, source_target_pairs={{0,6},{1,3},{2,0},{3,5},{4,2},{5,7},{6,4},{7,1},{8,14},{9,11},{10,... | collective-permute-start | bytes 6389768 | tf_op jit(solution)/shard_map/ppermute | solution.py:216
  37.0 7.0 %collective-permute-start.11 = (bf16[512,1024]{1,0:T(8,128)(2,1)}, bf16[512,1024]{1,0:T(8,128)(2,1)}, u32[]{:S(2)}, u32[]{:S(2)}) collective-permute-start(bf16[512,1024]{1,0:T(8,128)(2,1)} %collective-permute-done.3.refs_4_), channel_id=1, source_target_pairs={{0,1},{1,0},{2,3},{3,2},{4,5},{5,4},{6,7},{7,6},{8,9},{9,8},{10,11... | collective-permute-start | bytes 3145736 | tf_op jit(solution)/shard_map/ppermute | solution.py:216
  41.3 5.3 %collective-permute-start.12 = (bf16[512,1024]{1,0:T(8,128)(2,1)}, bf16[512,1024]{1,0:T(8,128)(2,1)}, u32[]{:S(2)}, u32[]{:S(2)}) collective-permute-start(bf16[512,1024]{1,0:T(8,128)(2,1)} %collective-permute-done.4.refs_5_), channel_id=1, source_target_pairs={{0,1},{1,0},{2,3},{3,2},{4,5},{5,4},{6,7},{7,6},{8,9},{9,8},{10,11... | collective-permute-start | bytes 3145736 | tf_op jit(solution)/shard_map/ppermute | solution.py:216
  41.3 24.9 %collective-permute-start.15 = (s16[2,1040,256]{2,1,0:T(8,128)(2,1)}, s16[2,1040,256]{2,1,0:T(8,128)(2,1)}, u32[]{:S(2)}, u32[]{:S(2)}) collective-permute-start(s16[2,1040,256]{2,1,0:T(8,128)(2,1)} %get-tuple-element.106), channel_id=1, source_target_pairs={{0,8},{1,9},{2,10},{3,11},{4,12},{5,13},{6,14},{7,15},{8,0},{9,1},... | collective-permute-start | bytes 3194888 | tf_op jit(solution)/shard_map/ppermute | solution.py:216
  42.6 28.3 %collective-permute-start.10 = (bf16[512,1024]{1,0:T(8,128)(2,1)}, bf16[512,1024]{1,0:T(8,128)(2,1)}, u32[]{:S(2)}, u32[]{:S(2)}) collective-permute-start(bf16[512,1024]{1,0:T(8,128)(2,1)} %collective-permute-done.3.refs_4_), channel_id=1, source_target_pairs={{0,2},{1,7},{2,4},{3,1},{4,6},{5,3},{6,0},{7,5},{8,10},{9,15},{10,... | collective-permute-start | bytes 3145736 | tf_op jit(solution)/shard_map/ppermute | solution.py:216
  43.9 30.2 %collective-permute-start.13 = (bf16[512,1024]{1,0:T(8,128)(2,1)}, bf16[512,1024]{1,0:T(8,128)(2,1)}, u32[]{:S(2)}, u32[]{:S(2)}) collective-permute-start(bf16[512,1024]{1,0:T(8,128)(2,1)} %copy-done.9), channel_id=1, source_target_pairs={{0,1},{1,0},{2,3},{3,2},{4,5},{5,4},{6,7},{7,6},{8,9},{9,8},{10,11... | collective-permute-start | bytes 3145736 | tf_op jit(solution)/shard_map/ppermute | solution.py:216
  46.7 27.5 %collective-permute-start.14 = (f32[512,128]{1,0:T(8,128)S(1)}, f32[512,128]{1,0:T(8,128)S(1)}, u32[]{:S(2)}, u32[]{:S(2)}) collective-permute-start(f32[512,128]{1,0:T(8,128)S(1)} %slice.9), channel_id=1, source_target_pairs={{0,64},{16,80},{32,96},{48,112},{64,0},{80,16},{96,32},{112,48},{1... | collective-permute-start | bytes 786440 | tf_op jit(solution)/shard_map/ppermute | solution.py:221
  74.1 12.7 %copy-start.13 = (f32[512,128]{1,0:T(8,128)}, f32[512,128]{1,0:T(8,128)S(1)}, u32[]{:S(2)}) copy-start(f32[512,128]{1,0:T(8,128)S(1)} %collective-permute-done.14) | copy-start | bytes 786436
  75.4 11.4 %copy-start.1 = (s16[4,1040,256]{2,1,0:T(8,128)(2,1)}, s16[4,1040,256]{2,1,0:T(8,128)(2,1)S(1)}, u32[]{:S(2)}) copy-start(s16[4,1040,256]{2,1,0:T(8,128)(2,1)S(1)} %collective-permute-done.9.refs_5_.refs_4_) | copy-start | bytes 6389764
  75.4 14.4 %collective-permute-start.16 = (s16[2,1040,256]{2,1,0:T(8,128)(2,1)}, s16[2,1040,256]{2,1,0:T(8,128)(2,1)}, u32[]{:S(2)}, u32[]{:S(2)}) collective-permute-start(s16[2,1040,256]{2,1,0:T(8,128)(2,1)} %partial_sums.5), channel_id=1, source_target_pairs={{0,2},{1,7},{2,4},{3,1},{4,6},{5,3},{6,0},{7,5},{8,10},{9,15},{10,... | collective-permute-start | bytes 3194888 | tf_op jit(solution)/shard_map/ppermute | solution.py:216
  77.2 24.1 %collective-permute-start.17 = (s16[2,1040,256]{2,1,0:T(8,128)(2,1)}, s16[2,1040,256]{2,1,0:T(8,128)(2,1)}, u32[]{:S(2)}, u32[]{:S(2)}) collective-permute-start(s16[2,1040,256]{2,1,0:T(8,128)(2,1)} %get-tuple-element.116), channel_id=1, source_target_pairs={{0,2},{1,7},{2,4},{3,1},{4,6},{5,3},{6,0},{7,5},{8,10},{9,15},{10,... | collective-permute-start | bytes 3194888 | tf_op jit(solution)/shard_map/ppermute | solution.py:216
  77.2 31.6 %collective-permute-start.18 = (bf16[512,1024]{1,0:T(8,128)(2,1)}, bf16[512,1024]{1,0:T(8,128)(2,1)}, u32[]{:S(2)}, u32[]{:S(2)}) collective-permute-start(bf16[512,1024]{1,0:T(8,128)(2,1)} %collective-permute-done.10.refs_2_), channel_id=1, source_target_pairs={{0,8},{1,9},{2,10},{3,11},{4,12},{5,13},{6,14},{7,15},{8,0},{9,1},... | collective-permute-start | bytes 3145736 | tf_op jit(solution)/shard_map/ppermute | solution.py:216
  78.5 30.3 %collective-permute-start.19 = (bf16[512,1024]{1,0:T(8,128)(2,1)}, bf16[512,1024]{1,0:T(8,128)(2,1)}, u32[]{:S(2)}, u32[]{:S(2)}) collective-permute-start(bf16[512,1024]{1,0:T(8,128)(2,1)} %collective-permute-done.10.refs_2_), channel_id=1, source_target_pairs={{0,1},{1,0},{2,3},{3,2},{4,5},{5,4},{6,7},{7,6},{8,9},{9,8},{10,11... | collective-permute-start | bytes 3145736 | tf_op jit(solution)/shard_map/ppermute | solution.py:216
  89.9 22.6 %collective-permute-start.20 = (bf16[512,1024]{1,0:T(8,128)(2,1)}, bf16[512,1024]{1,0:T(8,128)(2,1)}, u32[]{:S(2)}, u32[]{:S(2)}) collective-permute-start(bf16[512,1024]{1,0:T(8,128)(2,1)} %copy-done.9), channel_id=1, source_target_pairs={{0,2},{1,7},{2,4},{3,1},{4,6},{5,3},{6,0},{7,5},{8,10},{9,15},{10,... | collective-permute-start | bytes 3145736 | tf_op jit(solution)/shard_map/ppermute | solution.py:216
  94.4 14.4 %collective-permute-start.21 = (f32[512,128]{1,0:T(8,128)S(1)}, f32[512,128]{1,0:T(8,128)S(1)}, u32[]{:S(2)}, u32[]{:S(2)}) collective-permute-start(f32[512,128]{1,0:T(8,128)S(1)} %get-tuple-element.126), channel_id=1, source_target_pairs={{0,64},{16,80},{32,96},{48,112},{64,0},{80,16},{96,32},{112,48},{1... | collective-permute-start | bytes 786440 | tf_op jit(solution)/shard_map/ppermute | solution.py:221
  112.5 7.8 %collective-permute-start.24 = (bf16[512,1024]{1,0:T(8,128)(2,1)}, bf16[512,1024]{1,0:T(8,128)(2,1)}, u32[]{:S(2)}, u32[]{:S(2)}) collective-permute-start(bf16[512,1024]{1,0:T(8,128)(2,1)} %collective-permute-done.20.refs_5_), channel_id=1, source_target_pairs={{0,1},{1,0},{2,3},{3,2},{4,5},{5,4},{6,7},{7,6},{8,9},{9,8},{10,11... | collective-permute-start | bytes 3145736 | tf_op jit(solution)/shard_map/ppermute | solution.py:216
  116.3 14.3 %collective-permute-start.26 = (s16[2,1040,256]{2,1,0:T(8,128)(2,1)}, s16[2,1040,256]{2,1,0:T(8,128)(2,1)S(1)}, u32[]{:S(2)}, u32[]{:S(2)}) collective-permute-start(s16[2,1040,256]{2,1,0:T(8,128)(2,1)} %get-tuple-element.135), channel_id=1, source_target_pairs={{0,2},{1,7},{2,4},{3,1},{4,6},{5,3},{6,0},{7,5},{8,10},{9,15},{10,... | collective-permute-start | bytes 3194888 | tf_op jit(solution)/shard_map/ppermute | solution.py:216
  118.0 24.6 %collective-permute-start.27 = (s16[2,1040,256]{2,1,0:T(8,128)(2,1)}, s16[2,1040,256]{2,1,0:T(8,128)(2,1)S(1)}, u32[]{:S(2)}, u32[]{:S(2)}) collective-permute-start(s16[2,1040,256]{2,1,0:T(8,128)(2,1)} %get-tuple-element.136), channel_id=1, source_target_pairs={{0,8},{1,9},{2,10},{3,11},{4,12},{5,13},{6,14},{7,15},{8,0},{9,1},... | collective-permute-start | bytes 3194888 | tf_op jit(solution)/shard_map/ppermute | solution.py:216
  119.3 30.0 %collective-permute-start.22 = (bf16[512,1024]{1,0:T(8,128)(2,1)}, bf16[512,1024]{1,0:T(8,128)(2,1)}, u32[]{:S(2)}, u32[]{:S(2)}) collective-permute-start(bf16[512,1024]{1,0:T(8,128)(2,1)} %collective-permute-done.13.refs_5_), channel_id=1, source_target_pairs={{0,2},{1,7},{2,4},{3,1},{4,6},{5,3},{6,0},{7,5},{8,10},{9,15},{10,... | collective-permute-start | bytes 3145736 | tf_op jit(solution)/shard_map/ppermute | solution.py:216
  119.3 10.7 %copy-start.3 = (f32[1024,128]{1,0:T(8,128)}, f32[1024,128]{1,0:T(8,128)S(1)}, u32[]{:S(2)}) copy-start(f32[1024,128]{1,0:T(8,128)S(1)} %constant_dynamic-update-slice_fusion.refs_0_.refs_1_) | copy-start | bytes 1572868
  119.4 29.9 %collective-permute-start.23 = (f32[1024,128]{1,0:T(8,128)S(1)}, f32[1024,128]{1,0:T(8,128)S(1)}, u32[]{:S(2)}, u32[]{:S(2)}) collective-permute-start(f32[1024,128]{1,0:T(8,128)S(1)} %constant_dynamic-update-slice_fusion.refs_0_.refs_1_), channel_id=1, source_target_pairs={{0,16},{16,32},{32,48},{48,0},{64,80},{80,96},{96,112},{112,64},{1... | collective-permute-start | bytes 1572872 | tf_op jit(solution)/shard_map/ppermute | solution.py:221
  120.3 29.0 %collective-permute-start.25 = (f32[1024,128]{1,0:T(8,128)S(1)}, f32[1024,128]{1,0:T(8,128)S(1)}, u32[]{:S(2)}, u32[]{:S(2)}) collective-permute-start(f32[1024,128]{1,0:T(8,128)S(1)} %constant_dynamic-update-slice_fusion.refs_0_.refs_1_), channel_id=1, source_target_pairs={{0,48},{16,0},{32,16},{48,32},{64,112},{80,64},{96,80},{112,96},{1... | collective-permute-start | bytes 1572872 | tf_op jit(solution)/shard_map/ppermute | solution.py:221
  130.6 12.0 %copy-start.7 = (s16[2,1040,256]{2,1,0:T(8,128)(2,1)}, s16[2,1040,256]{2,1,0:T(8,128)(2,1)S(1)}, u32[]{:S(2)}) copy-start(s16[2,1040,256]{2,1,0:T(8,128)(2,1)S(1)} %collective-permute-done.26.refs_5_) | copy-start | bytes 3194884
  142.6 1.0 copy-start.8
  149.2 7.7 %copy-start.4 = (f32[1024,128]{1,0:T(8,128)}, f32[1024,128]{1,0:T(8,128)S(1)}, u32[]{:S(2)}) copy-start(f32[1024,128]{1,0:T(8,128)S(1)} %collective-permute-done.23.refs_2_.refs_3_) | copy-start | bytes 1572868
  149.3 7.6 %copy-start.5 = (f32[1024,128]{1,0:T(8,128)}, f32[1024,128]{1,0:T(8,128)S(1)}, u32[]{:S(2)}) copy-start(f32[1024,128]{1,0:T(8,128)S(1)} %collective-permute-done.25.refs_4_.refs_5_) | copy-start | bytes 1572868
  149.3 7.6 %collective-permute-start.28 = (bf16[512,1024]{1,0:T(8,128)(2,1)}, bf16[512,1024]{1,0:T(8,128)(2,1)S(1)}, u32[]{:S(2)}, u32[]{:S(2)}) collective-permute-start(bf16[512,1024]{1,0:T(8,128)(2,1)} %collective-permute-done.18.refs_4_), channel_id=1, source_target_pairs={{0,1},{1,0},{2,3},{3,2},{4,5},{5,4},{6,7},{7,6},{8,9},{9,8},{10,11... | collective-permute-start | bytes 3145736 | tf_op jit(solution)/shard_map/ppermute | solution.py:216
  149.4 7.6 %collective-permute-start.29 = (bf16[512,1024]{1,0:T(8,128)(2,1)}, bf16[512,1024]{1,0:T(8,128)(2,1)S(1)}, u32[]{:S(2)}, u32[]{:S(2)}) collective-permute-start(bf16[512,1024]{1,0:T(8,128)(2,1)} %collective-permute-done.22.refs_3_), channel_id=1, source_target_pairs={{0,1},{1,0},{2,3},{3,2},{4,5},{5,4},{6,7},{7,6},{8,9},{9,8},{10,11... | collective-permute-start | bytes 3145736 | tf_op jit(solution)/shard_map/ppermute | solution.py:216
  149.9 4.0 %collective-permute-start.30 = (s16[1,1040,256]{2,1,0:T(8,128)(2,1)}, s16[1,1040,256]{2,1,0:T(8,128)(2,1)}, u32[]{:S(2)}, u32[]{:S(2)}) collective-permute-start(s16[1,1040,256]{2,1,0:T(8,128)(2,1)} %get-tuple-element.142), channel_id=1, source_target_pairs={{0,1},{1,0},{2,3},{3,2},{4,5},{5,4},{6,7},{7,6},{8,9},{9,8},{10,11... | collective-permute-start | bytes 1597448 | tf_op jit(solution)/shard_map/ppermute | solution.py:216
  150.0 14.7 %collective-permute-start.31 = (f32[1024,128]{1,0:T(8,128)S(1)}, f32[1024,128]{1,0:T(8,128)S(1)}, u32[]{:S(2)}, u32[]{:S(2)}) collective-permute-start(f32[1024,128]{1,0:T(8,128)S(1)} %collective-permute-done.23.refs_2_.refs_3_), channel_id=1, source_target_pairs={{0,16},{16,32},{32,48},{48,0},{64,80},{80,96},{96,112},{112,64},{1... | collective-permute-start | bytes 1572872 | tf_op jit(solution)/shard_map/ppermute | solution.py:221
  156.9 1.0 copy-start.10
  157.9 1.0 copy-start.11
  164.7 0.8 copy-start.6

commit v4 on v3

--- a/solution.py
+++ b/solution.py
@@ -12,7 +12,7 @@
 group_rows = 64
 half = 256
 MB = 1 << 20
-vmem = 60 * MB
+vmem = 28 * MB
 tiny = pl.CostEstimate(flops=1000, bytes_accessed=1000, transcendentals=0)
 
 

time: 171 us -> 164 us (0.959)
  Pallas kernels: 66 us -> 49 us
  waiting for transfers between devices: 45.5 us -> 57.2 us
    ppermute x8, waiting for transfers between devices: 3.56 us -> 11.8 us  [sent_rep(): return lax.ppermute(array, 'rep', pairs)]
    pallas_call x4, Pallas kernels: 28.4 us -> 22.2 us  [sums(): pl.pallas_call(lambda *refs: sums_kernel(groups, len(adds), *refs), grid_...]
    pallas_call x4, Pallas kernels: 27.1 us -> 21.9 us  [grad_columns(): pl.pallas_call(lambda *refs: columns_kernel(n, *refs), grid_spec=pltpu.Pr...]
    ppermute x24, waiting for transfers between devices: 41.9 us -> 45.3 us  [sent(): return lax.ppermute(array, 'fsdp', pairs)]
    pallas_call x1, Pallas kernels: 2.97 us -> 0.46 us  [transposed(): pl.pallas_call(transpose_kernel, grid=(1,), in_specs=[pl.BlockSpec(own.sh...]
    pallas_call x1, Pallas kernels: 4.49 us -> 2.48 us  [assembled(): pl.pallas_call(assemble_kernel, grid_spec=pltpu.PrefetchScalarGridSpec(nu...]
  transfers between devices with their start and end apart: 32 -> 32, of which waited for: 13 -> 13; matrix products, arithmetic and copies ran while one was open for 5% -> 4% of each run, Pallas kernels for 36% -> 28%
where the time goes in v4:
time: 164 us; the launch traced here: 163 us
  waiting for transfers between devices  57.2 us (35%)
  Pallas kernels  49 us (30%)
  starting transfers between devices  45.3 us (28%)
  local copies, waits for them, and re-layouts  6.74 us (4%)
  other arithmetic  4.21 us (3%)
    ppermute x24, waiting for transfers between devices, sent(): return lax.ppermute(array, 'fsdp', pairs)  45.3 us
    ppermute x24, starting transfers between devices, sent(): return lax.ppermute(array, 'fsdp', pairs)  30.8 us
    pallas_call x4, Pallas kernels, sums(): pl.pallas_call(lambda *refs: sums_kernel(groups, len(adds), *refs), grid_...  22.2 us
    pallas_call x4, Pallas kernels, grad_columns(): pl.pallas_call(lambda *refs: columns_kernel(n, *refs), grid_spec=pltpu.Pr...  21.9 us
    ppermute x8, starting transfers between devices, sent_rep(): return lax.ppermute(array, 'rep', pairs)  14.6 us
    ppermute x8, waiting for transfers between devices, sent_rep(): return lax.ppermute(array, 'rep', pairs)  11.8 us
    unnamed x29, local copies, waits for them, and re-layouts  4.03 us
  transfers between devices with their start and end apart: 32, of which 13 were waited for; matrix products, arithmetic and copies ran while one was open for 4% of the time, Pallas kernels for 28%

profile of v4, /device:TPU:1, one launch (start us, length us, event | category | flops | bytes accessed | tf_op | source)
XLA Modules:
  0.0 163.3 jit_solution(15137824744761759429)
XLA Ops:
  0.6 1.5 collective-permute-start.2
  2.9 1.3 broadcast_multiply_fusion.own_ref.refs_1_
  4.8 2.6 %collective-permute-start.3 = (bf16[512,1024]{1,0:T(8,128)(2,1)}, bf16[512,1024]{1,0:T(8,128)(2,1)}, u32[]{:S(2)}, u32[]{:S(2)}) collective-permute-start(bf16[512,1024]{1,0:T(8,128)(2,1)} %bitcast.9), channel_id=1, source_target_pairs={{0,2},{1,7},{2,4},{3,1},{4,6},{5,3},{6,0},{7,5},{8,10},{9,15},{10,... | collective-permute-start | bytes 3145736 | tf_op jit(solution)/shard_map/ppermute | solution.py:216
  7.3 1.3 collective-permute-start.5
  10.0 4.2 %collective-permute-done.sib_ref = bf16[384,1024]{1,0:T(8,128)(2,1)S(1)} collective-permute-done((bf16[384,1024]{1,0:T(8,128)(2,1)S(1)}, bf16[384,1024]{1,0:T(8,128)(2,1)S(1)}, u32[]{:S(2)}, u32[]{:S(2)}) %collective-permute-start) | collective-permute-done | bytes 786464 | tf_op jit(solution)/shard_map/ppermute | solution.py:216
  15.0 1.1 copy-done.5
  17.0 2.6 %collective-permute-start.4 = (bf16[512,1024]{1,0:T(8,128)(2,1)}, bf16[512,1024]{1,0:T(8,128)(2,1)}, u32[]{:S(2)}, u32[]{:S(2)}) collective-permute-start(bf16[512,1024]{1,0:T(8,128)(2,1)} %collective-permute-done.1.refs_3_), channel_id=1, source_target_pairs={{0,2},{1,7},{2,4},{3,1},{4,6},{5,3},{6,0},{7,5},{8,10},{9,15},{10,... | collective-permute-start | bytes 3145736 | tf_op jit(solution)/shard_map/ppermute | solution.py:216
  19.6 1.6 %collective-permute-start.6 = (bf16[1024,128]{1,0:T(8,128)(2,1)S(1)}, bf16[1024,128]{1,0:T(8,128)(2,1)S(1)}, u32[]{:S(2)}, u32[]{:S(2)}) collective-permute-start(bf16[1024,128]{1,0:T(8,128)(2,1)S(1)} %get-tuple-element.88), channel_id=1, source_target_pairs={{0,16},{16,32},{32,48},{48,0},{64,80},{80,96},{96,112},{112,64},{1... | collective-permute-start | bytes 786440 | tf_op jit(solution)/shard_map/ppermute | solution.py:221
  21.2 2.1 %collective-permute-start.7 = (bf16[1024,128]{1,0:T(8,128)(2,1)S(1)}, bf16[1024,128]{1,0:T(8,128)(2,1)S(1)}, u32[]{:S(2)}, u32[]{:S(2)}) collective-permute-start(bf16[1024,128]{1,0:T(8,128)(2,1)S(1)} %pad_maximum_fusion.2), channel_id=1, source_target_pairs={{0,48},{16,0},{32,16},{48,32},{64,112},{80,64},{96,80},{112,96},{1... | collective-permute-start | bytes 786440 | tf_op jit(solution)/shard_map/ppermute | solution.py:221
  23.4 1.3 collective-permute-start.8
  24.7 9.2 %partial_sums.4 = (s16[2,1040,256]{2,1,0:T(8,128)(2,1)}, s16[4,1040,256]{2,1,0:T(8,128)(2,1)}, s16[2,1040,256]{2,1,0:T(8,128)(2,1)S(1)}) custom-call(s32[34]{0:T(128)S(1)} %fusion.refs_0_.at_ref, bf16[1024,768]{1,0:T(8,128)(2,1)S(1)} %transposed.1.refs_1_, bf16[384,8192]{1,0:T(8,128)(2,1)S(1)} %copy-done, bf16[384,8192]{1,0:T(8,128)(2,1)} %collective-permute-done.2.refs_3_), custom_call_target="tpu_custom_call" | custom-call | flops 1000 | bytes 1000 | tf_op jit(solution)/shard_map/partial_sums/pallas_call | solution.py:87
  34.9 1.3 collective-permute-start.9
  36.3 4.3 %collective-permute-start.11 = (bf16[512,1024]{1,0:T(8,128)(2,1)}, bf16[512,1024]{1,0:T(8,128)(2,1)S(1)}, u32[]{:S(2)}, u32[]{:S(2)}) collective-permute-start(bf16[512,1024]{1,0:T(8,128)(2,1)} %collective-permute-done.3.refs_4_), channel_id=1, source_target_pairs={{0,1},{1,0},{2,3},{3,2},{4,5},{5,4},{6,7},{7,6},{8,9},{9,8},{10,11... | collective-permute-start | bytes 3145736 | tf_op jit(solution)/shard_map/ppermute | solution.py:216
  40.6 1.3 collective-permute-start.15
  41.9 2.7 %collective-permute-done.11.refs_2_ = bf16[512,1024]{1,0:T(8,128)(2,1)S(1)} collective-permute-done((bf16[512,1024]{1,0:T(8,128)(2,1)}, bf16[512,1024]{1,0:T(8,128)(2,1)S(1)}, u32[]{:S(2)}, u32[]{:S(2)}) %collective-permute-start.11) | collective-permute-done | bytes 1048608 | tf_op jit(solution)/shard_map/ppermute | solution.py:216
  44.6 1.0 copy-done.2
  45.9 1.0 constant_dynamic-slice_fusion.3
  47.0 1.3 subtract_add_fusion
  48.4 3.0 %collective-permute-start.14 = (f32[512,128]{1,0:T(8,128)S(1)}, f32[512,128]{1,0:T(8,128)S(1)}, u32[]{:S(2)}, u32[]{:S(2)}) collective-permute-start(f32[512,128]{1,0:T(8,128)S(1)} %slice.9), channel_id=1, source_target_pairs={{0,64},{16,80},{32,96},{48,112},{64,0},{80,16},{96,32},{112,48},{1... | collective-permute-start | bytes 786440 | tf_op jit(solution)/shard_map/ppermute | solution.py:221
  51.4 6.1 %grad_columns.4.refs_6_ = f32[384,8192]{1,0:T(8,128)} custom-call(s32[34]{0:T(128)S(1)} %fusion.refs_0_.at_ref, bf16[384,1024]{1,0:T(8,128)(2,1)S(1)} %broadcast_multiply_fusion.own_ref.refs_1_, bf16[512,1024]{1,0:T(8,128)(2,1)S(1)} %bitcast.13, bf16[512,1024]{1,0:T(8,128)(2,1)} %collective-permute-done.1.refs_3_, ...), custom_call_target="tpu_custom_call" | custom-call | flops 1000 | bytes 1000 | tf_op jit(solution)/shard_map/grad_columns/pallas_call | solution.py:144
  57.4 8.0 %collective-permute-done.15.refs_4_ = s16[2,1040,256]{2,1,0:T(8,128)(2,1)} collective-permute-done((s16[2,1040,256]{2,1,0:T(8,128)(2,1)}, s16[2,1040,256]{2,1,0:T(8,128)(2,1)}, u32[]{:S(2)}, u32[]{:S(2)}) %collective-permute-start.15) | collective-permute-done | bytes 1064992 | tf_op jit(solution)/shard_map/ppermute | solution.py:216
  65.5 3.2 %partial_sums.5 = s16[2,1040,256]{2,1,0:T(8,128)(2,1)S(1)} custom-call(s32[34]{0:T(128)S(1)} %fusion.refs_0_.at_ref, bf16[1024,768]{1,0:T(8,128)(2,1)S(1)} %transposed.1.refs_1_, bf16[384,8192]{1,0:T(8,128)(2,1)S(1)} %bitcast.7, bf16[384,8192]{1,0:T(8,128)(2,1)} %collective-permute-done.2.refs_3_, s16[2,1040,256]{2,1,0:T(8,128)(2,1)} %collective-permute-done.15.refs_4_), custom_call_target="tpu_custom_call" | custom-call | flops 1000 | bytes 1000 | tf_op jit(solution)/shard_map/partial_sums/pallas_call | solution.py:87
  68.7 4.7 %collective-permute-done.14 = f32[512,128]{1,0:T(8,128)S(1)} collective-permute-done((f32[512,128]{1,0:T(8,128)S(1)}, f32[512,128]{1,0:T(8,128)S(1)}, u32[]{:S(2)}, u32[]{:S(2)}) %collective-permute-start.14) | collective-permute-done | bytes 262176 | tf_op jit(solution)/shard_map/ppermute | solution.py:221
  73.4 1.4 collective-permute-done.9.refs_5_.refs_4_
  74.8 1.8 %collective-permute-start.16 = (s16[2,1040,256]{2,1,0:T(8,128)(2,1)S(1)}, s16[2,1040,256]{2,1,0:T(8,128)(2,1)S(1)}, u32[]{:S(2)}, u32[]{:S(2)}) collective-permute-start(s16[2,1040,256]{2,1,0:T(8,128)(2,1)S(1)} %partial_sums.5), channel_id=1, source_target_pairs={{0,2},{1,7},{2,4},{3,1},{4,6},{5,3},{6,0},{7,5},{8,10},{9,15},{10,... | collective-permute-start | bytes 3194888 | tf_op jit(solution)/shard_map/ppermute | solution.py:216
  76.6 1.3 collective-permute-start.18
  77.9 1.6 collective-permute-start.19
  79.5 6.1 %grad_columns.5.refs_7_ = f32[384,8192]{1,0:T(8,128)} custom-call(s32[34]{0:T(128)S(1)} %fusion.refs_0_.at_ref, bf16[384,1024]{1,0:T(8,128)(2,1)S(1)} %broadcast_multiply_fusion.own_ref.refs_1_, bf16[512,1024]{1,0:T(8,128)(2,1)S(1)} %copy-done.3, bf16[512,1024]{1,0:T(8,128)(2,1)} %collective-permute-done.12.refs_3_, ...), custom_call_target="tpu_custom_call", output_to_operand_aliasing={{}: (6, {})} | custom-call | flops 1000 | bytes 1000 | tf_op jit(solution)/shard_map/grad_columns/pallas_call | solution.py:144
  85.6 3.4 %collective-permute-done.16.refs_4_ = s16[2,1040,256]{2,1,0:T(8,128)(2,1)S(1)} collective-permute-done((s16[2,1040,256]{2,1,0:T(8,128)(2,1)S(1)}, s16[2,1040,256]{2,1,0:T(8,128)(2,1)S(1)}, u32[]{:S(2)}, u32[]{:S(2)}) %collective-permute-start.16) | collective-permute-done | bytes 1064992 | tf_op jit(solution)/shard_map/ppermute | solution.py:216
  88.9 2.7 %collective-permute-start.20 = (bf16[512,1024]{1,0:T(8,128)(2,1)}, bf16[512,1024]{1,0:T(8,128)(2,1)S(1)}, u32[]{:S(2)}, u32[]{:S(2)}) collective-permute-start(bf16[512,1024]{1,0:T(8,128)(2,1)} %collective-permute-done.5.refs_4_), channel_id=1, source_target_pairs={{0,2},{1,7},{2,4},{3,1},{4,6},{5,3},{6,0},{7,5},{8,10},{9,15},{10,... | collective-permute-start | bytes 3145736 | tf_op jit(solution)/shard_map/ppermute | solution.py:216
  92.4 2.9 %collective-permute-start.21 = (f32[512,128]{1,0:T(8,128)S(1)}, f32[512,128]{1,0:T(8,128)S(1)}, u32[]{:S(2)}, u32[]{:S(2)}) collective-permute-start(f32[512,128]{1,0:T(8,128)S(1)} %get-tuple-element.126), channel_id=1, source_target_pairs={{0,64},{16,80},{32,96},{48,112},{64,0},{80,16},{96,32},{112,48},{1... | collective-permute-start | bytes 786440 | tf_op jit(solution)/shard_map/ppermute | solution.py:221
  95.4 5.0 %collective-permute-done.17.refs_6_ = s16[2,1040,256]{2,1,0:T(8,128)(2,1)S(1)} collective-permute-done((s16[2,1040,256]{2,1,0:T(8,128)(2,1)S(1)}, s16[2,1040,256]{2,1,0:T(8,128)(2,1)S(1)}, u32[]{:S(2)}, u32[]{:S(2)}) %collective-permute-start.17) | collective-permute-done | bytes 1064992 | tf_op jit(solution)/shard_map/ppermute | solution.py:216
  100.3 5.3 %partial_sums.6 = (s16[2,1040,256]{2,1,0:T(8,128)(2,1)S(1)}, s16[2,1040,256]{2,1,0:T(8,128)(2,1)S(1)}) custom-call(s32[34]{0:T(128)S(1)} %fusion.refs_0_.at_ref, bf16[1024,768]{1,0:T(8,128)(2,1)S(1)} %transposed.1.refs_1_, bf16[384,8192]{1,0:T(8,128)(2,1)S(1)} %bitcast.7, bf16[384,8192]{1,0:T(8,128)(2,1)} %collective-permute-done.2.refs_3_, ...), custom_call_target="tpu_custom_call" | custom-call | flops 1000 | bytes 1000 | tf_op jit(solution)/shard_map/partial_sums/pallas_call | solution.py:87
  105.7 2.5 %collective-permute-done.21 = f32[512,128]{1,0:T(8,128)S(1)} collective-permute-done((f32[512,128]{1,0:T(8,128)S(1)}, f32[512,128]{1,0:T(8,128)S(1)}, u32[]{:S(2)}, u32[]{:S(2)}) %collective-permute-start.21) | collective-permute-done | bytes 262176 | tf_op jit(solution)/shard_map/ppermute | solution.py:221
  108.2 3.4 %collective-permute-done.20.refs_5_ = bf16[512,1024]{1,0:T(8,128)(2,1)S(1)} collective-permute-done((bf16[512,1024]{1,0:T(8,128)(2,1)}, bf16[512,1024]{1,0:T(8,128)(2,1)S(1)}, u32[]{:S(2)}, u32[]{:S(2)}) %collective-permute-start.20) | collective-permute-done | bytes 1048608 | tf_op jit(solution)/shard_map/ppermute | solution.py:216
  111.6 3.8 %collective-permute-start.24 = (bf16[512,1024]{1,0:T(8,128)(2,1)S(1)}, bf16[512,1024]{1,0:T(8,128)(2,1)S(1)}, u32[]{:S(2)}, u32[]{:S(2)}) collective-permute-start(bf16[512,1024]{1,0:T(8,128)(2,1)S(1)} %collective-permute-done.20.refs_5_), channel_id=1, source_target_pairs={{0,1},{1,0},{2,3},{3,2},{4,5},{5,4},{6,7},{7,6},{8,9},{9,8},{10,11... | collective-permute-start | bytes 3145736 | tf_op jit(solution)/shard_map/ppermute | solution.py:216
  115.3 1.7 %collective-permute-start.26 = (s16[2,1040,256]{2,1,0:T(8,128)(2,1)S(1)}, s16[2,1040,256]{2,1,0:T(8,128)(2,1)S(1)}, u32[]{:S(2)}, u32[]{:S(2)}) collective-permute-start(s16[2,1040,256]{2,1,0:T(8,128)(2,1)S(1)} %get-tuple-element.135), channel_id=1, source_target_pairs={{0,2},{1,7},{2,4},{3,1},{4,6},{5,3},{6,0},{7,5},{8,10},{9,15},{10,... | collective-permute-start | bytes 3194888 | tf_op jit(solution)/shard_map/ppermute | solution.py:216
  117.1 1.3 collective-permute-start.27
  119.4 1.8 %collective-permute-start.25 = (f32[1024,128]{1,0:T(8,128)S(1)}, f32[1024,128]{1,0:T(8,128)S(1)}, u32[]{:S(2)}, u32[]{:S(2)}) collective-permute-start(f32[1024,128]{1,0:T(8,128)S(1)} %constant_dynamic-update-slice_fusion.refs_0_.refs_1_), channel_id=1, source_target_pairs={{0,48},{16,0},{32,16},{48,32},{64,112},{80,64},{96,80},{112,96},{1... | collective-permute-start | bytes 1572872 | tf_op jit(solution)/shard_map/ppermute | solution.py:221
  121.2 6.3 %grad_columns.6.refs_5_ = f32[384,8192]{1,0:T(8,128)} custom-call(s32[34]{0:T(128)S(1)} %fusion.refs_0_.at_ref, bf16[384,1024]{1,0:T(8,128)(2,1)S(1)} %broadcast_multiply_fusion.own_ref.refs_1_, bf16[512,1024]{1,0:T(8,128)(2,1)} %collective-permute-done.10.refs_2_, ...), custom_call_target="tpu_custom_call", output_to_operand_aliasing={{}: (7, {})} | custom-call | flops 1000 | bytes 1000 | tf_op jit(solution)/shard_map/grad_columns/pallas_call | solution.py:144
  127.4 2.0 %collective-permute-done.26.refs_5_ = s16[2,1040,256]{2,1,0:T(8,128)(2,1)S(1)} collective-permute-done((s16[2,1040,256]{2,1,0:T(8,128)(2,1)S(1)}, s16[2,1040,256]{2,1,0:T(8,128)(2,1)S(1)}, u32[]{:S(2)}, u32[]{:S(2)}) %collective-permute-start.26) | collective-permute-done | bytes 1064992 | tf_op jit(solution)/shard_map/ppermute | solution.py:216
  129.5 11.9 %collective-permute-done.27.refs_6_ = s16[2,1040,256]{2,1,0:T(8,128)(2,1)S(1)} collective-permute-done((s16[2,1040,256]{2,1,0:T(8,128)(2,1)S(1)}, s16[2,1040,256]{2,1,0:T(8,128)(2,1)S(1)}, u32[]{:S(2)}, u32[]{:S(2)}) %collective-permute-start.27) | collective-permute-done | bytes 1064992 | tf_op jit(solution)/shard_map/ppermute | solution.py:216
  141.3 4.5 %partial_sums.7 = (s16[1,1040,256]{2,1,0:T(8,128)(2,1)S(1)}, f32[512,1024]{1,0:T(8,128)}) custom-call(s32[34]{0:T(128)S(1)} %fusion.refs_0_.at_ref, bf16[1024,768]{1,0:T(8,128)(2,1)S(1)} %transposed.1.refs_1_, bf16[384,8192]{1,0:T(8,128)(2,1)S(1)} %bitcast.7, bf16[384,8192]{1,0:T(8,128)(2,1)} %collective-permute-done.2.refs_3_, ...), custom_call_target="tpu_custom_call" | custom-call | flops 1000 | bytes 1000 | tf_op jit(solution)/shard_map/partial_sums/pallas_call | solution.py:87
  147.4 3.5 %collective-permute-done.30.add_ref = s16[1,1040,256]{2,1,0:T(8,128)(2,1)S(1)} collective-permute-done((s16[1,1040,256]{2,1,0:T(8,128)(2,1)S(1)}, s16[1,1040,256]{2,1,0:T(8,128)(2,1)S(1)}, u32[]{:S(2)}, u32[]{:S(2)}) %collective-permute-start.30) | collective-permute-done | bytes 532512 | tf_op jit(solution)/shard_map/ppermute | solution.py:216
  150.9 1.9 %last_rows.1 = f32[512,1024]{1,0:T(8,128)} custom-call(s32[34]{0:T(128)S(1)} %fusion.refs_0_.at_ref, s16[1,1040,256]{2,1,0:T(8,128)(2,1)S(1)} %collective-permute-done.30.add_ref, f32[512,1024]{1,0:T(8,128)} %get-tuple-element.143._), custom_call_target="tpu_custom_call", output_to_operand_aliasing={{}: (2, {})} | custom-call | flops 1000 | bytes 1000 | tf_op jit(solution)/shard_map/last_rows/pallas_call | solution.py:104
  152.7 3.5 %grad_columns.7 = f32[384,8192]{1,0:T(8,128)} custom-call(s32[34]{0:T(128)S(1)} %fusion.refs_0_.at_ref, bf16[384,1024]{1,0:T(8,128)(2,1)S(1)} %broadcast_multiply_fusion.own_ref.refs_1_, bf16[512,1024]{1,0:T(8,128)(2,1)S(1)} %collective-permute-done.28.refs_2_, ...), custom_call_target="tpu_custom_call", output_to_operand_aliasing={{}: (5, {})} | custom-call | flops 1000 | bytes 1000 | tf_op jit(solution)/shard_map/grad_columns/pallas_call | solution.py:144
  156.3 4.6 %collective-permute-done.31.refs_6_.refs_7_ = f32[1024,128]{1,0:T(8,128)S(1)} collective-permute-done((f32[1024,128]{1,0:T(8,128)S(1)}, f32[1024,128]{1,0:T(8,128)S(1)}, u32[]{:S(2)}, u32[]{:S(2)}) %collective-permute-start.31) | collective-permute-done | bytes 524320 | tf_op jit(solution)/shard_map/ppermute | solution.py:221
  160.8 2.5 %assembled.1 = f32[512,1024]{1,0:T(8,128)} custom-call(s32[8]{0:T(128)S(1)} %fusion.1.at_ref, f32[1024,128]{1,0:T(8,128)S(1)} %constant_dynamic-update-slice_fusion.refs_0_.refs_1_, f32[1024,128]{1,0:T(8,128)S(1)} %constant_dynamic-update-slice_fusion.refs_0_.refs_1_, f32[1024,128]{1,0:T(8,128)S(1)} %collective-permute-done.23.refs_2_.refs_3_, ...), custom_call_target="tpu_custom_call" | custom-call | flops 1000 | bytes 1000 | tf_op jit(solution)/shard_map/assembled/pallas_call | solution.py:191
  (71 shorter events, 9.2 us)
Async XLA Ops:
  0.6 16.3 %collective-permute-start.2 = (bf16[384,8192]{1,0:T(8,128)(2,1)}, bf16[384,8192]{1,0:T(8,128)(2,1)}, u32[]{:S(2)}, u32[]{:S(2)}) collective-permute-start(bf16[384,8192]{1,0:T(8,128)(2,1)} %refs_2_.7), channel_id=1, source_target_pairs={{0,1},{1,0},{2,3},{3,2},{4,5},{5,4},{6,7},{7,6},{8,9},{9,8},{10,11... | collective-permute-start | bytes 18874376 | tf_op jit(solution)/shard_map/ppermute | solution.py:216
  2.1 14.5 %collective-permute-start.1 = (bf16[512,1024]{1,0:T(8,128)(2,1)}, bf16[512,1024]{1,0:T(8,128)(2,1)}, u32[]{:S(2)}, u32[]{:S(2)}) collective-permute-start(bf16[512,1024]{1,0:T(8,128)(2,1)} %bitcast.8), channel_id=1, source_target_pairs={{0,1},{1,0},{2,3},{3,2},{4,5},{5,4},{6,7},{7,6},{8,9},{9,8},{10,11... | collective-permute-start | bytes 3145736 | tf_op jit(solution)/shard_map/ppermute | solution.py:216
  2.9 13.7 %copy-start.1 = (bf16[1,512,1024]{2,1,0:T(8,128)(2,1)S(1)}, bf16[1,512,1024]{2,1,0:T(8,128)(2,1)}, u32[]{:S(2)}) copy-start(bf16[1,512,1024]{2,1,0:T(8,128)(2,1)} %param.11) | copy-start | bytes 3145732
  4.3 9.9 %collective-permute-start = (bf16[384,1024]{1,0:T(8,128)(2,1)S(1)}, bf16[384,1024]{1,0:T(8,128)(2,1)S(1)}, u32[]{:S(2)}, u32[]{:S(2)}) collective-permute-start(bf16[384,1024]{1,0:T(8,128)(2,1)S(1)} %broadcast_multiply_fusion.own_ref.refs_1_), channel_id=1, source_target_pairs={{0,1},{1,0},{2,3},{3,2},{4,5},{5,4},{6,7},{7,6},{8,9},{9,8},{10,11... | collective-permute-start | bytes 2359304 | tf_op jit(solution)/shard_map/ppermute | solution.py:216
  4.8 14.9 %collective-permute-start.3 = (bf16[512,1024]{1,0:T(8,128)(2,1)}, bf16[512,1024]{1,0:T(8,128)(2,1)}, u32[]{:S(2)}, u32[]{:S(2)}) collective-permute-start(bf16[512,1024]{1,0:T(8,128)(2,1)} %bitcast.9), channel_id=1, source_target_pairs={{0,2},{1,7},{2,4},{3,1},{4,6},{5,3},{6,0},{7,5},{8,10},{9,15},{10,... | collective-permute-start | bytes 3145736 | tf_op jit(solution)/shard_map/ppermute | solution.py:216
  7.3 27.5 %collective-permute-start.5 = (bf16[512,1024]{1,0:T(8,128)(2,1)}, bf16[512,1024]{1,0:T(8,128)(2,1)}, u32[]{:S(2)}, u32[]{:S(2)}) collective-permute-start(bf16[512,1024]{1,0:T(8,128)(2,1)} %bitcast.10), channel_id=1, source_target_pairs={{0,8},{1,9},{2,10},{3,11},{4,12},{5,13},{6,14},{7,15},{8,0},{9,1},... | collective-permute-start | bytes 3145736 | tf_op jit(solution)/shard_map/ppermute | solution.py:216
  14.2 0.9 copy-start.4
  15.0 1.1 copy-start.5
  16.2 8.5 %copy-start = (bf16[384,8192]{1,0:T(8,128)(2,1)S(1)}, bf16[384,8192]{1,0:T(8,128)(2,1)}, u32[]{:S(2)}) copy-start(bf16[384,8192]{1,0:T(8,128)(2,1)} %refs_2_.7) | copy-start | bytes 18874372
  17.0 17.9 %collective-permute-start.4 = (bf16[512,1024]{1,0:T(8,128)(2,1)}, bf16[512,1024]{1,0:T(8,128)(2,1)}, u32[]{:S(2)}, u32[]{:S(2)}) collective-permute-start(bf16[512,1024]{1,0:T(8,128)(2,1)} %collective-permute-done.1.refs_3_), channel_id=1, source_target_pairs={{0,2},{1,7},{2,4},{3,1},{4,6},{5,3},{6,0},{7,5},{8,10},{9,15},{10,... | collective-permute-start | bytes 3145736 | tf_op jit(solution)/shard_map/ppermute | solution.py:216
  19.6 15.3 %collective-permute-start.6 = (bf16[1024,128]{1,0:T(8,128)(2,1)S(1)}, bf16[1024,128]{1,0:T(8,128)(2,1)S(1)}, u32[]{:S(2)}, u32[]{:S(2)}) collective-permute-start(bf16[1024,128]{1,0:T(8,128)(2,1)S(1)} %get-tuple-element.88), channel_id=1, source_target_pairs={{0,16},{16,32},{32,48},{48,0},{64,80},{80,96},{96,112},{112,64},{1... | collective-permute-start | bytes 786440 | tf_op jit(solution)/shard_map/ppermute | solution.py:221
  21.2 13.6 %collective-permute-start.7 = (bf16[1024,128]{1,0:T(8,128)(2,1)S(1)}, bf16[1024,128]{1,0:T(8,128)(2,1)S(1)}, u32[]{:S(2)}, u32[]{:S(2)}) collective-permute-start(bf16[1024,128]{1,0:T(8,128)(2,1)S(1)} %pad_maximum_fusion.2), channel_id=1, source_target_pairs={{0,48},{16,0},{32,16},{48,32},{64,112},{80,64},{96,80},{112,96},{1... | collective-permute-start | bytes 786440 | tf_op jit(solution)/shard_map/ppermute | solution.py:221
  23.4 11.5 %collective-permute-start.8 = (bf16[1024,128]{1,0:T(8,128)(2,1)S(1)}, bf16[1024,128]{1,0:T(8,128)(2,1)S(1)}, u32[]{:S(2)}, u32[]{:S(2)}) collective-permute-start(bf16[1024,128]{1,0:T(8,128)(2,1)S(1)} %get-tuple-element.90), channel_id=1, source_target_pairs={{0,32},{16,48},{32,0},{48,16},{64,96},{80,112},{96,64},{112,80},{1... | collective-permute-start | bytes 786440 | tf_op jit(solution)/shard_map/ppermute | solution.py:221
  33.9 1.0 copy-start.6
  34.9 9.7 %copy-start.8 = (bf16[1024,128]{1,0:T(8,128)(2,1)}, bf16[1024,128]{1,0:T(8,128)(2,1)S(1)}, u32[]{:S(2)}) copy-start(bf16[1024,128]{1,0:T(8,128)(2,1)S(1)} %collective-permute-done.6) | copy-start | bytes 786436
  34.9 9.7 %copy-start.9 = (bf16[1024,128]{1,0:T(8,128)(2,1)}, bf16[1024,128]{1,0:T(8,128)(2,1)S(1)}, u32[]{:S(2)}) copy-start(bf16[1024,128]{1,0:T(8,128)(2,1)S(1)} %collective-permute-done.7) | copy-start | bytes 786436
  34.9 9.7 %copy-start.10 = (bf16[1024,128]{1,0:T(8,128)(2,1)}, bf16[1024,128]{1,0:T(8,128)(2,1)S(1)}, u32[]{:S(2)}) copy-start(bf16[1024,128]{1,0:T(8,128)(2,1)S(1)} %collective-permute-done.8) | copy-start | bytes 786436
  34.9 39.9 %collective-permute-start.9 = (s16[4,1040,256]{2,1,0:T(8,128)(2,1)}, s16[4,1040,256]{2,1,0:T(8,128)(2,1)}, u32[]{:S(2)}, u32[]{:S(2)}) collective-permute-start(s16[4,1040,256]{2,1,0:T(8,128)(2,1)} %get-tuple-element.91), channel_id=1, source_target_pairs={{0,6},{1,3},{2,0},{3,5},{4,2},{5,7},{6,4},{7,1},{8,14},{9,11},{10,... | collective-permute-start | bytes 6389768 | tf_op jit(solution)/shard_map/ppermute | solution.py:216
  36.3 8.3 %collective-permute-start.11 = (bf16[512,1024]{1,0:T(8,128)(2,1)}, bf16[512,1024]{1,0:T(8,128)(2,1)S(1)}, u32[]{:S(2)}, u32[]{:S(2)}) collective-permute-start(bf16[512,1024]{1,0:T(8,128)(2,1)} %collective-permute-done.3.refs_4_), channel_id=1, source_target_pairs={{0,1},{1,0},{2,3},{3,2},{4,5},{5,4},{6,7},{7,6},{8,9},{9,8},{10,11... | collective-permute-start | bytes 3145736 | tf_op jit(solution)/shard_map/ppermute | solution.py:216
  40.6 7.7 %collective-permute-start.12 = (bf16[512,1024]{1,0:T(8,128)(2,1)}, bf16[512,1024]{1,0:T(8,128)(2,1)}, u32[]{:S(2)}, u32[]{:S(2)}) collective-permute-start(bf16[512,1024]{1,0:T(8,128)(2,1)} %collective-permute-done.4.refs_5_), channel_id=1, source_target_pairs={{0,1},{1,0},{2,3},{3,2},{4,5},{5,4},{6,7},{7,6},{8,9},{9,8},{10,11... | collective-permute-start | bytes 3145736 | tf_op jit(solution)/shard_map/ppermute | solution.py:216
  40.6 24.9 %collective-permute-start.15 = (s16[2,1040,256]{2,1,0:T(8,128)(2,1)}, s16[2,1040,256]{2,1,0:T(8,128)(2,1)}, u32[]{:S(2)}, u32[]{:S(2)}) collective-permute-start(s16[2,1040,256]{2,1,0:T(8,128)(2,1)} %get-tuple-element.106), channel_id=1, source_target_pairs={{0,8},{1,9},{2,10},{3,11},{4,12},{5,13},{6,14},{7,15},{8,0},{9,1},... | collective-permute-start | bytes 3194888 | tf_op jit(solution)/shard_map/ppermute | solution.py:216
  41.9 26.8 %collective-permute-start.10 = (bf16[512,1024]{1,0:T(8,128)(2,1)}, bf16[512,1024]{1,0:T(8,128)(2,1)}, u32[]{:S(2)}, u32[]{:S(2)}) collective-permute-start(bf16[512,1024]{1,0:T(8,128)(2,1)} %collective-permute-done.3.refs_4_), channel_id=1, source_target_pairs={{0,2},{1,7},{2,4},{3,1},{4,6},{5,3},{6,0},{7,5},{8,10},{9,15},{10,... | collective-permute-start | bytes 3145736 | tf_op jit(solution)/shard_map/ppermute | solution.py:216
  44.6 1.0 copy-start.2
  45.5 27.9 %collective-permute-start.13 = (bf16[512,1024]{1,0:T(8,128)(2,1)}, bf16[512,1024]{1,0:T(8,128)(2,1)}, u32[]{:S(2)}, u32[]{:S(2)}) collective-permute-start(bf16[512,1024]{1,0:T(8,128)(2,1)} %collective-permute-done.5.refs_4_), channel_id=1, source_target_pairs={{0,1},{1,0},{2,3},{3,2},{4,5},{5,4},{6,7},{7,6},{8,9},{9,8},{10,11... | collective-permute-start | bytes 3145736 | tf_op jit(solution)/shard_map/ppermute | solution.py:216
  48.3 17.1 %slice-start = ((s8[6291456]{0:T(1024)(128)(4,1)}), s8[4194304]{0:T(1024)(128)(4,1)S(1)}, s32[]{:S(2)}) async-start(s8[6291456]{0:T(1024)(128)(4,1)} %bitcast.6), calls=%async_computation | async-start | bytes 8388608
  48.4 17.1 %slice-start.1 = ((s8[6291456]{0:T(1024)(128)(4,1)}), s8[2097152]{0:T(1024)(128)(4,1)S(1)}, s32[]{:S(2)}) async-start(s8[6291456]{0:T(1024)(128)(4,1)} %bitcast.6), calls=%async_computation.1 | async-start | bytes 4194304
  48.4 25.1 %collective-permute-start.14 = (f32[512,128]{1,0:T(8,128)S(1)}, f32[512,128]{1,0:T(8,128)S(1)}, u32[]{:S(2)}, u32[]{:S(2)}) collective-permute-start(f32[512,128]{1,0:T(8,128)S(1)} %slice.9), channel_id=1, source_target_pairs={{0,64},{16,80},{32,96},{48,112},{64,0},{80,16},{96,32},{112,48},{1... | collective-permute-start | bytes 786440 | tf_op jit(solution)/shard_map/ppermute | solution.py:221
  57.4 19.1 %copy-start.7 = (s16[2,1040,256]{2,1,0:T(8,128)(2,1)S(1)}, s16[2,1040,256]{2,1,0:T(8,128)(2,1)}, u32[]{:S(2)}) copy-start(s16[2,1040,256]{2,1,0:T(8,128)(2,1)} %copy-done.6) | copy-start | bytes 3194884
  57.4 22.1 %copy-start.3 = (bf16[512,1024]{1,0:T(8,128)(2,1)S(1)}, bf16[512,1024]{1,0:T(8,128)(2,1)}, u32[]{:S(2)}) copy-start(bf16[512,1024]{1,0:T(8,128)(2,1)} %copy-done.2) | copy-start | bytes 3145732
  68.7 22.9 %copy-start.11 = (f32[512,128]{1,0:T(8,128)S(1)}, f32[512,128]{1,0:T(8,128)}, u32[]{:S(2)}) copy-start(f32[512,128]{1,0:T(8,128)} %param.13) | copy-start | bytes 786436
  74.8 14.1 %collective-permute-start.16 = (s16[2,1040,256]{2,1,0:T(8,128)(2,1)S(1)}, s16[2,1040,256]{2,1,0:T(8,128)(2,1)S(1)}, u32[]{:S(2)}, u32[]{:S(2)}) collective-permute-start(s16[2,1040,256]{2,1,0:T(8,128)(2,1)S(1)} %partial_sums.5), channel_id=1, source_target_pairs={{0,2},{1,7},{2,4},{3,1},{4,6},{5,3},{6,0},{7,5},{8,10},{9,15},{10,... | collective-permute-start | bytes 3194888 | tf_op jit(solution)/shard_map/ppermute | solution.py:216
  76.6 23.8 %collective-permute-start.17 = (s16[2,1040,256]{2,1,0:T(8,128)(2,1)S(1)}, s16[2,1040,256]{2,1,0:T(8,128)(2,1)S(1)}, u32[]{:S(2)}, u32[]{:S(2)}) collective-permute-start(s16[2,1040,256]{2,1,0:T(8,128)(2,1)S(1)} %copy-done.7), channel_id=1, source_target_pairs={{0,2},{1,7},{2,4},{3,1},{4,6},{5,3},{6,0},{7,5},{8,10},{9,15},{10,... | collective-permute-start | bytes 3194888 | tf_op jit(solution)/shard_map/ppermute | solution.py:216
  76.6 31.6 %collective-permute-start.18 = (bf16[512,1024]{1,0:T(8,128)(2,1)}, bf16[512,1024]{1,0:T(8,128)(2,1)S(1)}, u32[]{:S(2)}, u32[]{:S(2)}) collective-permute-start(bf16[512,1024]{1,0:T(8,128)(2,1)} %collective-permute-done.10.refs_2_), channel_id=1, source_target_pairs={{0,8},{1,9},{2,10},{3,11},{4,12},{5,13},{6,14},{7,15},{8,0},{9,1},... | collective-permute-start | bytes 3145736 | tf_op jit(solution)/shard_map/ppermute | solution.py:216
  77.9 30.3 %collective-permute-start.19 = (bf16[512,1024]{1,0:T(8,128)(2,1)}, bf16[512,1024]{1,0:T(8,128)(2,1)S(1)}, u32[]{:S(2)}, u32[]{:S(2)}) collective-permute-start(bf16[512,1024]{1,0:T(8,128)(2,1)} %collective-permute-done.10.refs_2_), channel_id=1, source_target_pairs={{0,1},{1,0},{2,3},{3,2},{4,5},{5,4},{6,7},{7,6},{8,9},{9,8},{10,11... | collective-permute-start | bytes 3145736 | tf_op jit(solution)/shard_map/ppermute | solution.py:216
  88.9 22.6 %collective-permute-start.20 = (bf16[512,1024]{1,0:T(8,128)(2,1)}, bf16[512,1024]{1,0:T(8,128)(2,1)S(1)}, u32[]{:S(2)}, u32[]{:S(2)}) collective-permute-start(bf16[512,1024]{1,0:T(8,128)(2,1)} %collective-permute-done.5.refs_4_), channel_id=1, source_target_pairs={{0,2},{1,7},{2,4},{3,1},{4,6},{5,3},{6,0},{7,5},{8,10},{9,15},{10,... | collective-permute-start | bytes 3145736 | tf_op jit(solution)/shard_map/ppermute | solution.py:216
  92.4 15.8 %collective-permute-start.21 = (f32[512,128]{1,0:T(8,128)S(1)}, f32[512,128]{1,0:T(8,128)S(1)}, u32[]{:S(2)}, u32[]{:S(2)}) collective-permute-start(f32[512,128]{1,0:T(8,128)S(1)} %get-tuple-element.126), channel_id=1, source_target_pairs={{0,64},{16,80},{32,96},{48,112},{64,0},{80,16},{96,32},{112,48},{1... | collective-permute-start | bytes 786440 | tf_op jit(solution)/shard_map/ppermute | solution.py:221
  111.6 7.8 %collective-permute-start.24 = (bf16[512,1024]{1,0:T(8,128)(2,1)S(1)}, bf16[512,1024]{1,0:T(8,128)(2,1)S(1)}, u32[]{:S(2)}, u32[]{:S(2)}) collective-permute-start(bf16[512,1024]{1,0:T(8,128)(2,1)S(1)} %collective-permute-done.20.refs_5_), channel_id=1, source_target_pairs={{0,1},{1,0},{2,3},{3,2},{4,5},{5,4},{6,7},{7,6},{8,9},{9,8},{10,11... | collective-permute-start | bytes 3145736 | tf_op jit(solution)/shard_map/ppermute | solution.py:216
  115.3 14.1 %collective-permute-start.26 = (s16[2,1040,256]{2,1,0:T(8,128)(2,1)S(1)}, s16[2,1040,256]{2,1,0:T(8,128)(2,1)S(1)}, u32[]{:S(2)}, u32[]{:S(2)}) collective-permute-start(s16[2,1040,256]{2,1,0:T(8,128)(2,1)S(1)} %get-tuple-element.135), channel_id=1, source_target_pairs={{0,2},{1,7},{2,4},{3,1},{4,6},{5,3},{6,0},{7,5},{8,10},{9,15},{10,... | collective-permute-start | bytes 3194888 | tf_op jit(solution)/shard_map/ppermute | solution.py:216
  117.1 24.3 %collective-permute-start.27 = (s16[2,1040,256]{2,1,0:T(8,128)(2,1)S(1)}, s16[2,1040,256]{2,1,0:T(8,128)(2,1)S(1)}, u32[]{:S(2)}, u32[]{:S(2)}) collective-permute-start(s16[2,1040,256]{2,1,0:T(8,128)(2,1)S(1)} %get-tuple-element.136), channel_id=1, source_target_pairs={{0,8},{1,9},{2,10},{3,11},{4,12},{5,13},{6,14},{7,15},{8,0},{9,1},... | collective-permute-start | bytes 3194888 | tf_op jit(solution)/shard_map/ppermute | solution.py:216
  118.4 27.5 %collective-permute-start.22 = (bf16[512,1024]{1,0:T(8,128)(2,1)}, bf16[512,1024]{1,0:T(8,128)(2,1)S(1)}, u32[]{:S(2)}, u32[]{:S(2)}) collective-permute-start(bf16[512,1024]{1,0:T(8,128)(2,1)} %collective-permute-done.13.refs_5_), channel_id=1, source_target_pairs={{0,2},{1,7},{2,4},{3,1},{4,6},{5,3},{6,0},{7,5},{8,10},{9,15},{10,... | collective-permute-start | bytes 3145736 | tf_op jit(solution)/shard_map/ppermute | solution.py:216
  118.4 27.4 %collective-permute-start.23 = (f32[1024,128]{1,0:T(8,128)S(1)}, f32[1024,128]{1,0:T(8,128)S(1)}, u32[]{:S(2)}, u32[]{:S(2)}) collective-permute-start(f32[1024,128]{1,0:T(8,128)S(1)} %constant_dynamic-update-slice_fusion.refs_0_.refs_1_), channel_id=1, source_target_pairs={{0,16},{16,32},{32,48},{48,0},{64,80},{80,96},{96,112},{112,64},{1... | collective-permute-start | bytes 1572872 | tf_op jit(solution)/shard_map/ppermute | solution.py:221
  119.4 26.5 %collective-permute-start.25 = (f32[1024,128]{1,0:T(8,128)S(1)}, f32[1024,128]{1,0:T(8,128)S(1)}, u32[]{:S(2)}, u32[]{:S(2)}) collective-permute-start(f32[1024,128]{1,0:T(8,128)S(1)} %constant_dynamic-update-slice_fusion.refs_0_.refs_1_), channel_id=1, source_target_pairs={{0,48},{16,0},{32,16},{48,32},{64,112},{80,64},{96,80},{112,96},{1... | collective-permute-start | bytes 1572872 | tf_op jit(solution)/shard_map/ppermute | solution.py:221
  145.9 6.9 %collective-permute-start.28 = (bf16[512,1024]{1,0:T(8,128)(2,1)S(1)}, bf16[512,1024]{1,0:T(8,128)(2,1)S(1)}, u32[]{:S(2)}, u32[]{:S(2)}) collective-permute-start(bf16[512,1024]{1,0:T(8,128)(2,1)S(1)} %collective-permute-done.18.refs_4_), channel_id=1, source_target_pairs={{0,1},{1,0},{2,3},{3,2},{4,5},{5,4},{6,7},{7,6},{8,9},{9,8},{10,11... | collective-permute-start | bytes 3145736 | tf_op jit(solution)/shard_map/ppermute | solution.py:216
  146.0 6.8 %collective-permute-start.29 = (bf16[512,1024]{1,0:T(8,128)(2,1)S(1)}, bf16[512,1024]{1,0:T(8,128)(2,1)S(1)}, u32[]{:S(2)}, u32[]{:S(2)}) collective-permute-start(bf16[512,1024]{1,0:T(8,128)(2,1)S(1)} %collective-permute-done.22.refs_3_), channel_id=1, source_target_pairs={{0,1},{1,0},{2,3},{3,2},{4,5},{5,4},{6,7},{7,6},{8,9},{9,8},{10,11... | collective-permute-start | bytes 3145736 | tf_op jit(solution)/shard_map/ppermute | solution.py:216
  146.5 4.4 %collective-permute-start.30 = (s16[1,1040,256]{2,1,0:T(8,128)(2,1)S(1)}, s16[1,1040,256]{2,1,0:T(8,128)(2,1)S(1)}, u32[]{:S(2)}, u32[]{:S(2)}) collective-permute-start(s16[1,1040,256]{2,1,0:T(8,128)(2,1)S(1)} %get-tuple-element.142), channel_id=1, source_target_pairs={{0,1},{1,0},{2,3},{3,2},{4,5},{5,4},{6,7},{7,6},{8,9},{9,8},{10,11... | collective-permute-start | bytes 1597448 | tf_op jit(solution)/shard_map/ppermute | solution.py:216
  146.5 14.3 %collective-permute-start.31 = (f32[1024,128]{1,0:T(8,128)S(1)}, f32[1024,128]{1,0:T(8,128)S(1)}, u32[]{:S(2)}, u32[]{:S(2)}) collective-permute-start(f32[1024,128]{1,0:T(8,128)S(1)} %collective-permute-done.23.refs_2_.refs_3_), channel_id=1, source_target_pairs={{0,16},{16,32},{32,48},{48,0},{64,80},{80,96},{96,112},{112,64},{1... | collective-permute-start | bytes 1572872 | tf_op jit(solution)/shard_map/ppermute | solution.py:221
